TPU v7x, 32 devices: a whole 2x2x4 slice. The times are simulated.
32 devices in a mesh: lat: 4 (over y, x), rad: 8 (over z, core).
Axes of the slice: x: 2, y: 2, z: 4, core: 2. Of those that a mesh axis runs over, the one named last changes fastest.
Arguments:
- displacement: float32 [3, 32, 256, 384], P(None, 'rad', 'lat'), may hold values from -6 to 6
- forcing: float32 [3, 32, 256, 384], P(None, 'rad', 'lat'), may hold values from -12 to 12
- layer_id: int32 [32], P('rad'), may hold values from 0 to 11
- stiffness: float32 [12], replicated, may hold values from 0.3 to 3
- coupling: float32 [12, 3, 3], replicated, may hold values from -0.5 to 0.5
- cycle_id: int32 [256, 384], P('lat'), may hold values from 0 to 1535, as said below
- cycle_count: int32 [1536], replicated, may hold values from 32 to 96, as said below
- gravity: float32 [2, 2, 512], replicated, may hold values from -96 to 96
Outputs:
- smoothed: float32 [3, 32, 256, 384], P(None, 'rad', 'lat')
- potential: float32 [2, 256, 384], P(None, 'lat')
Inputs may be any that keep to these rules, and one draw needn't show every extreme that they name: Every cycle holds at least one point, and cycle_id never falls along the lateral points taken row by row. cycle_count[j] is the number of points whose cycle_id is j.
All inputs are finite; a program needn't handle non-finite values.
Results may differ from a plain program's by a relative error of at most 0.0001.
Values sent between devices are 32-bit elements; how exact they have to be, the bound alone decides.
No kernel may reach another device: no remote copies, remote signals or barrier semaphores. Data moves between devices by JAX's collectives and lax.ppermute only.
A program may use at most 64 MiB of HBM per device.

v0:
```python
import math

import jax
import jax.numpy as jnp
from jax import lax
from jax.sharding import PartitionSpec as P

SWEEPS = 2


OMEGA = 0.8
HIGHEST = lax.Precision.HIGHEST


def with_halo(block, sides, width):
    for axis, dim in sides:
        count = lax.axis_size(axis)
        forward = [(i, i + 1) for i in range(count - 1)]
        backward = [(target, source) for source, target in forward]
        low = lax.ppermute(
            lax.slice_in_dim(block, block.shape[dim] - width, None, axis=dim), axis, forward
        )
        high = lax.ppermute(lax.slice_in_dim(block, 0, width, axis=dim), axis, backward)
        block = jnp.concatenate([low, block, high], axis=dim)
    return block


def zonal_table(degrees, cycle_span, cycle_total):
    degree = jnp.arange(degrees, dtype=jnp.int32)[:, None]
    cycle_index = jnp.arange(cycle_span, dtype=jnp.int32)[None, :]
    phases = degree * (2 * cycle_index + 1) % (4 * cycle_total)
    return jnp.cos(jnp.pi * phases.astype(jnp.float32) / (2.0 * cycle_total))


def material(layer_id, stiffness, coupling):
    matches = layer_id[:, None] == jnp.arange(stiffness.shape[0], dtype=jnp.int32)[None, :]
    layer_mu = jnp.sum(jnp.where(matches, stiffness[None, :], 0.0), axis=1)
    layer_coupling = jnp.sum(jnp.where(matches[:, :, None, None], coupling[None], 0.0), axis=1)
    return (layer_mu, layer_coupling)


def apply_operator(padded, layer_mu, layer_coupling):
    center = padded[:, 1:-1, 1:-1, 1:-1]
    beside = padded[:, 2:, 1:-1, 1:-1] + padded[:, :-2, 1:-1, 1:-1]
    beside = beside + padded[:, 1:-1, 2:, 1:-1] + padded[:, 1:-1, :-2, 1:-1]
    beside = beside + padded[:, 1:-1, 1:-1, 2:] + padded[:, 1:-1, 1:-1, :-2]
    coupled = jnp.einsum("rcd,drab->crab", layer_coupling, center, precision=HIGHEST)
    return layer_mu[None, :, None, None] * (6.0 * center - beside) + coupled


def diagonal_of(layer_mu, layer_coupling):
    own = jnp.transpose(jnp.diagonal(layer_coupling, axis1=1, axis2=2))
    return 6.0 * layer_mu[None, :, None, None] + own[:, :, None, None]


def pad_columns(values):
    return jnp.pad(values, ((0, 0), (0, 0), (0, 0), (1, 1)))


def local(displacement, forcing, layer_id, stiffness, coupling, cycle_id, cycle_count, gravity):
    layer_mu, layer_coupling = material(layer_id, stiffness, coupling)
    diagonal = diagonal_of(layer_mu, layer_coupling)
    rad_index = lax.axis_index("rad")
    rad_count = lax.axis_size("rad")
    current = displacement
    for sweep_index in range(SWEEPS):
        padded = with_halo(current, (("lat", 2), ("rad", 1)), 1)
        padded = pad_columns(padded)
        current = (
            current
            + OMEGA * (forcing - apply_operator(padded, layer_mu, layer_coupling)) / diagonal
        )
    surface = jnp.where(rad_index == rad_count - 1, current[0, -1], 0.0)
    bottom = jnp.where(rad_index == 0, current[0, 0], 0.0)
    boundary = jnp.stack([surface, bottom])
    cycle_total = cycle_count.shape[0]
    degrees = gravity.shape[2]
    scale = math.sqrt(2.0 / cycle_total)
    flat_ids = cycle_id.reshape(-1)
    cycle_sums = jax.vmap(
        lambda row_values: jax.ops.segment_sum(row_values, flat_ids, num_segments=cycle_total)
    )(boundary.reshape(2, -1))
    basis = zonal_table(degrees, cycle_total, cycle_total)
    totals = lax.psum(cycle_sums, ("lat", "rad"))
    cycle_means = totals / cycle_count.astype(jnp.float32)[None, :]
    coefficients = scale * jnp.dot(cycle_means, basis.T, precision=HIGHEST)
    modes = gravity[:, 0] * coefficients[0][None, :] + gravity[:, 1] * coefficients[1][None, :]
    cycle_potential = scale * jnp.dot(modes, basis, precision=HIGHEST)
    potential = jnp.take(cycle_potential, cycle_id, axis=1)
    return (current, potential)


def solution(mesh):
    in_specs = (
        P(None, "rad", "lat", None),
        P(None, "rad", "lat", None),
        P("rad"),
        P(),
        P(),
        P("lat", None),
        P(),
        P(),
    )
    out_specs = (P(None, "rad", "lat", None), P(None, "lat", None))
    return jax.shard_map(local, mesh=mesh, in_specs=in_specs, out_specs=out_specs, check_vma=False)
```

profile of v0, /device:TPU:1, one launch (start us, length us, event | category | flops | bytes accessed | tf_op | source)
XLA Modules:
  0.0 415.8 jit_solution(9300221996324555976)
XLA Ops:
  0.7 2.2 copy.79
  2.9 1.2 copy-done.1
  4.0 3.9 collective-permute-start
  8.0 1.3 collective-permute-start.1
  9.3 0.0 copy-done.11
  9.3 0.1 iota_compare_fusion.2
  9.4 0.2 select_reduce_fusion.1
  9.7 0.1 select_reduce_fusion
  9.8 0.1 copy.87
  9.9 0.0 collective-permute-done
  9.9 1.0 copy_dynamic-update-slice_fusion
  10.9 1.7 collective-permute-done.1
  12.6 0.9 fusion.55
  13.5 4.0 collective-permute-start.2
  17.5 3.1 collective-permute-start.3
  20.6 0.6 gather_fusion
  21.2 0.1 copy.78
  21.3 3.1 collective-permute-done.2
  24.5 1.0 collective-permute-done.3
  25.4 0.7 copy-done.5
  26.2 2.7 select_maximum_fusion.4
  28.9 0.0 copy-start.6
  28.9 0.0 copy-start.7
  28.9 7.5 %divide_add_fusion.1 = f32[3,4,64,384]{3,0,2,1:T(4,128)S(1)} fusion(f32[3,4,64,384]{3,0,2,1:T(4,128)S(1)} %copy-done.2, f32[3,4,64,384]{3,2,1,0:T(8,128)S(1)} %copy-done.9, f32[3,6,66,386]{3,0,2,1:T(4,128)S(1)} %select_maximum_fusion.4, f32[3,4,1,384]{3,0,2,1:T(4,128)S(1)} %collective-permute-done, f32[3,4,1,384]{3,0,2,1:T(4,128)S(1)} %collective-permute-done.1, ...), kind=kOutput, calls=%fused_computation.26 | convolution fusion | flops 15630336 | bytes 10940928 | tf_op jit(solution)/shard_map/rcd,drab->crab/dot_general | solution.py:47
  36.5 1.3 collective-permute-start.5
  37.8 4.7 %collective-permute-start.4 = (f32[3,4,1,384]{3,0,2,1:T(4,128)S(1)}, f32[3,4,1,384]{3,0,2,1:T(4,128)S(1)}, u32[]{:S(2)}, u32[]{:S(2)}) collective-permute-start(f32[3,4,1,384]{3,0,2,1:T(4,128)S(1)} %get-tuple-element.16), channel_id=1, source_target_pairs={{0,8},{8,16},{16,24},{1,9},{9,17},{17,25},{2,10},{10,18},{18,26},{... | collective-permute-start | bytes 55304 | tf_op jit(solution)/shard_map/ppermute | solution.py:20
  42.5 0.0 collective-permute-done.5
  42.5 0.8 collective-permute-done.4
  43.4 0.2 pad_maximum_fusion.12
  43.6 1.9 collective-permute-start.6
  45.5 5.4 %collective-permute-start.7 = (f32[3,1,66,384]{3,0,2,1:T(4,128)S(1)}, f32[3,1,66,384]{3,0,2,1:T(4,128)S(1)}, u32[]{:S(2)}, u32[]{:S(2)}) collective-permute-start(f32[3,1,66,384]{3,0,2,1:T(4,128)S(1)} %get-tuple-element.10), channel_id=1, source_target_pairs={{0,1},{1,2},{2,3},{3,4},{4,5},{5,6},{6,7},{8,9},{9,10},{10,11},{11... | collective-permute-start | bytes 912392 | tf_op jit(solution)/shard_map/ppermute | solution.py:20
  51.0 0.0 copy-start.10
  51.0 3.4 collective-permute-done.6
  54.4 1.2 collective-permute-done.7
  55.6 4.0 select_maximum_fusion
  59.6 9.3 %divide_add_fusion = f32[3,4,64,384]{3,0,2,1:T(4,128)S(1)} fusion(f32[3,4,64,384]{3,0,2,1:T(4,128)S(1)} %divide_add_fusion.1, f32[3,4,64,384]{3,2,1,0:T(8,128)S(1)} %copy-done.10, f32[3,6,66,386]{3,0,2,1:T(4,128)S(1)} %select_maximum_fusion, f32[3,4,1,384]{3,0,2,1:T(4,128)S(1)} %collective-permute-done.4, f32[3,4,1,384]{3,0,2,1:T(4,128)S(1)} %collective-permute-done.5, ...), kind=kOutput, calls=%fused_computation.25 | convolution fusion | flops 16809984 | bytes 9521664 | tf_op jit(solution)/shard_map/rcd,drab->crab/dot_general | solution.py:47
  68.9 1.1 copy.86
  70.1 0.2 broadcast_select_fusion.1
  70.3 0.2 maximum_bitcast_fusion
  70.5 6.9 %copy.83 = f32[24576,2]{1,0:T(8,128)} copy(f32[24576,2]{0,1:T(2,128)S(1)} %maximum_bitcast_fusion) | data formatting | bytes 393216 | tf_op jit(solution)/shard_map/stack | solution.py:75
  77.3 168.3 %scatter_custom_fusion = f32[2,1536]{0,1:T(8,128)S(1)} fusion(s32[24576]{0:T(1024)S(1)} %reshape.95, f32[24576,2]{1,0:T(8,128)} %copy.83, f32[]{:T(128)} %constant.21.clone.1), kind=kCustom, calls=%fused_computation.69 | custom fusion | flops 49152 | bytes 12800 | tf_op jit(solution)/shard_map/vmap()/scatter-add | solution.py:81
  245.6 51.1 %psum.7 = f32[2,1536]{0,1:T(8,128)S(1)} all-reduce(f32[2,1536]{0,1:T(8,128)S(1)} %scatter_custom_fusion), channel_id=1, replica_groups=mesh['lat'=4,'rad'=8] {'lat','rad'}, use_global_device_ids=true, to_apply=%region_3.4 | all-reduce | flops 3072 | bytes 24576 | tf_op jit(solution)/shard_map/psum | solution.py:84
  296.7 14.7 %fusion.36 = f32[2,512]{1,0:T(2,128)S(1)} fusion(s32[1536]{0:T(1024)S(1)} %multiply_add_fusion, f32[2,1536]{0,1:T(8,128)S(1)} %psum.7, f32[1536]{0:T(1024)S(1)} %convert_element_type.11), kind=kOutput, calls=%fused_computation.63 | convolution fusion | flops 25956352 | bytes 28672 | tf_op jit(solution)/shard_map/dot_general | solution.py:86
  311.4 13.9 %fusion.11 = f32[2,1536]{1,0:T(2,128)S(1)} fusion(s32[1536]{0:T(1024)S(1)} %multiply_add_fusion, f32[2,1,512]{2,1,0:T(1,128)S(1)} %get-tuple-element.21, f32[2,1,512]{2,1,0:T(1,128)S(1)} %get-tuple-element.20, f32[512]{0:T(512)S(1)} %bitcast.38, f32[512]{0:T(512)S(1)} %bitcast.37), kind=kOutput, calls=%fused_computation.22 | convolution fusion | flops 25958400 | bytes 30720 | tf_op jit(solution)/shard_map/dot_general | solution.py:88
  325.3 0.3 copy.84
  325.6 81.9 %gather_fusion.1 = f32[24576,2]{1,0:T(8,128)} fusion(f32[2,1536]{0,1:T(8,128)S(1)} %copy.84, s32[24576]{0:T(1024)S(1)} %broadcast_clamp_fusion), kind=kCustom, calls=%fused_computation.1 | custom fusion | bytes 491520 | tf_op jit(solution)/shard_map/jit(_take)/gather | solution.py:89
  407.5 7.6 %copy.85 = f32[64,384,2]{1,0,2:T(8,128)S(1)} copy(f32[64,384,2]{2,1,0:T(8,128)} %bitcast.33) | data formatting | bytes 393216 | tf_op jit(solution)/shard_map/jit(_take)/gather | solution.py:89
  415.1 0.7 select_bitcast_fusion
  (36 shorter events, 0.2 us)
Async XLA Ops:
  0.6 9.3 %copy-start = (f32[3,4,64,384]{3,2,1,0:T(8,128)S(1)}, f32[3,4,64,384]{3,2,1,0:T(8,128)}, u32[]{:S(2)}) copy-start(f32[3,4,64,384]{3,2,1,0:T(8,128)} %param.8) | copy-start | bytes 3538948
  0.6 8.7 %copy-start.11 = (s32[4]{0:T(128)S(1)}, s32[4]{0:T(128)}, u32[]{:S(2)}) copy-start(s32[4]{0:T(128)} %param.10) | copy-start | bytes 52
  0.7 8.7 %copy-start.12 = (f32[12]{0:T(128)S(1)}, f32[12]{0:T(128)}, u32[]{:S(2)}) copy-start(f32[12]{0:T(128)} %param.11) | copy-start | bytes 148
  0.7 8.9 %copy-start.3 = (s32[64,384]{1,0:T(8,128)S(1)}, s32[64,384]{1,0:T(8,128)}, u32[]{:S(2)}) copy-start(s32[64,384]{1,0:T(8,128)} %param.13) | copy-start | bytes 294916
  0.7 9.0 %copy-start.8 = (f32[12,3,3]{0,2,1:T(4,128)S(1)}, f32[12,3,3]{0,2,1:T(4,128)}, u32[]{:S(2)}) copy-start(f32[12,3,3]{0,2,1:T(4,128)} %param.12) | copy-start | bytes 1300
  2.9 1.2 copy-start.1
  4.0 5.8 %collective-permute-start = (f32[3,4,1,384]{3,0,2,1:T(4,128)S(1)}, f32[3,4,1,384]{3,0,2,1:T(4,128)S(1)}, u32[]{:S(2)}, u32[]{:S(2)}) collective-permute-start(f32[3,4,1,384]{3,0,2,1:T(4,128)S(1)} %get-tuple-element.19), channel_id=1, source_target_pairs={{0,8},{8,16},{16,24},{1,9},{9,17},{17,25},{2,10},{10,18},{18,26},{... | collective-permute-start | bytes 55304 | tf_op jit(solution)/shard_map/ppermute | solution.py:20
  8.0 4.6 %collective-permute-start.1 = (f32[3,4,1,384]{3,0,2,1:T(4,128)S(1)}, f32[3,4,1,384]{3,0,2,1:T(4,128)S(1)}, u32[]{:S(2)}, u32[]{:S(2)}) collective-permute-start(f32[3,4,1,384]{3,0,2,1:T(4,128)S(1)} %get-tuple-element.18), channel_id=1, source_target_pairs={{8,0},{16,8},{24,16},{9,1},{17,9},{25,17},{10,2},{18,10},{26,18},{... | collective-permute-start | bytes 55304 | tf_op jit(solution)/shard_map/ppermute | solution.py:23
  13.5 11.0 %collective-permute-start.2 = (f32[3,1,66,384]{3,0,2,1:T(4,128)}, f32[3,1,66,384]{3,0,2,1:T(4,128)S(1)}, u32[]{:S(2)}, u32[]{:S(2)}) collective-permute-start(f32[3,1,66,384]{3,0,2,1:T(4,128)} %get-tuple-element.13), channel_id=1, source_target_pairs={{1,0},{2,1},{3,2},{4,3},{5,4},{6,5},{7,6},{9,8},{10,9},{11,10},{12... | collective-permute-start | bytes 912392 | tf_op jit(solution)/shard_map/ppermute | solution.py:23
  17.5 7.9 %collective-permute-start.3 = (f32[3,1,66,384]{3,0,2,1:T(4,128)S(1)}, f32[3,1,66,384]{3,0,2,1:T(4,128)S(1)}, u32[]{:S(2)}, u32[]{:S(2)}) collective-permute-start(f32[3,1,66,384]{3,0,2,1:T(4,128)S(1)} %get-tuple-element.12), channel_id=1, source_target_pairs={{0,1},{1,2},{2,3},{3,4},{4,5},{5,6},{6,7},{8,9},{9,10},{10,11},{11... | collective-permute-start | bytes 912392 | tf_op jit(solution)/shard_map/ppermute | solution.py:20
  21.3 7.6 %copy-start.2 = (f32[3,4,64,384]{3,0,2,1:T(4,128)S(1)}, f32[3,4,64,384]{3,0,2,1:T(4,128)}, u32[]{:S(2)}) copy-start(f32[3,4,64,384]{3,0,2,1:T(4,128)} %copy-done.1) | copy-start | bytes 3538948
  21.3 7.6 %copy-start.9 = (f32[3,4,64,384]{3,2,1,0:T(8,128)S(1)}, f32[3,4,64,384]{3,2,1,0:T(8,128)}, u32[]{:S(2)}) copy-start(f32[3,4,64,384]{3,2,1,0:T(8,128)} %param.9) | copy-start | bytes 3538948
  24.5 1.0 copy-start.4
  25.4 0.8 copy-start.5
  28.9 13.6 %copy-start.6 = (f32[2,2,512]{2,1,0:T(2,128)S(1)}, f32[2,2,512]{2,1,0:T(2,128)}, u32[]{:S(2)}) copy-start(f32[2,2,512]{2,1,0:T(2,128)} %param.15) | copy-start | bytes 24580
  28.9 13.6 %copy-start.7 = (s32[1536]{0:T(1024)S(1)}, s32[1536]{0:T(1024)}, u32[]{:S(2)}) copy-start(s32[1536]{0:T(1024)} %param.14) | copy-start | bytes 18436
  36.5 6.0 %collective-permute-start.5 = (f32[3,4,1,384]{3,0,2,1:T(4,128)S(1)}, f32[3,4,1,384]{3,0,2,1:T(4,128)S(1)}, u32[]{:S(2)}, u32[]{:S(2)}) collective-permute-start(f32[3,4,1,384]{3,0,2,1:T(4,128)S(1)} %get-tuple-element.17), channel_id=1, source_target_pairs={{8,0},{16,8},{24,16},{9,1},{17,9},{25,17},{10,2},{18,10},{26,18},{... | collective-permute-start | bytes 55304 | tf_op jit(solution)/shard_map/ppermute | solution.py:23
  37.8 5.6 %collective-permute-start.4 = (f32[3,4,1,384]{3,0,2,1:T(4,128)S(1)}, f32[3,4,1,384]{3,0,2,1:T(4,128)S(1)}, u32[]{:S(2)}, u32[]{:S(2)}) collective-permute-start(f32[3,4,1,384]{3,0,2,1:T(4,128)S(1)} %get-tuple-element.16), channel_id=1, source_target_pairs={{0,8},{8,16},{16,24},{1,9},{9,17},{17,25},{2,10},{10,18},{18,26},{... | collective-permute-start | bytes 55304 | tf_op jit(solution)/shard_map/ppermute | solution.py:20
  43.6 10.8 %collective-permute-start.6 = (f32[3,1,66,384]{3,0,2,1:T(4,128)S(1)}, f32[3,1,66,384]{3,0,2,1:T(4,128)S(1)}, u32[]{:S(2)}, u32[]{:S(2)}) collective-permute-start(f32[3,1,66,384]{3,0,2,1:T(4,128)S(1)} %get-tuple-element.11), channel_id=1, source_target_pairs={{1,0},{2,1},{3,2},{4,3},{5,4},{6,5},{7,6},{9,8},{10,9},{11,10},{12... | collective-permute-start | bytes 912392 | tf_op jit(solution)/shard_map/ppermute | solution.py:23
  45.5 10.1 %collective-permute-start.7 = (f32[3,1,66,384]{3,0,2,1:T(4,128)S(1)}, f32[3,1,66,384]{3,0,2,1:T(4,128)S(1)}, u32[]{:S(2)}, u32[]{:S(2)}) collective-permute-start(f32[3,1,66,384]{3,0,2,1:T(4,128)S(1)} %get-tuple-element.10), channel_id=1, source_target_pairs={{0,1},{1,2},{2,3},{3,4},{4,5},{5,6},{6,7},{8,9},{9,10},{10,11},{11... | collective-permute-start | bytes 912392 | tf_op jit(solution)/shard_map/ppermute | solution.py:20
  51.0 8.6 %copy-start.10 = (f32[3,4,64,384]{3,2,1,0:T(8,128)S(1)}, f32[3,4,64,384]{3,2,1,0:T(8,128)}, u32[]{:S(2)}) copy-start(f32[3,4,64,384]{3,2,1,0:T(8,128)} %param.9) | copy-start | bytes 3538948
where the time goes:
time: 418 us; the launch traced here: 416 us
  other arithmetic  177 us (42%)
  local copies, waits for them, and re-layouts  105 us (25%)
  blocking collectives  51.1 us (12%)
  matrix products  45.4 us (11%)
  starting transfers between devices  25.6 us (6%)
  waiting for transfers between devices  11.3 us (3%)
    scatter-add x1, other arithmetic, local(): jax.ops.segment_sum(row_values, flat_ids, num_segments=cycle_total)  168 us
    gather x2, local copies, waits for them, and re-layouts, local(): potential = jnp.take(cycle_potential, cycle_id, axis=1)  89.5 us
    psum x1, blocking collectives, local(): totals = lax.psum(cycle_sums, ('lat', 'rad'))  51.1 us
    ppermute x4, starting transfers between devices, with_halo(): lax.ppermute(lax.slice_in_dim(block, block.shape[dim] - width, None, axis...  17.1 us
    dot_general x2, matrix products, apply_operator(): jnp.einsum('rcd,drab->crab', layer_coupling, center, precision=HIGHEST)  16.9 us
    dot_general x1, matrix products, local(): coefficients = scale * jnp.dot(cycle_means, basis.T, precision=HIGHEST)  14.7 us
    dot_general x1, matrix products, local(): cycle_potential = scale * jnp.dot(modes, basis, precision=HIGHEST)  13.9 us
    ppermute x4, starting transfers between devices, with_halo(): lax.ppermute(lax.slice_in_dim(block, 0, width, axis=dim), axis, backward)  8.51 us
  transfers between devices with their start and end apart: 8, of which 6 were waited for; matrix products, arithmetic and copies ran while one was open for 1% of the time, Pallas kernels for 0%

commit v1 on v0

v1 whole, which is shorter than its diff:
```python
import functools
import math

import jax
import jax.numpy as jnp
import numpy as np
from jax import lax
from jax.experimental import pallas as pl
from jax.experimental.pallas import tpu as pltpu
from jax.sharding import PartitionSpec as P

SWEEPS = 2
OMEGA = 0.8
LEAST_COUNT = 32
LANES = 128
SUB = 8
PAD = 8
COEFS = 16
VMEM_LIMIT = 40 * 1024 * 1024

VMEM = pl.BlockSpec(memory_space=pltpu.VMEM)
SMEM = pl.BlockSpec(memory_space=pltpu.SMEM)
ANY = pl.BlockSpec(memory_space=pl.ANY)


def basis_table(degrees, cycles):
    groups = degrees // SUB
    degree = np.arange(degrees, dtype=np.int64)[:, None]
    cycle = np.arange(cycles, dtype=np.int64)[None, :]
    phase = degree * (2 * cycle + 1) % (4 * cycles)
    table = np.cos(np.pi * phase / (2.0 * cycles)).astype(np.float32)
    table = table.reshape(SUB, groups, cycles // LANES, LANES).transpose(2, 1, 0, 3)
    return np.ascontiguousarray(table.reshape(cycles // LANES, degrees, LANES))


def iota(shape, dim):
    return lax.broadcasted_iota(jnp.int32, shape, dim)


def lane_gather(values, index):
    return jnp.take_along_axis(values, index, axis=1, mode="promise_in_bounds")


def layer_scalars(layer, lid, stiff, coup):
    material = lid[layer]
    mu = stiff[material]
    return mu, [[coup[material, c, d] for d in range(3)] for c in range(3)]


def coefficient_rows(mu, k, width=LANES):
    row = iota((COEFS, width), 0)
    top = jnp.zeros((COEFS, width), jnp.float32)
    below = jnp.ones((COEFS, width), jnp.float32)
    for c in range(3):
        diag = 6.0 * mu + k[c][c]
        others = [d for d in range(3) if d != c]
        entries = [(c, 1.0), (3 + c, mu), (6 + 2 * c, k[c][others[0]]), (7 + 2 * c, k[c][others[1]])]
        for at, value in entries:
            top = jnp.where(row == at, OMEGA * value, top)
            below = jnp.where(row == at, diag, below)
    return top / below


def spread(row, width):
    full = jnp.broadcast_to(row, (SUB, LANES))
    return jnp.concatenate([full] * (width // LANES), axis=1)


def beside(current, before, after):
    width = current.shape[1]
    sub, col = iota(current.shape, 0), iota(current.shape, 1)
    up = jnp.where(sub == 0, jnp.broadcast_to(before, current.shape), pltpu.roll(current, 1, 0))
    down = jnp.where(sub == SUB - 1, jnp.broadcast_to(after, current.shape), pltpu.roll(current, SUB - 1, 0))
    left = jnp.where(col == 0, 0.0, pltpu.roll(current, 1, 1))
    right = jnp.where(col == width - 1, 0.0, pltpu.roll(current, width - 1, 1))
    return (up + down) + (left + right)


def relax(c, centers, neighbours, force, rows):
    d0, d1 = [d for d in range(3) if d != c]
    value = rows[c] * force + rows[3 + c] * neighbours
    value = value - (rows[6 + 2 * c] * centers[d0] + rows[7 + 2 * c] * centers[d1])
    return value + (1.0 - OMEGA) * centers[c]


def analysis_kernel(
    disp, forc, lid, stiff, coup, ids, cnt, tbl,
    up, dn, pay, held, coef_out,
    ut, ub, uf, ft, fb, st, sb, ue, fe, tab, cur, far_sem, near_sem, tab_sem,
):
    layers, rows, width = disp.shape[1:]
    chunks = cnt.shape[0]
    groups = tbl.shape[1] // SUB
    per_row = width // LANES
    lat, lats = lax.axis_index("lat"), lax.axis_size("lat")
    rad, rads = lax.axis_index("rad"), lax.axis_size("rad")
    bottom = rad == 0
    edge = jnp.where(bottom, 0, layers - 1)
    inner = jnp.where(bottom, 1, layers - 2)
    deep = jnp.where(bottom, 2, layers - 3)
    inside = pl.ds(PAD, rows)

    near = [
        pltpu.make_async_copy(disp.at[:, edge], ut.at[:, inside], near_sem.at[0]),
        pltpu.make_async_copy(disp.at[:, inner], ub.at[:, inside], near_sem.at[1]),
        pltpu.make_async_copy(disp.at[0, deep], uf.at[inside], near_sem.at[2]),
        pltpu.make_async_copy(forc.at[:, edge], ft.at[:, inside], near_sem.at[3]),
        pltpu.make_async_copy(forc.at[0, inner], fb.at[inside], near_sem.at[4]),
    ]
    for copy in near:
        copy.start()
    edges = [
        pltpu.make_async_copy(disp.at[:, :, pl.ds(0, SUB)], ue.at[0], near_sem.at[5]),
        pltpu.make_async_copy(disp.at[:, :, pl.ds(rows - SUB, SUB)], ue.at[1], near_sem.at[6]),
        pltpu.make_async_copy(forc.at[:, :, pl.ds(0, SUB)], fe.at[0], near_sem.at[7]),
        pltpu.make_async_copy(forc.at[:, :, pl.ds(rows - SUB, SUB)], fe.at[1], near_sem.at[8]),
    ]
    for copy in edges:
        copy.start()
    table = [pltpu.make_async_copy(tbl.at[q], tab.at[q], tab_sem.at[q]) for q in range(chunks)]
    for copy in table:
        copy.start()
    bulk = [
        pltpu.make_async_copy(disp.at[:, layers - 1], up.at[0], far_sem.at[0]),
        pltpu.make_async_copy(disp.at[:, layers - 2], up.at[1], far_sem.at[1]),
        pltpu.make_async_copy(forc.at[:, layers - 1], up.at[2], far_sem.at[2]),
        pltpu.make_async_copy(disp.at[:, 0], dn.at[0], far_sem.at[3]),
        pltpu.make_async_copy(disp.at[:, 1], dn.at[1], far_sem.at[4]),
        pltpu.make_async_copy(forc.at[:, 0], dn.at[2], far_sem.at[5]),
    ]
    for copy in bulk:
        copy.start()

    blank = jnp.zeros((SUB, width), jnp.float32)
    for ref in (ut, ub, ft):
        for c in range(3):
            ref[c, 0:PAD, :] = blank
            ref[c, PAD + rows:, :] = blank
    for ref in (uf, fb):
        ref[0:PAD, :] = blank
        ref[PAD + rows:, :] = blank

    parity = lax.rem(rad, 2)
    coef_low = coefficient_rows(*layer_scalars(0, lid, stiff, coup))
    coef_high = coefficient_rows(*layer_scalars(layers - 1, lid, stiff, coup))
    coef_out[0] = jnp.where(parity == 0, coef_high, coef_low)
    coef_out[1] = jnp.where(parity == 0, coef_low, coef_high)
    cur[0] = jnp.where(bottom, coef_low, coef_high)
    cur[1] = coefficient_rows(*layer_scalars(inner, lid, stiff, coup))

    lane = iota((1, LANES), 1)
    counts = cnt[...]
    ends = counts
    step = 1
    while step < LANES:
        ends = ends + jnp.where(iota(counts.shape, 1) >= step, pltpu.roll(ends, step, 1), 0)
        step *= 2
    run = jnp.zeros((1, 1), jnp.int32)
    end_rows = []
    for q in range(chunks):
        row = ends[q:q + 1, :]
        end_rows.append(jnp.broadcast_to(row + run, (SUB, LANES)))
        run = run + row[:, LANES - 1:]

    sub8, lane8 = iota((SUB, LANES), 0), iota((SUB, LANES), 1)
    first_id = jnp.broadcast_to(ids[0:1, 0:1], (SUB, LANES))
    last_id = jnp.broadcast_to(ids[rows - 1:rows, width - 1:width], (SUB, LANES))
    before = sub8 < 2
    index = jnp.where(before, first_id - 1 - lane8, last_id + lane8)
    place, part = jnp.bitwise_and(index, LANES - 1), jnp.right_shift(index, 7)
    limits = jnp.where(before, 0, 2 ** 30)
    for q in range(chunks):
        limits = jnp.where(part == q, lane_gather(end_rows[q], place), limits)
    limits = jnp.where(before, limits, -limits)
    wide_sub = iota((SUB, width), 0)
    wide_before = wide_sub < 2
    row_of = lat * rows + jnp.where(wide_before, wide_sub - 2, wide_sub - 2 + rows)
    point = row_of * width + iota((SUB, width), 1)
    point = jnp.where(wide_before, point, -1 - point)
    passed = jnp.zeros((SUB, width), jnp.int32)
    for i in range(2 * width // LEAST_COUNT + 2):
        limit = jnp.broadcast_to(limits[:, i:i + 1], (SUB, width))
        passed = passed + jnp.where(point < limit, 1, 0)
    wide = lambda x: jnp.concatenate([x] * per_row, axis=1)
    spill_ids = jnp.where(wide_before, wide(first_id) - passed, wide(last_id) + passed)
    spill_ids = jnp.where(wide_sub < 4, spill_ids, 0)

    for copy in near:
        copy.wait()

    total = rows // SUB + 2
    outer = [spread(cur[0, j:j + 1, :], width) for j in range(12)]
    inward = [spread(cur[1, j:j + 1, :], width) for j in range(12)]
    mu_inner = inward

    def group(ref, g):
        return ref[SUB * g:SUB * g + SUB, :]

    def lateral(ref, g):
        zero = jnp.zeros((1, width), jnp.float32)
        row_before = ref[SUB * g - 1:SUB * g, :] if g > 0 else zero
        row_after = ref[SUB * g + SUB:SUB * g + SUB + 1, :] if g < total - 1 else zero
        return beside(group(ref, g), row_before, row_after)

    for g in range(total):
        tops = [group(ut.at[c], g) for c in range(3)]
        inners = [group(ub.at[c], g) for c in range(3)]
        keep = None
        if g == 0:
            keep = lat > 0
        if g == total - 1:
            keep = lat < lats - 1
        for c in range(3):
            value = relax(c, tops, inners[c] + lateral(ut.at[c], g), group(ft.at[c], g), outer)
            if keep is not None:
                value = jnp.where(keep, value, 0.0)
            st[c, SUB * g:SUB * g + SUB, :] = value
        value = relax(0, inners, tops[0] + group(uf, g) + lateral(ub.at[0], g), group(fb, g), mu_inner)
        if keep is not None:
            value = jnp.where(keep, value, 0.0)
        sb[SUB * g:SUB * g + SUB, :] = value

    def swept(g):
        sts = [group(st.at[c], g) for c in range(3)]
        return relax(0, sts, group(sb, g) + lateral(st.at[0], g), group(ft.at[0], g), outer)

    met = (width - 2) // LEAST_COUNT + 2
    parts = [jnp.zeros((SUB, LANES), jnp.float32) for _ in range(chunks)]

    def add_window(values, cycle, parts):
        first = cycle[:, 0:1]
        offset = cycle - jnp.broadcast_to(first, cycle.shape)
        window = jnp.zeros((SUB, LANES), jnp.float32)
        for t in range(met):
            total_t = jnp.sum(jnp.where(offset == t, values, 0.0), axis=1, keepdims=True)
            window = jnp.where(lane8 == t, jnp.broadcast_to(total_t, window.shape), window)
        start = jnp.broadcast_to(first, (SUB, LANES))
        out = []
        for q in range(chunks):
            at = q * LANES + lane8 - start
            got = lane_gather(window, jnp.bitwise_and(at, LANES - 1))
            out.append(parts[q] + jnp.where(jnp.right_shift(at, 7) == 0, got, 0.0))
        return out

    head, tail = swept(0), swept(total - 1)
    spilled = jnp.where(wide_before, pltpu.roll(head, 2, 0), pltpu.roll(tail, 2, 0))
    weight = jnp.where(wide_before, jnp.where(lat > 0, 1.0, 0.0), jnp.where(lat < lats - 1, 1.0, 0.0))
    parts = add_window(spilled * jnp.where(wide_sub < 4, weight, 0.0), spill_ids, parts)
    for g in range(1, total - 1):
        parts = add_window(swept(g), ids[SUB * (g - 1):SUB * g, :], parts)

    means = []
    for q in range(chunks):
        mean = jnp.sum(parts[q], axis=0, keepdims=True) / counts[q:q + 1, :].astype(jnp.float32)
        means.append(jnp.broadcast_to(mean, (SUB, LANES)))

    for copy in table:
        copy.wait()
    half = jnp.where(bottom, groups, 0)
    result = jnp.zeros((SUB, LANES), jnp.float32)
    for g in range(groups):
        acc = tab[0, SUB * g:SUB * g + SUB, :] * means[0]
        for q in range(1, chunks):
            acc = acc + tab[q, SUB * g:SUB * g + SUB, :] * means[q]
        column = jnp.sum(acc, axis=1, keepdims=True)
        result = jnp.where(lane8 == g + half, jnp.broadcast_to(column, result.shape), result)
    at_end = jnp.logical_or(bottom, rad == rads - 1)
    pay[0:SUB, :] = jnp.concatenate(
        [jnp.where(at_end, result, 0.0)] + [jnp.zeros((SUB, LANES), jnp.float32)] * (per_row - 1), axis=1
    )

    for copy in edges:
        copy.wait()
    tall = 3 * layers

    def pack(side, ref, base):
        first = 0 if side == 0 else SUB - 2
        last = 0 if side == 0 else SUB - 1
        for c in range(3):
            for r in range(layers):
                at = base + 2 * (c * layers + r)
                ref[at:at + 2, :] = ue[side, c, r, first:first + 2, :]
                at = base + 2 * tall + c * layers + r
                ref[at:at + 1, :] = fe[side, c, r, last:last + 1, :]

    @pl.when(lax.rem(lat, 2) == 0)
    def _():
        pack(1, pay, SUB)
        pack(0, held, 0)

    @pl.when(lax.rem(lat, 2) == 1)
    def _():
        pack(0, pay, SUB)
        pack(1, held, 0)

    for copy in bulk:
        copy.wait()


def sweep_kernel(
    disp, forc, lid, stiff, coup, lo, hi, low, high, cor_lo, cor_hi, coef_lo, coef_hi,
    out,
    u, f, s, cf, near_sem,
):
    layers, rows, width = disp.shape[1:]
    lat, lats = lax.axis_index("lat"), lax.axis_size("lat")
    inside = pl.ds(PAD, rows)
    top = layers + 2
    copies = [
        pltpu.make_async_copy(disp, u.at[:, pl.ds(2, layers), inside], near_sem.at[0]),
        pltpu.make_async_copy(lo.at[0], u.at[:, 1, inside], near_sem.at[1]),
        pltpu.make_async_copy(lo.at[1], u.at[:, 0, inside], near_sem.at[2]),
        pltpu.make_async_copy(hi.at[0], u.at[:, top, inside], near_sem.at[3]),
        pltpu.make_async_copy(hi.at[1], u.at[:, top + 1, inside], near_sem.at[4]),
        pltpu.make_async_copy(forc, f.at[:, pl.ds(2, layers), inside], near_sem.at[5]),
        pltpu.make_async_copy(lo.at[2], f.at[:, 1, inside], near_sem.at[6]),
        pltpu.make_async_copy(hi.at[2], f.at[:, top, inside], near_sem.at[7]),
    ]
    for copy in copies:
        copy.start()

    cf[1] = coef_lo[...]
    cf[top] = coef_hi[...]
    for r in range(layers):
        cf[2 + r] = coefficient_rows(*layer_scalars(r, lid, stiff, coup))
    tall = 3 * layers
    end = PAD + rows
    for c in range(3):
        for r in range(layers):
            at = 2 * (c * layers + r)
            u[c, 2 + r, PAD - 2:PAD, :] = low[at:at + 2, :]
            u[c, 2 + r, end:end + 2, :] = high[at:at + 2, :]
            at = 2 * tall + c * layers + r
            f[c, 2 + r, PAD - 1:PAD, :] = low[at:at + 1, :]
            f[c, 2 + r, end:end + 1, :] = high[at:at + 1, :]
        u[c, 1, PAD - 1:PAD, :] = cor_lo[c:c + 1, :]
        u[c, 1, end:end + 1, :] = cor_lo[3 + c:4 + c, :]
        u[c, top, PAD - 1:PAD, :] = cor_hi[c:c + 1, :]
        u[c, top, end:end + 1, :] = cor_hi[3 + c:4 + c, :]
    for copy in copies:
        copy.wait()

    total = rows // SUB + 2

    def update(src, layer, g):
        rows_of = [spread(cf[layer, j:j + 1, :], width) for j in range(12)]
        start = pl.multiple_of(SUB * g, SUB)
        here = pl.ds(start, SUB)
        ahead = pl.ds(jnp.maximum(start - 1, 0), 1)
        behind = pl.ds(jnp.minimum(start + SUB, SUB * total - 1), 1)
        centers = [src[c, layer, here, :] for c in range(3)]
        values = []
        for c in range(3):
            near = src[c, layer - 1, here, :] + src[c, layer + 1, here, :]
            near = near + beside(centers[c], src[c, layer, ahead, :], src[c, layer, behind, :])
            values.append(relax(c, centers, near, f[c, layer, here, :], rows_of))
        return values, here

    def first(step, carry):
        layer, g = 1 + step // total, lax.rem(step, total)
        values, here = update(u, layer, g)
        drop = jnp.logical_or(
            jnp.logical_and(g == 0, lat == 0), jnp.logical_and(g == total - 1, lat == lats - 1)
        )
        for c in range(3):
            s[c, layer, here, :] = jnp.where(drop, 0.0, values[c])
        return carry

    lax.fori_loop(0, (layers + 2) * total, first, 0)

    inner = total - 2

    def second(step, carry):
        layer, g = 2 + step // inner, 1 + lax.rem(step, inner)
        values, here = update(s, layer, g)
        there = pl.ds(pl.multiple_of(SUB * (g - 1), SUB), SUB)
        for c in range(3):
            out[c, layer - 2, there, :] = values[c]
        return carry

    lax.fori_loop(0, layers * inner, second, 0)


def synthesis_kernel(scale, coef, gain_a, gain_b, ids, tbl, out, tab, tab_sem):
    rows, width = ids.shape
    chunks = tbl.shape[0]
    groups = tbl.shape[1] // SUB
    table = [pltpu.make_async_copy(tbl.at[q], tab.at[q], tab_sem.at[q]) for q in range(chunks)]
    for copy in table:
        copy.start()
    lane8 = iota((SUB, LANES), 1)
    here = coef[...]
    other = pltpu.roll(here, groups, 1)
    left = lane8 < groups
    surface = jnp.where(left, here, other)
    core = jnp.where(left, other, here)
    modes = (gain_a[...] * surface + gain_b[...] * core) * scale
    for copy in table:
        copy.wait()
    zero = jnp.zeros((SUB, LANES), jnp.float32)
    sums = [[zero] * chunks for _ in range(2)]
    for g in range(groups):
        factors = [
            jnp.broadcast_to(modes[:, k * groups + g:k * groups + g + 1], (SUB, LANES)) for k in range(2)
        ]
        for q in range(chunks):
            block = tab[q, SUB * g:SUB * g + SUB, :]
            for k in range(2):
                sums[k][q] = sums[k][q] + factors[k] * block
    for k in range(2):
        for q in range(chunks):
            sums[k][q] = jnp.broadcast_to(jnp.sum(sums[k][q], axis=0, keepdims=True), (SUB, LANES))
    for a in range(rows // SUB):
        for b in range(width // LANES):
            spot = (slice(SUB * a, SUB * a + SUB), slice(LANES * b, LANES * b + LANES))
            cycle = ids[spot]
            place, part = jnp.bitwise_and(cycle, LANES - 1), jnp.right_shift(cycle, 7)
            values = [zero, zero]
            for q in range(chunks):
                chosen = part == q
                for k in range(2):
                    values[k] = jnp.where(chosen, lane_gather(sums[k][q], place), values[k])
            for k in range(2):
                out[(k,) + spot] = values[k]


def even_pairs(count):
    return [(i, i ^ 1) for i in range(count)]


def odd_pairs(count):
    pairs = []
    for i in range(1, count, 2):
        j = (i + 1) % count
        pairs += [(i, j), (j, i)]
    return pairs


def local(displacement, forcing, layer_id, stiffness, coupling, cycle_id, cycle_count, gravity):
    _, layers, rows, width = displacement.shape
    cycles, degrees = cycle_count.shape[0], gravity.shape[2]
    chunks, groups = cycles // LANES, degrees // SUB
    if 2 * groups != LANES or layers < 3:
        raise ValueError("unsupported sizes")
    lat, lats = lax.axis_index("lat"), lax.axis_size("lat")
    rad, rads = lax.axis_index("rad"), lax.axis_size("rad")
    lat_odd, rad_odd = lat % 2 == 1, rad % 2 == 1
    f32 = jnp.float32
    table = jnp.asarray(basis_table(degrees, cycles))
    tall = 3 * layers
    padded = rows + 2 * PAD
    edge_rows = -(-3 * tall // SUB) * SUB
    face = jax.ShapeDtypeStruct((3, 3, rows, width), f32)
    params = pltpu.CompilerParams(vmem_limit_bytes=VMEM_LIMIT)

    up, dn, pay, held, coefs = pl.pallas_call(
        analysis_kernel,
        out_shape=(
            face, face,
            jax.ShapeDtypeStruct((SUB + edge_rows, width), f32),
            jax.ShapeDtypeStruct((edge_rows, width), f32),
            jax.ShapeDtypeStruct((2, COEFS, LANES), f32),
        ),
        in_specs=[ANY, ANY, SMEM, SMEM, SMEM, VMEM, VMEM, ANY],
        out_specs=(ANY, ANY, VMEM, VMEM, VMEM),
        scratch_shapes=[
            pltpu.VMEM((3, padded, width), f32),
            pltpu.VMEM((3, padded, width), f32),
            pltpu.VMEM((padded, width), f32),
            pltpu.VMEM((3, padded, width), f32),
            pltpu.VMEM((padded, width), f32),
            pltpu.VMEM((3, padded, width), f32),
            pltpu.VMEM((padded, width), f32),
            pltpu.VMEM((2, 3, layers, SUB, width), f32),
            pltpu.VMEM((2, 3, layers, SUB, width), f32),
            pltpu.VMEM((chunks, degrees, LANES), f32),
            pltpu.VMEM((2, COEFS, LANES), f32),
            pltpu.SemaphoreType.DMA((6,)),
            pltpu.SemaphoreType.DMA((9,)),
            pltpu.SemaphoreType.DMA((chunks,)),
        ],
        compiler_params=params,
        name="analysis",
    )(displacement, forcing, layer_id, stiffness, coupling, cycle_id, cycle_count.reshape(chunks, LANES), table)

    low_far = lax.ppermute(up, "rad", [(i, i + 1) for i in range(rads - 1)])
    high_far = lax.ppermute(dn, "rad", [(i + 1, i) for i in range(rads - 1)])

    butterfly = lats == 4 and rads == 8
    coef = pay[:SUB, :LANES]
    got1 = lax.ppermute(pay, "lat", even_pairs(lats))
    if butterfly:
        coef = coef + got1[:SUB, :LANES]
    else:
        coef = lax.psum(coef, ("lat", "rad"))
    strip = jnp.concatenate([coef, jnp.zeros((SUB, width - LANES), f32)], axis=1)
    got2 = lax.ppermute(jnp.concatenate([strip, held], axis=0), "lat", odd_pairs(lats))
    if butterfly:
        coef = coef + got2[:SUB, :LANES]
    edge1, edge2 = got1[SUB:], got2[SUB:]
    low = jnp.where(lat > 0, jnp.where(lat_odd, edge1, edge2), 0.0)
    high = jnp.where(lat < lats - 1, jnp.where(lat_odd, edge2, edge1), 0.0)

    def corners(layer):
        picks = [low[2 * (c * layers + layer) + 1][None] for c in range(3)]
        picks += [high[2 * (c * layers + layer)][None] for c in range(3)]
        return jnp.concatenate(picks + [jnp.zeros((2, width), f32)], axis=0)

    def split(block):
        return jnp.concatenate(jnp.split(block, width // LANES, axis=1), axis=0)

    corner_low, corner_high = split(corners(0)), split(corners(layers - 1))
    send1 = jnp.where(rad_odd, corner_low, corner_high)
    send2 = jnp.where(rad_odd, corner_high, corner_low)
    got3 = lax.ppermute(jnp.concatenate([coef, coefs[0], send1], axis=0), "rad", even_pairs(rads))
    if butterfly:
        coef = coef + got3[:SUB]
    got4 = lax.ppermute(jnp.concatenate([coef, coefs[1], send2], axis=0), "rad", odd_pairs(rads))
    if butterfly:
        coef = coef + got4[:SUB]
        coef = coef + lax.ppermute(coef, "rad", [(0, 3), (7, 4), (2, 5), (5, 2), (1, 6), (6, 1)])

    below = jnp.where(rad > 0, jnp.where(rad_odd, got3, got4), 0.0)
    above = jnp.where(rad < rads - 1, jnp.where(rad_odd, got4, got3), 0.0)

    def join(block):
        return jnp.concatenate(jnp.split(block, width // LANES, axis=0), axis=1)

    corner_at = SUB + COEFS
    smoothed = pl.pallas_call(
        sweep_kernel,
        out_shape=jax.ShapeDtypeStruct(displacement.shape, f32),
        in_specs=[ANY, ANY, SMEM, SMEM, SMEM, ANY, ANY] + [VMEM] * 6,
        out_specs=VMEM,
        scratch_shapes=[
            pltpu.VMEM((3, layers + 4, padded, width), f32),
            pltpu.VMEM((3, layers + 4, padded, width), f32),
            pltpu.VMEM((3, layers + 4, padded, width), f32),
            pltpu.VMEM((layers + 4, COEFS, LANES), f32),
            pltpu.SemaphoreType.DMA((8,)),
        ],
        compiler_params=params,
        name="sweeps",
    )(
        displacement, forcing, layer_id, stiffness, coupling, low_far, high_far, low, high,
        join(below[corner_at:]), join(above[corner_at:]), below[SUB:corner_at], above[SUB:corner_at],
    )

    shaped = gravity.reshape(2, 2, SUB, groups)
    gain_a = jnp.concatenate([shaped[0, 0], shaped[1, 0]], axis=1)
    gain_b = jnp.concatenate([shaped[0, 1], shaped[1, 1]], axis=1)
    potential = pl.pallas_call(
        functools.partial(synthesis_kernel, 2.0 / cycles),
        out_shape=jax.ShapeDtypeStruct((2, rows, width), f32),
        in_specs=[VMEM, VMEM, VMEM, VMEM, ANY],
        out_specs=VMEM,
        scratch_shapes=[
            pltpu.VMEM((chunks, degrees, LANES), f32),
            pltpu.SemaphoreType.DMA((chunks,)),
        ],
        compiler_params=params,
        name="synthesis",
    )(coef, gain_a, gain_b, cycle_id, table)
    return smoothed, potential


def solution(mesh):
    in_specs = (
        P(None, "rad", "lat", None),
        P(None, "rad", "lat", None),
        P("rad"),
        P(),
        P(),
        P("lat", None),
        P(),
        P(),
    )
    out_specs = (P(None, "rad", "lat", None), P(None, "lat", None))
    return jax.shard_map(local, mesh=mesh, in_specs=in_specs, out_specs=out_specs, check_vma=False)
```

time: 418 us -> 58.1 us (0.14)
  other arithmetic: 177 us -> 2.2 us
  local copies, waits for them, and re-layouts: 105 us -> 8.96 us
  blocking collectives: 51.1 us -> 0 us
  matrix products: 45.4 us -> 0 us
  Pallas kernels: 0 us -> 20.9 us
  starting transfers between devices: 25.6 us -> 17 us
    scatter-add x1 -> x0, other arithmetic: 168 us -> none  [local(): jax.ops.segment_sum(row_values, flat_ids, num_segments=cycle_total)]
    gather x3 -> x0, local copies, waits for them, and re-layouts: 90.1 us -> none  [the longest x2 89.5 us: local(): potential = jnp.take(cycle_potential, cycle_id, axis=1)]
    psum x1 -> x0, blocking collectives: 51.1 us -> none  [local(): totals = lax.psum(cycle_sums, ('lat', 'rad'))]
    dot_general x4 -> x0, matrix products: 45.4 us -> none  [the longest x2 16.9 us: apply_operator(): jnp.einsum('rcd,drab->crab', layer_coupling, center, precision=HIGHEST)]
    pallas_call x0 -> x3, Pallas kernels: none -> 20.9 us  [the longest x1 13.4 us: local(): pl.pallas_call(sweep_kernel, out_shape=jax.ShapeDtypeStruct(displacement....]
    ppermute x8 -> x7, starting transfers between devices: 25.6 us -> 17 us  [the longest x1 4.79 us: local(): lax.ppermute(coef, 'rad', [(0, 3), (7, 4), (2, 5), (5, 2), (1, 6), (6, 1)])]
    another operation x2 -> x1, local copies, waits for them, and re-layouts: 6.89 us -> 0.01 us  [the longest x1 6.88 us: local(): boundary = jnp.stack([surface, bottom])]
    concatenate x4 -> x6, other arithmetic: 6.9 us -> 1.49 us  [the longest x1 0.7 us: local(): jnp.concatenate([coef, coefs[0], send1], axis=0)]
  transfers between devices with their start and end apart: 8 -> 7, of which waited for: 6 -> 4; matrix products, arithmetic and copies ran while one was open for 1% -> 5% of each run, Pallas kernels for 0% -> 4%
where the time goes in v1:
time: 58.1 us; the launch traced here: 57.5 us
  Pallas kernels  20.9 us (36%)
  starting transfers between devices  17 us (29%)
  local copies, waits for them, and re-layouts  8.96 us (15%)
  waiting for transfers between devices  7.58 us (13%)
  other arithmetic  2.2 us (4%)
  between operations  0.9 us (2%)
    pallas_call x1, Pallas kernels, local(): pl.pallas_call(sweep_kernel, out_shape=jax.ShapeDtypeStruct(displacement....  13.4 us
    unnamed x31, local copies, waits for them, and re-layouts  8.17 us
    pallas_call x1, Pallas kernels, local(): pl.pallas_call(analysis_kernel, out_shape=(face, face, jax.ShapeDtypeStru...  5.13 us
    ppermute x1, starting transfers between devices, local(): lax.ppermute(coef, 'rad', [(0, 3), (7, 4), (2, 5), (5, 2), (1, 6), (6, 1)])  4.79 us
    ppermute x1, starting transfers between devices, local(): low_far = lax.ppermute(up, 'rad', [(i, i + 1) for i in range(rads - 1)])  4.03 us
    ppermute x1, starting transfers between devices, local(): lax.ppermute(jnp.concatenate([coef, coefs[1], send2], axis=0), 'rad', odd...  2.88 us
    pallas_call x1, Pallas kernels, local(): pl.pallas_call(functools.partial(synthesis_kernel, 2.0 / cycles), out_sha...  2.35 us
    ppermute x1, waiting for transfers between devices, local(): lax.ppermute(jnp.concatenate([coef, coefs[1], send2], axis=0), 'rad', odd...  2.31 us
  transfers between devices with their start and end apart: 7, of which 4 were waited for; matrix products, arithmetic and copies ran while one was open for 5% of the time, Pallas kernels for 4%

profile of v1, /device:TPU:1, one launch (start us, length us, event | category | flops | bytes accessed | tf_op | source)
XLA Modules:
  0.0 57.5 jit_solution(3060725321008921273)
XLA Ops:
  0.6 0.8 %copy.12.coup = f32[12,3,3]{2,1,0:T(4,128)S(1)} copy(f32[12,3,3]{0,2,1:T(4,128)} %param.13) | data formatting | bytes 864 | tf_op args[4]
  1.4 0.0 copy-start
  1.4 1.9 %copy-done = f32[12,512,128]{2,1,0:T(8,128)S(1)} copy-done((f32[12,512,128]{2,1,0:T(8,128)S(1)}, f32[12,512,128]{2,1,0:T(8,128)}, u32[]{:S(2)}) %copy-start) | copy-done | bytes 3145752
  3.3 0.0 copy-start.2
  3.3 1.3 %copy-done.2 = f32[3,4,64,384]{3,2,1,0:T(8,128)S(1)} copy-done((f32[3,4,64,384]{3,2,1,0:T(8,128)S(1)}, f32[3,4,64,384]{3,2,1,0:T(8,128)}, u32[]{:S(2)}) %copy-start.2) | copy-done | bytes 1179672
  4.6 0.0 copy-start.4
  4.6 1.3 %copy-done.4 = f32[3,4,64,384]{3,2,1,0:T(8,128)S(1)} copy-done((f32[3,4,64,384]{3,2,1,0:T(8,128)S(1)}, f32[3,4,64,384]{3,2,1,0:T(8,128)}, u32[]{:S(2)}) %copy-start.4) | copy-done | bytes 1179672
  5.9 0.9 %copy-done.6 = s32[64,384]{1,0:T(8,128)S(1)} copy-done((s32[64,384]{1,0:T(8,128)S(1)}, s32[64,384]{1,0:T(8,128)}, u32[]{:S(2)}) %copy-start.6) | copy-done | bytes 98328
  6.8 0.7 %copy-done.8 = s32[1536]{0:T(1024)S(1)} copy-done((s32[1536]{0:T(1024)S(1)}, s32[1536]{0:T(1024)}, u32[]{:S(2)}) %copy-start.8) | copy-done | bytes 6168
  7.5 0.7 %copy-done.9 = s32[4]{0:T(128)S(1)} copy-done((s32[4]{0:T(128)S(1)}, s32[4]{0:T(128)}, u32[]{:S(2)}) %copy-start.9) | copy-done | bytes 40
  8.1 0.7 %copy-done.11 = f32[12]{0:T(128)S(1)} copy-done((f32[12]{0:T(128)S(1)}, f32[12]{0:T(128)}, u32[]{:S(2)}) %copy-start.11) | copy-done | bytes 72
  8.8 5.1 %analysis.1 = (f32[3,3,64,384]{3,2,1,0:T(8,128)}, f32[3,3,64,384]{3,2,1,0:T(8,128)}, f32[48,384]{1,0:T(8,128)S(1)}, f32[40,384]{1,0:T(8,128)S(1)}, f32[2,16,128]{2,1,0:T(8,128)S(1)}) custom-call(f32[3,4,64,384]{3,2,1,0:T(8,128)S(1)} %copy-done.2, f32[3,4,64,384]{3,2,1,0:T(8,128)S(1)} %copy-done.4, s32[4]{0:T(128)S(1)} %copy-done.9, f32[12]{0:T(128)S(1)} %copy-done.11, ...), custom_call_target="tpu_custom_call" | custom-call | tf_op jit(solution)/shard_map/analysis/pallas_call | solution.py:456
  13.9 0.0 copy-start.7
  13.9 2.1 %collective-permute-start.2 = (f32[48,384]{1,0:T(8,128)S(1)}, f32[48,384]{1,0:T(8,128)S(1)}, u32[]{:S(2)}, u32[]{:S(2)}) collective-permute-start(f32[48,384]{1,0:T(8,128)S(1)} %get-tuple-element.9), channel_id=1, source_target_pairs={{0,8},{8,0},{16,24},{24,16},{1,9},{9,1},{17,25},{25,17},{2,10},{10... | collective-permute-start | bytes 221192 | tf_op jit(solution)/shard_map/ppermute | solution.py:491
  16.0 4.0 %collective-permute-start = (f32[3,3,64,384]{3,2,1,0:T(8,128)}, f32[3,3,64,384]{3,2,1,0:T(8,128)}, u32[]{:S(2)}, u32[]{:S(2)}) collective-permute-start(f32[3,3,64,384]{3,2,1,0:T(8,128)} %get-tuple-element.7), channel_id=1, source_target_pairs={{0,1},{1,2},{2,3},{3,4},{4,5},{5,6},{6,7},{8,9},{9,10},{10,11},{11... | collective-permute-start | bytes 2654216 | tf_op jit(solution)/shard_map/ppermute | solution.py:486
  20.1 1.9 %collective-permute-start.1 = (f32[3,3,64,384]{3,2,1,0:T(8,128)}, f32[3,3,64,384]{3,2,1,0:T(8,128)}, u32[]{:S(2)}, u32[]{:S(2)}) collective-permute-start(f32[3,3,64,384]{3,2,1,0:T(8,128)} %get-tuple-element.8), channel_id=1, source_target_pairs={{1,0},{2,1},{3,2},{4,3},{5,4},{6,5},{7,6},{9,8},{10,9},{11,10},{12... | collective-permute-start | bytes 2654216 | tf_op jit(solution)/shard_map/ppermute | solution.py:487
  22.0 0.0 collective-permute-done.2
  22.0 0.0 copy-start.13
  22.0 1.3 %collective-permute-start.3 = (f32[48,384]{1,0:T(8,128)S(1)}, f32[48,384]{1,0:T(8,128)S(1)}, u32[]{:S(2)}, u32[]{:S(2)}) collective-permute-start(f32[48,384]{1,0:T(8,128)S(1)} %select_maximum_fusion), channel_id=1, source_target_pairs={{8,16},{16,8},{24,0},{0,24},{9,17},{17,9},{25,1},{1,25},{10,18},{1... | collective-permute-start | bytes 221192 | tf_op jit(solution)/shard_map/ppermute | solution.py:497
  23.3 0.6 %slice_bitcast_fusion = (f32[16,128]{1,0:T(8,128)}, f32[16,128]{1,0:T(8,128)}) fusion(f32[2,16,128]{2,1,0:T(8,128)S(1)} %get-tuple-element.11), kind=kLoop, calls=%fused_computation.14 | loop fusion | bytes 32768 | tf_op jit(solution)/shard_map/squeeze | solution.py:518
  23.9 0.0 copy-done.14
  23.9 0.1 reshape.11
  24.0 0.0 copy-done.13
  24.0 2.2 %collective-permute-done.3 = f32[48,384]{1,0:T(8,128)S(1)} collective-permute-done((f32[48,384]{1,0:T(8,128)S(1)}, f32[48,384]{1,0:T(8,128)S(1)}, u32[]{:S(2)}, u32[]{:S(2)}) %collective-permute-start.3) | collective-permute-done | bytes 73760 | tf_op jit(solution)/shard_map/ppermute | solution.py:497
  26.4 0.7 %slice_add_fusion.2 = f32[8,128]{1,0:T(8,128)S(1)} fusion(f32[8,128]{1,0:T(8,128)} %copy-done.13, f32[48,384]{1,0:T(8,128)S(1)} %collective-permute-done.3), kind=kLoop, calls=%fused_computation.22 | loop fusion | flops 1024 | bytes 12288 | tf_op jit(solution)/shard_map/add | solution.py:499
  27.0 0.7 %pad_maximum_fusion = f32[48,128]{1,0:T(8,128)S(1)} fusion(f32[24,128]{1,0:T(8,128)S(1)} %get-tuple-element.35, f32[16,128]{1,0:T(8,128)} %get-tuple-element.41, f32[8,128]{1,0:T(8,128)S(1)} %slice_add_fusion.2), kind=kLoop, calls=%fused_computation.4 | loop fusion | flops 12288 | bytes 49152 | tf_op jit(solution)/shard_map/concatenate | solution.py:515
  27.7 0.0 collective-permute-start.4
  27.7 1.2 %collective-permute-done.4 = f32[48,128]{1,0:T(8,128)S(1)} collective-permute-done((f32[48,128]{1,0:T(8,128)S(1)}, f32[48,128]{1,0:T(8,128)S(1)}, u32[]{:S(2)}, u32[]{:S(2)}) %collective-permute-start.4) | collective-permute-done | bytes 24608 | tf_op jit(solution)/shard_map/ppermute | solution.py:515
  28.9 0.7 %pad_maximum_fusion.1 = f32[48,128]{1,0:T(8,128)S(1)} fusion(f32[24,128]{1,0:T(8,128)S(1)} %get-tuple-element.34, f32[16,128]{1,0:T(8,128)} %get-tuple-element.40, f32[8,128]{1,0:T(8,128)S(1)} %slice_add_fusion.1), kind=kLoop, calls=%fused_computation.5 | loop fusion | flops 12288 | bytes 49152 | tf_op jit(solution)/shard_map/concatenate | solution.py:518
  29.6 2.9 %collective-permute-start.5 = (f32[48,128]{1,0:T(8,128)S(1)}, f32[48,128]{1,0:T(8,128)S(1)}, u32[]{:S(2)}, u32[]{:S(2)}) collective-permute-start(f32[48,128]{1,0:T(8,128)S(1)} %pad_maximum_fusion.1), channel_id=1, source_target_pairs={{1,2},{2,1},{3,4},{4,3},{5,6},{6,5},{7,0},{0,7},{9,10},{10,9},{11,... | collective-permute-start | bytes 73736 | tf_op jit(solution)/shard_map/ppermute | solution.py:518
  32.5 0.1 pad_maximum_fusion.6
  32.6 2.3 %collective-permute-done.5 = f32[48,128]{1,0:T(8,128)S(1)} collective-permute-done((f32[48,128]{1,0:T(8,128)S(1)}, f32[48,128]{1,0:T(8,128)S(1)}, u32[]{:S(2)}, u32[]{:S(2)}) %collective-permute-start.5) | collective-permute-done | bytes 24608 | tf_op jit(solution)/shard_map/ppermute | solution.py:518
  34.9 4.8 %collective-permute-start.6 = (f32[8,128]{1,0:T(8,128)S(1)}, f32[8,128]{1,0:T(8,128)S(1)}, u32[]{:S(2)}, u32[]{:S(2)}) collective-permute-start(f32[8,128]{1,0:T(8,128)S(1)} %slice_add_fusion), channel_id=1, source_target_pairs={{0,3},{7,4},{2,5},{5,2},{1,6},{6,1},{8,11},{15,12},{10,13},{13,10}... | collective-permute-start | bytes 12296 | tf_op jit(solution)/shard_map/ppermute | solution.py:521
  39.8 1.9 %collective-permute-done.6 = f32[8,128]{1,0:T(8,128)S(1)} collective-permute-done((f32[8,128]{1,0:T(8,128)S(1)}, f32[8,128]{1,0:T(8,128)S(1)}, u32[]{:S(2)}, u32[]{:S(2)}) %collective-permute-start.6) | collective-permute-done | bytes 4128 | tf_op jit(solution)/shard_map/ppermute | solution.py:521
  41.7 0.0 copy-done.1
  41.7 0.0 copy-done.7
  41.7 0.0 copy-start.3
  41.7 0.0 copy-start.5
  41.7 0.0 copy-start.10
  41.7 0.0 copy-start.12
  41.7 2.3 %synthesis.1 = f32[2,64,384]{2,1,0:T(8,128)} custom-call(f32[8,128]{1,0:T(8,128)S(1)} %add.30.coef, f32[8,128]{1,0:T(8,128)S(1)} %get-tuple-element.54.gain_a, f32[8,128]{1,0:T(8,128)S(1)} %get-tuple-element.55.gain_b, s32[64,384]{1,0:T(8,128)S(1)} %copy-done.7, f32[12,512,128]{2,1,0:T(8,128)S(1)} %copy-done.1), custom_call_target="tpu_custom_call" | custom-call | tf_op jit(solution)/shard_map/synthesis/pallas_call | solution.py:552
  44.1 0.0 collective-permute-done.lo
  44.1 0.0 collective-permute-done.1.hi
  44.1 0.0 copy-done.3
  44.1 0.0 copy-done.5
  44.1 0.0 copy-done.10
  44.1 0.0 copy-done.12
  44.1 13.4 %sweeps.1 = f32[3,4,64,384]{3,2,1,0:T(8,128)} custom-call(f32[3,4,64,384]{3,2,1,0:T(8,128)S(1)} %copy-done.3, f32[3,4,64,384]{3,2,1,0:T(8,128)S(1)} %copy-done.5, s32[4]{0:T(128)S(1)} %copy-done.10, f32[12]{0:T(128)S(1)} %copy-done.12, f32[12,3,3]{2,1,0:T(4,128)S(1)} %copy.12.coup, f32[3,3,64,384]{3,2,1,0:T(8,128)} %collective-permute-done.lo, ...), custom_call_target="tpu_custom_call" | custom-call | tf_op jit(solution)/shard_map/sweeps/pallas_call | solution.py:530
  (27 shorter events, 0.2 us)
Async XLA Ops:
  1.4 1.9 %copy-start = (f32[12,512,128]{2,1,0:T(8,128)S(1)}, f32[12,512,128]{2,1,0:T(8,128)}, u32[]{:S(2)}) copy-start(f32[12,512,128]{2,1,0:T(8,128)} %constant.37.clone.tbl) | copy-start | bytes 9437188
  3.3 1.3 %copy-start.2 = (f32[3,4,64,384]{3,2,1,0:T(8,128)S(1)}, f32[3,4,64,384]{3,2,1,0:T(8,128)}, u32[]{:S(2)}) copy-start(f32[3,4,64,384]{3,2,1,0:T(8,128)} %disp.3) | copy-start | bytes 3538948
  4.6 1.3 %copy-start.4 = (f32[3,4,64,384]{3,2,1,0:T(8,128)S(1)}, f32[3,4,64,384]{3,2,1,0:T(8,128)}, u32[]{:S(2)}) copy-start(f32[3,4,64,384]{3,2,1,0:T(8,128)} %forc.3) | copy-start | bytes 3538948
  5.9 0.9 %copy-start.6 = (s32[64,384]{1,0:T(8,128)S(1)}, s32[64,384]{1,0:T(8,128)}, u32[]{:S(2)}) copy-start(s32[64,384]{1,0:T(8,128)} %ids.3) | copy-start | bytes 294916
  6.8 0.7 %copy-start.8 = (s32[1536]{0:T(1024)S(1)}, s32[1536]{0:T(1024)}, u32[]{:S(2)}) copy-start(s32[1536]{0:T(1024)} %param.15) | copy-start | bytes 18436
  7.5 0.7 %copy-start.9 = (s32[4]{0:T(128)S(1)}, s32[4]{0:T(128)}, u32[]{:S(2)}) copy-start(s32[4]{0:T(128)} %lid.3) | copy-start | bytes 52
  8.1 0.7 %copy-start.11 = (f32[12]{0:T(128)S(1)}, f32[12]{0:T(128)}, u32[]{:S(2)}) copy-start(f32[12]{0:T(128)} %stiff.3) | copy-start | bytes 148
  8.8 15.2 %copy-start.14 = (f32[2,2,512]{2,1,0:T(2,128)S(1)}, f32[2,2,512]{2,1,0:T(2,128)}, u32[]{:S(2)}) copy-start(f32[2,2,512]{2,1,0:T(2,128)} %param.16) | copy-start | bytes 24580
  8.8 32.9 %copy-start.1 = (f32[12,512,128]{2,1,0:T(8,128)S(1)}, f32[12,512,128]{2,1,0:T(8,128)}, u32[]{:S(2)}) copy-start(f32[12,512,128]{2,1,0:T(8,128)} %constant.37.clone.tbl) | copy-start | bytes 9437188
  13.9 27.8 %copy-start.7 = (s32[64,384]{1,0:T(8,128)S(1)}, s32[64,384]{1,0:T(8,128)}, u32[]{:S(2)}) copy-start(s32[64,384]{1,0:T(8,128)} %ids.3) | copy-start | bytes 294916
  13.9 8.1 %collective-permute-start.2 = (f32[48,384]{1,0:T(8,128)S(1)}, f32[48,384]{1,0:T(8,128)S(1)}, u32[]{:S(2)}, u32[]{:S(2)}) collective-permute-start(f32[48,384]{1,0:T(8,128)S(1)} %get-tuple-element.9), channel_id=1, source_target_pairs={{0,8},{8,0},{16,24},{24,16},{1,9},{9,1},{17,25},{25,17},{2,10},{10... | collective-permute-start | bytes 221192 | tf_op jit(solution)/shard_map/ppermute | solution.py:491
  16.0 28.1 %collective-permute-start = (f32[3,3,64,384]{3,2,1,0:T(8,128)}, f32[3,3,64,384]{3,2,1,0:T(8,128)}, u32[]{:S(2)}, u32[]{:S(2)}) collective-permute-start(f32[3,3,64,384]{3,2,1,0:T(8,128)} %get-tuple-element.7), channel_id=1, source_target_pairs={{0,1},{1,2},{2,3},{3,4},{4,5},{5,6},{6,7},{8,9},{9,10},{10,11},{11... | collective-permute-start | bytes 2654216 | tf_op jit(solution)/shard_map/ppermute | solution.py:486
  20.1 24.0 %collective-permute-start.1 = (f32[3,3,64,384]{3,2,1,0:T(8,128)}, f32[3,3,64,384]{3,2,1,0:T(8,128)}, u32[]{:S(2)}, u32[]{:S(2)}) collective-permute-start(f32[3,3,64,384]{3,2,1,0:T(8,128)} %get-tuple-element.8), channel_id=1, source_target_pairs={{1,0},{2,1},{3,2},{4,3},{5,4},{6,5},{7,6},{9,8},{10,9},{11,10},{12... | collective-permute-start | bytes 2654216 | tf_op jit(solution)/shard_map/ppermute | solution.py:487
  22.0 2.0 %copy-start.13 = (f32[8,128]{1,0:T(8,128)}, f32[8,128]{1,0:T(8,128)S(1)}, u32[]{:S(2)}) copy-start(f32[8,128]{1,0:T(8,128)S(1)} %slice_add_fusion.3) | copy-start | bytes 12292
  22.0 4.2 %collective-permute-start.3 = (f32[48,384]{1,0:T(8,128)S(1)}, f32[48,384]{1,0:T(8,128)S(1)}, u32[]{:S(2)}, u32[]{:S(2)}) collective-permute-start(f32[48,384]{1,0:T(8,128)S(1)} %select_maximum_fusion), channel_id=1, source_target_pairs={{8,16},{16,8},{24,0},{0,24},{9,17},{17,9},{25,1},{1,25},{10,18},{1... | collective-permute-start | bytes 221192 | tf_op jit(solution)/shard_map/ppermute | solution.py:497
  27.7 1.2 %collective-permute-start.4 = (f32[48,128]{1,0:T(8,128)S(1)}, f32[48,128]{1,0:T(8,128)S(1)}, u32[]{:S(2)}, u32[]{:S(2)}) collective-permute-start(f32[48,128]{1,0:T(8,128)S(1)} %pad_maximum_fusion), channel_id=1, source_target_pairs={{0,1},{1,0},{2,3},{3,2},{4,5},{5,4},{6,7},{7,6},{8,9},{9,8},{10,11... | collective-permute-start | bytes 73736 | tf_op jit(solution)/shard_map/ppermute | solution.py:515
  29.6 5.3 %collective-permute-start.5 = (f32[48,128]{1,0:T(8,128)S(1)}, f32[48,128]{1,0:T(8,128)S(1)}, u32[]{:S(2)}, u32[]{:S(2)}) collective-permute-start(f32[48,128]{1,0:T(8,128)S(1)} %pad_maximum_fusion.1), channel_id=1, source_target_pairs={{1,2},{2,1},{3,4},{4,3},{5,6},{6,5},{7,0},{0,7},{9,10},{10,9},{11,... | collective-permute-start | bytes 73736 | tf_op jit(solution)/shard_map/ppermute | solution.py:518
  34.9 6.8 %collective-permute-start.6 = (f32[8,128]{1,0:T(8,128)S(1)}, f32[8,128]{1,0:T(8,128)S(1)}, u32[]{:S(2)}, u32[]{:S(2)}) collective-permute-start(f32[8,128]{1,0:T(8,128)S(1)} %slice_add_fusion), channel_id=1, source_target_pairs={{0,3},{7,4},{2,5},{5,2},{1,6},{6,1},{8,11},{15,12},{10,13},{13,10}... | collective-permute-start | bytes 12296 | tf_op jit(solution)/shard_map/ppermute | solution.py:521
  41.7 2.4 %copy-start.3 = (f32[3,4,64,384]{3,2,1,0:T(8,128)S(1)}, f32[3,4,64,384]{3,2,1,0:T(8,128)}, u32[]{:S(2)}) copy-start(f32[3,4,64,384]{3,2,1,0:T(8,128)} %disp.3) | copy-start | bytes 3538948
  41.7 2.4 %copy-start.5 = (f32[3,4,64,384]{3,2,1,0:T(8,128)S(1)}, f32[3,4,64,384]{3,2,1,0:T(8,128)}, u32[]{:S(2)}) copy-start(f32[3,4,64,384]{3,2,1,0:T(8,128)} %forc.3) | copy-start | bytes 3538948
  41.7 2.4 %copy-start.10 = (s32[4]{0:T(128)S(1)}, s32[4]{0:T(128)}, u32[]{:S(2)}) copy-start(s32[4]{0:T(128)} %lid.3) | copy-start | bytes 52
  41.7 2.4 %copy-start.12 = (f32[12]{0:T(128)S(1)}, f32[12]{0:T(128)}, u32[]{:S(2)}) copy-start(f32[12]{0:T(128)} %stiff.3) | copy-start | bytes 148

commit v2 on v0

v2 whole, which is shorter than its diff:
```python
import functools
import math

import jax
import jax.numpy as jnp
import numpy as np
from jax import lax
from jax.experimental import pallas as pl
from jax.experimental.pallas import tpu as pltpu
from jax.sharding import PartitionSpec as P

SWEEPS = 2
OMEGA = 0.8
LEAST_COUNT = 32
LANES = 128
SUB = 8
PAD = 8
COEFS = 16
BATCH = 5
VMEM_LIMIT = 16 * 1024 * 1024

VMEM = pl.BlockSpec(memory_space=pltpu.VMEM)
SMEM = pl.BlockSpec(memory_space=pltpu.SMEM)
HBM = pl.BlockSpec(memory_space=pltpu.HBM)
ANY = pl.BlockSpec(memory_space=pl.ANY)


def basis_table(degrees, cycles):
    groups = degrees // SUB
    degree = np.arange(degrees, dtype=np.int64)[:, None]
    cycle = np.arange(cycles, dtype=np.int64)[None, :]
    phase = degree * (2 * cycle + 1) % (4 * cycles)
    table = np.cos(np.pi * phase / (2.0 * cycles)).astype(np.float32)
    table = table.reshape(SUB, groups, cycles // LANES, LANES).transpose(2, 1, 0, 3)
    return np.ascontiguousarray(table.reshape(cycles // LANES, degrees, LANES))


def iota(shape, dim):
    return lax.broadcasted_iota(jnp.int32, shape, dim)


def lane_gather(values, index):
    return jnp.take_along_axis(values, index, axis=1, mode="promise_in_bounds")


def layer_scalars(layer, lid, stiff, coup):
    material = lid[layer]
    mu = stiff[material]
    return mu, [[coup[c, d, material] for d in range(3)] for c in range(3)]


def coefficient_rows(mu, k, width=LANES):
    row = iota((COEFS, width), 0)
    top = jnp.zeros((COEFS, width), jnp.float32)
    below = jnp.ones((COEFS, width), jnp.float32)
    for c in range(3):
        diag = 6.0 * mu + k[c][c]
        others = [d for d in range(3) if d != c]
        entries = [(c, 1.0), (3 + c, mu), (6 + 2 * c, k[c][others[0]]), (7 + 2 * c, k[c][others[1]])]
        for at, value in entries:
            top = jnp.where(row == at, OMEGA * value, top)
            below = jnp.where(row == at, diag, below)
    return top / below


def roll_rows(value, before, after):
    sub = iota(value.shape, 0)
    up = jnp.where(sub == 0, jnp.broadcast_to(before, value.shape), pltpu.roll(value, 1, 0))
    down = jnp.where(sub == SUB - 1, jnp.broadcast_to(after, value.shape), pltpu.roll(value, SUB - 1, 0))
    return up + down


def roll_columns(values):
    lane = iota(values[0].shape, 1)
    right = [pltpu.roll(value, 1, 1) for value in values]
    left = [pltpu.roll(value, LANES - 1, 1) for value in values]
    last = len(values) - 1
    return [
        jnp.where(lane == 0, right[j - 1] if j > 0 else 0.0, right[j])
        + jnp.where(lane == LANES - 1, left[j + 1] if j < last else 0.0, left[j])
        for j in range(len(values))
    ]


def relax(c, centers, neighbours, force, rows):
    d0, d1 = [d for d in range(3) if d != c]
    value = rows[c] * force + rows[3 + c] * neighbours
    value = value - (rows[6 + 2 * c] * centers[d0] + rows[7 + 2 * c] * centers[d1])
    return value + (1.0 - OMEGA) * centers[c]


def chunk(j):
    return pl.ds(LANES * j, LANES)


def spans(per_row, ref, *index):
    return [ref[index + (chunk(j),)] for j in range(per_row)]


def lane_scan(values, steps):
    lane = iota(values.shape, 1)
    step = 1
    while step < steps:
        values = values + jnp.where(lane >= step, pltpu.roll(values, step, 1), 0)
        step *= 2
    return values


def analysis_kernel(
    disp, forc, lid, stiff, coup, ids, cnt, tbl,
    up, dn, pay, held, send1, send2, every,
    u, f, cyc, num, tab, mat, s, windows, lids, stiffs, coups, first_ids, last_ids, near_sem, far_sem, tab_sem,
):
    layers, rows, width = disp.shape[1:]
    chunks = cnt.shape[0]
    groups = tbl.shape[1] // SUB
    per_row = width // LANES
    lat, lats = lax.axis_index("lat"), lax.axis_size("lat")
    rad, rads = lax.axis_index("rad"), lax.axis_size("rad")
    bottom = rad == 0
    at_end = jnp.logical_or(bottom, rad == rads - 1)
    edge = jnp.where(bottom, 0, layers - 1)
    inner = jnp.where(bottom, 1, layers - 2)
    deep = jnp.where(bottom, 2, layers - 3)
    total = rows // SUB

    small = [
        pltpu.make_async_copy(lid, lids, near_sem.at[0]),
        pltpu.make_async_copy(stiff, stiffs, near_sem.at[1]),
        pltpu.make_async_copy(coup, coups, near_sem.at[2]),
        pltpu.make_async_copy(ids.at[pl.ds(0, SUB), pl.ds(0, LANES)], first_ids, near_sem.at[3]),
        pltpu.make_async_copy(
            ids.at[pl.ds(rows - SUB, SUB), pl.ds(width - LANES, LANES)], last_ids, near_sem.at[4]
        ),
        pltpu.make_async_copy(cnt, num, near_sem.at[5]),
        pltpu.make_async_copy(ids, cyc, near_sem.at[6]),
    ]
    large = [
        pltpu.make_async_copy(disp, u, near_sem.at[7]),
        pltpu.make_async_copy(forc, f, near_sem.at[8]),
    ]
    table = [pltpu.make_async_copy(tbl.at[q], tab.at[q], tab_sem.at[q]) for q in range(chunks)]
    for copy in small + large + table:
        copy.start()
    bulk = [
        pltpu.make_async_copy(u.at[:, layers - 1], up.at[0], far_sem.at[0]),
        pltpu.make_async_copy(u.at[:, layers - 2], up.at[1], far_sem.at[1]),
        pltpu.make_async_copy(f.at[:, layers - 1], up.at[2], far_sem.at[2]),
        pltpu.make_async_copy(u.at[:, 0], dn.at[0], far_sem.at[3]),
        pltpu.make_async_copy(u.at[:, 1], dn.at[1], far_sem.at[4]),
        pltpu.make_async_copy(f.at[:, 0], dn.at[2], far_sem.at[5]),
    ]
    for copy in small:
        copy.wait()

    for r in range(layers):
        every[r] = coefficient_rows(*layer_scalars(r, lids, stiffs, coups))
    odd = lax.rem(rad, 2) == 1
    send1[...] = every[jnp.where(odd, 0, layers - 1)]
    send2[...] = every[jnp.where(odd, layers - 1, 0)]

    sub8, lane8 = iota((SUB, LANES), 0), iota((SUB, LANES), 1)
    before = sub8 < 2
    zero = jnp.zeros((SUB, LANES), jnp.float32)
    reach = 2 * width // LEAST_COUNT + 2
    first, last = first_ids[0, 0], last_ids[SUB - 1, LANES - 1]

    for copy in large:
        copy.wait()
    for copy in bulk:
        copy.start()
    pay[0:SUB, :] = jnp.zeros((SUB, width), jnp.float32)

    @pl.when(at_end)
    def _():
        own_first = jnp.zeros((SUB, LANES), jnp.int32)
        own_last = own_first
        for j in range(per_row):
            own_first = own_first + jnp.where(cyc[0:SUB, LANES * j:LANES * j + LANES] == first, 1, 0)
            own_last = own_last + jnp.where(cyc[rows - SUB:rows, LANES * j:LANES * j + LANES] == last, 1, 0)

        def total_of(count):
            count = jnp.sum(count.astype(jnp.float32), axis=1, keepdims=True)
            return jnp.broadcast_to(jnp.sum(count, axis=0, keepdims=True), (SUB, LANES)).astype(jnp.int32)

        held_here = jnp.where(before, total_of(own_first), total_of(own_last))
        index = jnp.where(before, first - lane8, last + lane8)
        place, part = jnp.bitwise_and(index, LANES - 1), jnp.right_shift(index, 7)
        lengths = jnp.full((SUB, LANES), 2 ** 20, jnp.int32)
        part_first, part_last = jnp.right_shift(first, 7), jnp.right_shift(last, 7)
        for q in (part_first - 1, part_first, part_last, part_last + 1):
            row = num[pl.ds(jnp.clip(q, 0, chunks - 1), 1), :]
            known = jnp.logical_and(part == q, jnp.logical_and(part >= 0, part < chunks))
            lengths = jnp.where(known, lane_gather(jnp.broadcast_to(row, (SUB, LANES)), place), lengths)
        lengths = lengths - jnp.where(lane8 == 0, held_here, 0)
        limits = lane_scan(lengths, reach)
        caps = [jnp.broadcast_to(limits[:, i:i + 1], (SUB, LANES)) for i in range(reach)]
        spill_ids = []
        for j in range(per_row):
            column = LANES * j + lane8
            away = jnp.where(before, (width - 1 - column) + jnp.where(sub8 == 0, width, 0),
                             column + jnp.where(sub8 == 3, width, 0))
            passed = jnp.zeros((SUB, LANES), jnp.int32)
            for i in range(reach):
                passed = passed + jnp.where(away >= caps[i], 1, 0)
            spill_ids.append(jnp.where(sub8 < 4, jnp.where(before, first - passed, last + passed), 0))

        mat[0] = every[edge]
        mat[1] = every[inner]
        outer = [jnp.broadcast_to(mat[0, j:j + 1, :], (SUB, LANES)) for j in range(12)]
        below = [jnp.broadcast_to(mat[1, j:j + 1, :], (SUB, LANES)) for j in range(12)]

        def rows_of(g):
            return slice(SUB * g, SUB * g + SUB)

        none = jnp.zeros((1, LANES), jnp.float32)

        def lateral(ref, g, index, ends):
            values = spans(per_row, ref, *index, rows_of(g))
            aside = roll_columns(values)
            out = []
            for j in range(per_row):
                above = ref[index + (slice(SUB * g - 1, SUB * g), chunk(j))] if g > 0 else ends[0][j]
                under = ref[index + (slice(SUB * g + SUB, SUB * g + SUB + 1), chunk(j))] if g < total - 1 else ends[1][j]
                out.append(roll_rows(values[j], above, under) + aside[j])
            return out

        nothing = [[none] * per_row] * 2
        for g in range(total):
            here = rows_of(g)
            tops = [spans(per_row, u, c, edge, here) for c in range(3)]
            unders = [spans(per_row, u, c, inner, here) for c in range(3)]
            deeper = spans(per_row, u, 0, deep, here)
            for c in range(3):
                near = lateral(u, g, (c, edge), nothing)
                force = spans(per_row, f, c, edge, here)
                for j in range(per_row):
                    s[c, here, chunk(j)] = relax(
                        c, [top[j] for top in tops], near[j] + unders[c][j], force[j], outer
                    )
            near = lateral(u, g, (0, inner), nothing)
            force = spans(per_row, f, 0, inner, here)
            for j in range(per_row):
                s[3, here, chunk(j)] = relax(
                    0, [under[j] for under in unders], near[j] + tops[0][j] + deeper[j], force[j], below
                )
        low_in = jnp.where(lat > 0, 1.0, 0.0)
        high_in = jnp.where(lat < lats - 1, 1.0, 0.0)
        weight = jnp.where(sub8 == 1, low_in, jnp.where(sub8 == 2, high_in, 0.0))

        def ends_of(ref, index, j):
            low = jnp.broadcast_to(ref[index + (slice(0, 1), chunk(j))], (SUB, LANES))
            high = jnp.broadcast_to(ref[index + (slice(rows - 1, rows), chunk(j))], (SUB, LANES))
            return jnp.where(sub8 == 1, low, jnp.where(sub8 == 2, high, 0.0))

        over = [[outer[3 + c] * ends_of(u, (c, edge), j) * weight for j in range(per_row)] for c in range(3)]
        over_inner = [below[3] * ends_of(u, (0, inner), j) * weight for j in range(per_row)]
        aside = roll_columns(over[0])
        spill = []
        for j in range(per_row):
            shifted = jnp.where(sub8 == 0, pltpu.roll(over[0][j], SUB - 1, 0),
                                jnp.where(sub8 == 3, pltpu.roll(over[0][j], 1, 0), 0.0))
            near = over_inner[j] + aside[j] + shifted + ends_of(s, (0,), j)
            value = relax(0, [over[c][j] for c in range(3)], near, zero, outer)
            spill.append(value * jnp.where(before, low_in, high_in))
        ends = [[over[0][j][1:2, :] for j in range(per_row)], [over[0][j][2:3, :] for j in range(per_row)]]

        met = (width - 2) // LEAST_COUNT + 2

        def window_of(values, cycles):
            start = jnp.broadcast_to(cycles[0][:, 0:1], (SUB, LANES))
            offsets = [cycle - start for cycle in cycles]
            window = zero
            for t in range(met):
                picked = [jnp.where(offset == t, value, 0.0) for offset, value in zip(offsets, values)]
                sum_t = jnp.sum(functools.reduce(jnp.add, picked), axis=1, keepdims=True)
                window = jnp.where(lane8 == t, jnp.broadcast_to(sum_t, (SUB, LANES)), window)
            return window, start

        windowed = [window_of(spill, spill_ids)]
        for g in range(total):
            here = rows_of(g)
            centers = [spans(per_row, s, c, here) for c in range(3)]
            near = lateral(s, g, (0,), ends)
            inners = spans(per_row, s, 3, here)
            force = spans(per_row, f, 0, edge, here)
            values = [
                relax(0, [center[j] for center in centers], near[j] + inners[j], force[j], outer)
                for j in range(per_row)
            ]
            windowed.append(window_of(values, spans(per_row, cyc, here)))
        for i, (window, start) in enumerate(windowed):
            windows[0, i] = window
            windows[1, i] = start.astype(jnp.float32)

        for copy in table:
            copy.wait()
        half = jnp.where(bottom, groups, 0)
        low_part = jnp.right_shift(jnp.maximum(first - reach, 0), 7)
        high_part = jnp.minimum(jnp.right_shift(last + reach, 7), chunks - 1)

        def batch(b, result):
            means = []
            parts = []
            for i in range(BATCH):
                q = low_part + b * BATCH + i
                part = jnp.minimum(q, chunks - 1)
                parts.append(part)
                acc = zero
                for w in range(total + 1):
                    at = q * LANES + lane8 - windows[1, w].astype(jnp.int32)
                    got = lane_gather(windows[0, w], jnp.bitwise_and(at, LANES - 1))
                    acc = acc + jnp.where(jnp.right_shift(at, 7) == 0, got, 0.0)
                mean = jnp.sum(acc, axis=0, keepdims=True) / num[pl.ds(part, 1), :].astype(jnp.float32)
                mean = jnp.where(q < chunks, mean, 0.0)
                means.append(jnp.broadcast_to(mean, (SUB, LANES)))
            for g in range(groups):
                acc = tab[parts[0], SUB * g:SUB * g + SUB, :] * means[0]
                for i in range(1, BATCH):
                    acc = acc + tab[parts[i], SUB * g:SUB * g + SUB, :] * means[i]
                column = jnp.broadcast_to(jnp.sum(acc, axis=1, keepdims=True), (SUB, LANES))
                result = jnp.where(lane8 == g + half, result + column, result)
            return result

        pay[0:SUB, 0:LANES] = lax.fori_loop(0, (high_part - low_part) // BATCH + 1, batch, zero)

    @pl.when(jnp.logical_not(at_end))
    def _():
        for copy in table:
            copy.wait()

    tall = 3 * layers

    def pack(ref, base, near, far):
        for c in range(3):
            for r in range(layers):
                at = base + c * layers + r
                ref[at:at + 1, :] = u[c, r, near:near + 1, :]
                ref[at + tall:at + tall + 1, :] = u[c, r, far:far + 1, :]
                ref[at + 2 * tall:at + 2 * tall + 1, :] = f[c, r, near:near + 1, :]

    @pl.when(lax.rem(lat, 2) == 0)
    def _():
        pack(pay, SUB, rows - 1, rows - 2)
        pack(held, 0, 0, 1)

    @pl.when(lax.rem(lat, 2) == 1)
    def _():
        pack(pay, SUB, 0, 1)
        pack(held, 0, rows - 1, rows - 2)

    for copy in bulk:
        copy.wait()


def sweep_kernel(
    u, f, lo, hi, got1, got2, got3, got4, every,
    out,
    s, rim, edges, cf,
):
    layers, rows, width = u.shape[1:]
    per_row = width // LANES
    total = rows // SUB
    tall = 3 * layers
    lat, lats = lax.axis_index("lat"), lax.axis_size("lat")
    rad, rads = lax.axis_index("rad"), lax.axis_size("rad")
    lat_odd, rad_odd = lax.rem(lat, 2) == 1, lax.rem(rad, 2) == 1
    low_in, high_in = lat > 0, lat < lats - 1
    sub8 = iota((SUB, LANES), 0)

    def side_rows(base, j):
        at = (slice(SUB + base, SUB + base + layers), chunk(j))
        one, two = got1[at], got2[at]
        low = jnp.where(low_in, jnp.where(lat_odd, one, two), 0.0)
        high = jnp.where(high_in, jnp.where(lat_odd, two, one), 0.0)
        return jnp.concatenate([low, high], axis=0)

    below = lambda at: jnp.where(rad > 0, jnp.where(rad_odd, got3[at], got4[at]), 0.0)
    above = lambda at: jnp.where(rad < rads - 1, jnp.where(rad_odd, got4[at], got3[at]), 0.0)
    cf[0] = below(slice(SUB, SUB + COEFS))
    cf[layers + 1] = above(slice(SUB, SUB + COEFS))
    for r in range(layers):
        cf[1 + r] = every[r]
    corner_low = [below(slice(SUB + COEFS + SUB * j, SUB + COEFS + SUB * j + SUB)) for j in range(per_row)]
    corner_high = [above(slice(SUB + COEFS + SUB * j, SUB + COEFS + SUB * j + SUB)) for j in range(per_row)]

    def coefficients(layer):
        return [jnp.broadcast_to(cf[layer, j:j + 1, :], (SUB, LANES)) for j in range(12)]

    near_rows = [[side_rows(c * layers, j) for j in range(per_row)] for c in range(3)]
    mixed = []
    for i in range(12):
        row = jnp.zeros((SUB, LANES), jnp.float32)
        for r in range(layers):
            here = jnp.broadcast_to(cf[1 + r, i:i + 1, :], (SUB, LANES))
            row = jnp.where(jnp.logical_or(sub8 == r, sub8 == layers + r), here, row)
        mixed.append(row)
    keep = jnp.where(sub8 < layers, jnp.where(low_in, 1.0, 0.0), jnp.where(high_in, 1.0, 0.0))
    for c in range(3):
        aside = roll_columns(near_rows[c])
        for j in range(per_row):
            value = near_rows[c][j]
            first_low, first_high = corner_low[j][c:c + 1, :], corner_low[j][3 + c:4 + c, :]
            last_low, last_high = corner_high[j][c:c + 1, :], corner_high[j][3 + c:4 + c, :]
            down = pltpu.roll(value, 1, 0)
            down = jnp.where(sub8 == 0, jnp.broadcast_to(first_low, down.shape), down)
            down = jnp.where(sub8 == layers, jnp.broadcast_to(first_high, down.shape), down)
            rise = pltpu.roll(value, SUB - 1, 0)
            rise = jnp.where(sub8 == layers - 1, jnp.broadcast_to(last_low, rise.shape), rise)
            rise = jnp.where(sub8 == SUB - 1, jnp.broadcast_to(last_high, rise.shape), rise)
            within = jnp.zeros((SUB, LANES), jnp.float32)
            for r in range(layers):
                head = jnp.broadcast_to(u[c, r, 0:1, chunk(j)], within.shape)
                tail = jnp.broadcast_to(u[c, r, rows - 1:rows, chunk(j)], within.shape)
                within = jnp.where(sub8 == r, head, jnp.where(sub8 == layers + r, tail, within))
            near = aside[j] + down + rise + within + side_rows(tall + c * layers, j)
            force = side_rows(2 * tall + c * layers, j)
            value = relax(c, [near_rows[d][j] for d in range(3)], near, force, mixed)
            value = value * keep
            for i in range(2 * layers):
                rim[i, c, :, chunk(j)] = jnp.broadcast_to(value[i:i + 1, :], (SUB, LANES))
                edges[i, c, :, chunk(j)] = jnp.broadcast_to(near_rows[c][j][i:i + 1, :], (SUB, LANES))

    def update(layer, g, center, lower, upper, force, ends):
        rows_here = slice(SUB * g, SUB * g + SUB)
        coef = coefficients(layer)
        values = [[center(c, rows_here, j) for j in range(per_row)] for c in range(3)]
        result = []
        for c in range(3):
            aside = roll_columns(values[c])
            line = []
            for j in range(per_row):
                before = center(c, slice(SUB * g - 1, SUB * g), j) if g > 0 else ends(c, 0, j)
                after = center(c, slice(SUB * g + SUB, SUB * g + SUB + 1), j) if g < total - 1 else ends(c, 1, j)
                near = roll_rows(values[c][j], before, after) + aside[j]
                near = near + (lower(c, rows_here, j) + upper(c, rows_here, j))
                line.append(relax(c, [values[d][j] for d in range(3)], near, force(c, rows_here, j), coef))
            result.append(line)
        return rows_here, result

    def reader(ref, *index):
        def read(c, at, j):
            full = tuple(c if i is None else i for i in index)
            return ref[full + (at, chunk(j))]
        return read

    def first(layer, center, lower, upper, force, ends):
        for g in range(total):
            at, result = update(layer, g, center, lower, upper, force, ends)
            for c in range(3):
                for j in range(per_row):
                    s[c, layer, at, chunk(j)] = result[c][j]

    def rows_beside(layer):
        return lambda c, side, j: edges[layer + layers * side, c, :, chunk(j)]

    def corner_rows(which):
        return lambda c, side, j: (corner_low, corner_high)[which][j][3 * side + c:3 * side + c + 1, :]

    top = layers - 1
    first(0, reader(lo, 0, None), reader(lo, 1, None), reader(u, None, 0), reader(lo, 2, None), corner_rows(0))
    first(1, reader(u, None, 0), reader(lo, 0, None), reader(u, None, 1), reader(f, None, 0), rows_beside(0))

    def middle(r, carry):
        first(r + 1, reader(u, None, r), reader(u, None, r - 1), reader(u, None, r + 1), reader(f, None, r), rows_beside(r))
        return carry

    lax.fori_loop(1, top, middle, 0)
    first(layers, reader(u, None, top), reader(u, None, top - 1), reader(hi, 0, None), reader(f, None, top), rows_beside(top))
    first(layers + 1, reader(hi, 0, None), reader(u, None, top), reader(hi, 1, None), reader(hi, 2, None), corner_rows(1))

    def last(r, carry):
        ends = lambda c, side, j: rim[r + layers * side, c, :, chunk(j)]
        for g in range(total):
            at, result = update(
                r + 1, g, reader(s, None, r + 1), reader(s, None, r), reader(s, None, r + 2), reader(f, None, r), ends
            )
            for c in range(3):
                for j in range(per_row):
                    out[c, r, at, chunk(j)] = result[c][j]
        return carry

    lax.fori_loop(0, layers, last, 0)


def synthesis_kernel(scale, coef, gain_a, gain_b, ids, tab, out, factors):
    rows, width = ids.shape
    chunks = tab.shape[0]
    groups = tab.shape[1] // SUB
    per_row = width // LANES
    lane8 = iota((SUB, LANES), 1)
    here = coef[...]
    other = pltpu.roll(here, groups, 1)
    left = lane8 < groups
    surface = jnp.where(left, here, other)
    core = jnp.where(left, other, here)
    modes = (gain_a[...] * surface + gain_b[...] * core) * scale
    zero = jnp.zeros((SUB, LANES), jnp.float32)
    for i in range(2 * groups):
        factors[i] = jnp.broadcast_to(modes[:, i:i + 1], (SUB, LANES))
    low_part = jnp.right_shift(jnp.min(ids[0:1, 0:LANES]), 7)
    high_part = jnp.right_shift(jnp.max(ids[rows - 1:rows, width - LANES:width]), 7)

    def batch(b, carry):
        parts = [low_part + b * BATCH + i for i in range(BATCH)]
        blocks = [jnp.minimum(part, chunks - 1) for part in parts]
        sums = [[zero] * BATCH for _ in range(2)]
        for g in range(groups):
            for i in range(BATCH):
                block = tab[blocks[i], SUB * g:SUB * g + SUB, :]
                for k in range(2):
                    sums[k][i] = sums[k][i] + factors[k * groups + g] * block
        for k in range(2):
            for i in range(BATCH):
                sums[k][i] = jnp.broadcast_to(jnp.sum(sums[k][i], axis=0, keepdims=True), (SUB, LANES))
        for a in range(rows // SUB):
            for j in range(per_row):
                spot = (slice(SUB * a, SUB * a + SUB), chunk(j))
                cycle = ids[spot]
                place, part = jnp.bitwise_and(cycle, LANES - 1), jnp.right_shift(cycle, 7)
                values = [jnp.where(b == 0, 0.0, out[(k,) + spot]) for k in range(2)]
                for i in range(BATCH):
                    chosen = part == parts[i]
                    for k in range(2):
                        values[k] = jnp.where(chosen, lane_gather(sums[k][i], place), values[k])
                for k in range(2):
                    out[(k,) + spot] = values[k]
        return carry

    lax.fori_loop(0, (high_part - low_part) // BATCH + 1, batch, 0)


def even_pairs(count):
    return [(i, i ^ 1) for i in range(count)]


def odd_pairs(count):
    pairs = []
    for i in range(1, count, 2):
        j = (i + 1) % count
        pairs += [(i, j), (j, i)]
    return pairs


def local(displacement, forcing, layer_id, stiffness, coupling, cycle_id, cycle_count, gravity):
    _, layers, rows, width = displacement.shape
    cycles, degrees = cycle_count.shape[0], gravity.shape[2]
    chunks, groups = cycles // LANES, degrees // SUB
    if 2 * groups != LANES or 2 * layers != SUB:
        raise ValueError("unsupported sizes")
    lat, lats = lax.axis_index("lat"), lax.axis_size("lat")
    rad, rads = lax.axis_index("rad"), lax.axis_size("rad")
    lat_odd, rad_odd = lat % 2 == 1, rad % 2 == 1
    f32 = jnp.float32
    table = jnp.asarray(basis_table(degrees, cycles))
    per_row = width // LANES
    tall = 3 * layers
    edge_rows = -(-3 * tall // SUB) * SUB
    face = jax.ShapeDtypeStruct((3, 3, rows, width), f32)
    grid = (3, layers, rows, width)

    up, dn, pay, held, mine1, mine2, every = pl.pallas_call(
        analysis_kernel,
        out_shape=(
            face, face,
            jax.ShapeDtypeStruct((SUB + edge_rows, width), f32),
            jax.ShapeDtypeStruct((edge_rows, width), f32),
            jax.ShapeDtypeStruct((COEFS, LANES), f32),
            jax.ShapeDtypeStruct((COEFS, LANES), f32),
            jax.ShapeDtypeStruct((layers, COEFS, LANES), f32),
        ),
        in_specs=[HBM] * 8,
        out_specs=(ANY, ANY) + (VMEM,) * 5,
        scratch_shapes=[
            pltpu.VMEM(grid, f32),
            pltpu.VMEM(grid, f32),
            pltpu.VMEM(cycle_id.shape, jnp.int32),
            pltpu.VMEM((chunks, LANES), jnp.int32),
            pltpu.VMEM((chunks, degrees, LANES), f32),
            pltpu.VMEM((2, COEFS, LANES), f32),
            pltpu.VMEM((4, rows, width), f32),
            pltpu.VMEM((2, rows // SUB + 1, SUB, LANES), f32),
            pltpu.SMEM(layer_id.shape, jnp.int32),
            pltpu.SMEM(stiffness.shape, f32),
            pltpu.SMEM(coupling.shape[1:] + coupling.shape[:1], f32),
            pltpu.SMEM((SUB, LANES), jnp.int32),
            pltpu.SMEM((SUB, LANES), jnp.int32),
            pltpu.SemaphoreType.DMA((9,)),
            pltpu.SemaphoreType.DMA((6,)),
            pltpu.SemaphoreType.DMA((chunks,)),
        ],
        compiler_params=pltpu.CompilerParams(vmem_limit_bytes=VMEM_LIMIT),
        name="analysis",
    )(
        *(
            pltpu.with_memory_space_constraint(value, pltpu.HBM)
            for value in (
                displacement, forcing, layer_id, stiffness, jnp.transpose(coupling, (1, 2, 0)), cycle_id,
                cycle_count.reshape(chunks, LANES), table,
            )
        )
    )

    low_far = lax.ppermute(up, "rad", [(i, i + 1) for i in range(rads - 1)])
    high_far = lax.ppermute(dn, "rad", [(i + 1, i) for i in range(rads - 1)])

    butterfly = lats == 4 and rads == 8
    coef = pay[:SUB, :LANES]
    got1 = lax.ppermute(pay, "lat", even_pairs(lats))
    if butterfly:
        coef = coef + got1[:SUB, :LANES]
    else:
        coef = lax.psum(coef, ("lat", "rad"))
    strip = jnp.concatenate([coef, jnp.zeros((SUB, width - LANES), f32)], axis=1)
    got2 = lax.ppermute(jnp.concatenate([strip, held], axis=0), "lat", odd_pairs(lats))
    if butterfly:
        coef = coef + got2[:SUB, :LANES]
    low = jnp.where(lat > 0, jnp.where(lat_odd, got1[SUB:SUB + tall], got2[SUB:SUB + tall]), 0.0)
    high = jnp.where(lat < lats - 1, jnp.where(lat_odd, got2[SUB:SUB + tall], got1[SUB:SUB + tall]), 0.0)

    def corners(layer):
        picks = [side[c * layers + layer][None] for side in (low, high) for c in range(3)]
        block = jnp.concatenate(picks + [jnp.zeros((SUB - 6, width), f32)], axis=0)
        return jnp.concatenate(jnp.split(block, per_row, axis=1), axis=0)

    corner_low, corner_high = corners(0), corners(layers - 1)
    send1 = jnp.where(rad_odd, corner_low, corner_high)
    send2 = jnp.where(rad_odd, corner_high, corner_low)
    got3 = lax.ppermute(jnp.concatenate([coef, mine1, send1], axis=0), "rad", even_pairs(rads))
    if butterfly:
        coef = coef + got3[:SUB]
    far = jnp.concatenate([coef, mine2, send2], axis=0)
    far, low_far, high_far = lax.optimization_barrier((far, low_far, high_far))
    got4 = lax.ppermute(far, "rad", odd_pairs(rads))
    if butterfly:
        coef = coef + got4[:SUB]
        coef = coef + lax.ppermute(coef, "rad", [(0, 3), (7, 4), (2, 5), (5, 2), (1, 6), (6, 1)])

    smoothed = pl.pallas_call(
        sweep_kernel,
        out_shape=jax.ShapeDtypeStruct(displacement.shape, f32),
        in_specs=[VMEM] * 9,
        out_specs=VMEM,
        scratch_shapes=[
            pltpu.VMEM((3, layers + 2, rows, width), f32),
            pltpu.VMEM((2 * layers, 3, SUB, width), f32),
            pltpu.VMEM((2 * layers, 3, SUB, width), f32),
            pltpu.VMEM((layers + 2, COEFS, LANES), f32),
        ],
        compiler_params=pltpu.CompilerParams(vmem_limit_bytes=VMEM_LIMIT),
        name="sweeps",
    )(displacement, forcing, low_far, high_far, got1, got2, got3, got4, every)
    coef, smoothed = lax.optimization_barrier((coef, smoothed))

    shaped = gravity.reshape(2, 2, SUB, groups)
    gain_a = jnp.concatenate([shaped[0, 0], shaped[1, 0]], axis=1)
    gain_b = jnp.concatenate([shaped[0, 1], shaped[1, 1]], axis=1)
    potential = pl.pallas_call(
        functools.partial(synthesis_kernel, 2.0 / cycles),
        out_shape=jax.ShapeDtypeStruct((2, rows, width), f32),
        in_specs=[VMEM] * 5,
        out_specs=VMEM,
        scratch_shapes=[pltpu.VMEM((2 * groups, SUB, LANES), f32)],
        compiler_params=pltpu.CompilerParams(vmem_limit_bytes=VMEM_LIMIT),
        name="synthesis",
    )(coef, gain_a, gain_b, cycle_id, table)
    return smoothed, potential


def solution(mesh):
    in_specs = (
        P(None, "rad", "lat", None),
        P(None, "rad", "lat", None),
        P("rad"),
        P(),
        P(),
        P("lat", None),
        P(),
        P(),
    )
    out_specs = (P(None, "rad", "lat", None), P(None, "lat", None))
    return jax.shard_map(local, mesh=mesh, in_specs=in_specs, out_specs=out_specs, check_vma=False)
```

time: 418 us -> 45.4 us (0.11)
  other arithmetic: 177 us -> 0.13 us
  local copies, waits for them, and re-layouts: 105 us -> 0.2 us
  blocking collectives: 51.1 us -> 0 us
  matrix products: 45.4 us -> 0 us
  Pallas kernels: 0 us -> 10.6 us
  starting transfers between devices: 25.6 us -> 15.8 us
  waiting for transfers between devices: 11.3 us -> 17.6 us
    scatter-add x1 -> x0, other arithmetic: 168 us -> none  [local(): jax.ops.segment_sum(row_values, flat_ids, num_segments=cycle_total)]
    gather x3 -> x0, local copies, waits for them, and re-layouts: 90.1 us -> none  [the longest x2 89.5 us: local(): potential = jnp.take(cycle_potential, cycle_id, axis=1)]
    psum x1 -> x0, blocking collectives: 51.1 us -> none  [local(): totals = lax.psum(cycle_sums, ('lat', 'rad'))]
    dot_general x4 -> x0, matrix products: 45.4 us -> none  [the longest x2 16.9 us: apply_operator(): jnp.einsum('rcd,drab->crab', layer_coupling, center, precision=HIGHEST)]
    pallas_call x0 -> x3, Pallas kernels: none -> 10.6 us  [the longest x1 4.78 us: local(): pl.pallas_call(sweep_kernel, out_shape=jax.ShapeDtypeStruct(displacement....]
    ppermute x8 -> x7, starting transfers between devices: 25.6 us -> 15.8 us  [the longest x1 5.18 us: local(): low_far = lax.ppermute(up, 'rad', [(i, i + 1) for i in range(rads - 1)])]
    another operation x2 -> x1, local copies, waits for them, and re-layouts: 6.89 us -> 0.01 us  [the longest x1 6.88 us: local(): boundary = jnp.stack([surface, bottom])]
    concatenate x4, other arithmetic: 6.9 us -> 0.1 us  [the longest x1 0.08 us: local(): gain_a = jnp.concatenate([shaped[0, 0], shaped[1, 0]], axis=1)]
  transfers between devices with their start and end apart: 8 -> 7, of which waited for: 6 -> 5; matrix products, arithmetic and copies ran while one was open for 1% -> 1% of each run, Pallas kernels for 0% -> 11%
where the time goes in v2:
time: 45.4 us; the launch traced here: 45.2 us
  waiting for transfers between devices  17.6 us (39%)
  starting transfers between devices  15.8 us (35%)
  Pallas kernels  10.6 us (23%)
  between operations  0.83 us (2%)
    ppermute x1, waiting for transfers between devices, local(): low_far = lax.ppermute(up, 'rad', [(i, i + 1) for i in range(rads - 1)])  6.54 us
    ppermute x1, starting transfers between devices, local(): low_far = lax.ppermute(up, 'rad', [(i, i + 1) for i in range(rads - 1)])  5.18 us
    pallas_call x1, Pallas kernels, local(): pl.pallas_call(sweep_kernel, out_shape=jax.ShapeDtypeStruct(displacement....  4.78 us
    ppermute x1, waiting for transfers between devices, local(): high_far = lax.ppermute(dn, 'rad', [(i + 1, i) for i in range(rads - 1)])  4.4 us
    pallas_call x1, Pallas kernels, local(): pl.pallas_call(analysis_kernel, out_shape=(face, face, jax.ShapeDtypeStru...  4.1 us
    ppermute x1, starting transfers between devices, local(): lax.ppermute(coef, 'rad', [(0, 3), (7, 4), (2, 5), (5, 2), (1, 6), (6, 1)])  4.02 us
    ppermute x1, waiting for transfers between devices, local(): got4 = lax.ppermute(far, 'rad', odd_pairs(rads))  3.25 us
    ppermute x1, starting transfers between devices, local(): lax.ppermute(jnp.concatenate([strip, held], axis=0), 'lat', odd_pairs(lats))  2.48 us
  transfers between devices with their start and end apart: 7, of which 5 were waited for; matrix products, arithmetic and copies ran while one was open for 1% of the time, Pallas kernels for 11%

profile of v2, /device:TPU:1, one launch (start us, length us, event | category | flops | bytes accessed | tf_op | source)
XLA Modules:
  0.0 45.2 jit_solution(198573376628876541)
XLA Ops:
  0.6 0.0 copy-start.4
  0.6 0.0 copy-start.1
  0.7 0.0 copy-start.2
  0.7 4.1 %analysis.1 = (f32[3,3,64,384]{3,2,1,0:T(8,128)}, f32[3,3,64,384]{3,2,1,0:T(8,128)}, f32[48,384]{1,0:T(8,128)S(1)}, f32[40,384]{1,0:T(8,128)S(1)}, f32[16,128]{1...) custom-call(f32[3,4,64,384]{3,2,1,0:T(8,128)} %u.1, f32[3,4,64,384]{3,2,1,0:T(8,128)} %f.1, s32[4]{0:T(128)} %lid.1, ...), custom_call_target="tpu_custom_call" | custom-call | tf_op jit(solution)/shard_map/analysis/pallas_call | solution.py:562
  4.8 2.1 %collective-permute-start = (f32[48,384]{1,0:T(8,128)S(1)}, f32[48,384]{1,0:T(8,128)S(1)}, u32[]{:S(2)}, u32[]{:S(2)}) collective-permute-start(f32[48,384]{1,0:T(8,128)S(1)} %get-tuple-element.14), channel_id=1, source_target_pairs={{0,8},{8,0},{16,24},{24,16},{1,9},{9,1},{17,25},{25,17},{2,10},{10... | collective-permute-start | bytes 221192 | tf_op jit(solution)/shard_map/ppermute | solution.py:609
  6.9 1.7 %collective-permute-done.got1 = f32[48,384]{1,0:T(8,128)S(1)} collective-permute-done((f32[48,384]{1,0:T(8,128)S(1)}, f32[48,384]{1,0:T(8,128)S(1)}, u32[]{:S(2)}, u32[]{:S(2)}) %collective-permute-start) | collective-permute-done | bytes 73760 | tf_op jit(solution)/shard_map/ppermute | solution.py:609
  8.6 2.5 %collective-permute-start.1 = (f32[48,384]{1,0:T(8,128)S(1)}, f32[48,384]{1,0:T(8,128)S(1)}, u32[]{:S(2)}, u32[]{:S(2)}) collective-permute-start(f32[48,384]{1,0:T(8,128)S(1)} %select_maximum_fusion), channel_id=1, source_target_pairs={{8,16},{16,8},{24,0},{0,24},{9,17},{17,9},{25,1},{1,25},{10,18},{1... | collective-permute-start | bytes 221192 | tf_op jit(solution)/shard_map/ppermute | solution.py:615
  11.1 5.2 %collective-permute-start.3 = (f32[3,3,64,384]{3,2,1,0:T(8,128)}, f32[3,3,64,384]{3,2,1,0:T(8,128)S(1)}, u32[]{:S(2)}, u32[]{:S(2)}) collective-permute-start(f32[3,3,64,384]{3,2,1,0:T(8,128)} %get-tuple-element.18), channel_id=1, source_target_pairs={{0,1},{1,2},{2,3},{3,4},{4,5},{5,6},{6,7},{8,9},{9,10},{10,11},{11... | collective-permute-start | bytes 2654216 | tf_op jit(solution)/shard_map/ppermute | solution.py:604
  16.3 1.9 %collective-permute-start.4 = (f32[3,3,64,384]{3,2,1,0:T(8,128)}, f32[3,3,64,384]{3,2,1,0:T(8,128)}, u32[]{:S(2)}, u32[]{:S(2)}) collective-permute-start(f32[3,3,64,384]{3,2,1,0:T(8,128)} %get-tuple-element.19), channel_id=1, source_target_pairs={{1,0},{2,1},{3,2},{4,3},{5,4},{6,5},{7,6},{9,8},{10,9},{11,10},{12... | collective-permute-start | bytes 2654216 | tf_op jit(solution)/shard_map/ppermute | solution.py:605
  18.3 0.0 collective-permute-done.1.got2
  18.5 0.1 collective-permute-start.2
  18.5 0.0 copy-done.4
  18.5 0.1 reshape.11
  18.6 1.7 %collective-permute-done.2.got3 = f32[48,128]{1,0:T(8,128)S(1)} collective-permute-done((f32[48,128]{1,0:T(8,128)S(1)}, f32[48,128]{1,0:T(8,128)S(1)}, u32[]{:S(2)}, u32[]{:S(2)}) %collective-permute-start.2) | collective-permute-done | bytes 24608 | tf_op jit(solution)/shard_map/ppermute | solution.py:629
  20.3 6.5 %collective-permute-done.3.lo = f32[3,3,64,384]{3,2,1,0:T(8,128)S(1)} collective-permute-done((f32[3,3,64,384]{3,2,1,0:T(8,128)}, f32[3,3,64,384]{3,2,1,0:T(8,128)S(1)}, u32[]{:S(2)}, u32[]{:S(2)}) %collective-permute-start.3) | collective-permute-done | bytes 884768 | tf_op jit(solution)/shard_map/ppermute | solution.py:604
  26.9 4.4 %collective-permute-done.4.hi = f32[3,3,64,384]{3,2,1,0:T(8,128)} collective-permute-done((f32[3,3,64,384]{3,2,1,0:T(8,128)}, f32[3,3,64,384]{3,2,1,0:T(8,128)}, u32[]{:S(2)}, u32[]{:S(2)}) %collective-permute-start.4) | collective-permute-done | bytes 884768 | tf_op jit(solution)/shard_map/ppermute | solution.py:605
  31.3 0.0 collective-permute-start.5
  31.3 3.2 %collective-permute-done.5.got4 = f32[48,128]{1,0:T(8,128)S(1)} collective-permute-done((f32[48,128]{1,0:T(8,128)S(1)}, f32[48,128]{1,0:T(8,128)S(1)}, u32[]{:S(2)}, u32[]{:S(2)}) %collective-permute-start.5) | collective-permute-done | bytes 24608 | tf_op jit(solution)/shard_map/ppermute | solution.py:634
  34.5 4.0 %collective-permute-start.6 = (f32[8,128]{1,0:T(8,128)S(1)}, f32[8,128]{1,0:T(8,128)S(1)}, u32[]{:S(2)}, u32[]{:S(2)}) collective-permute-start(f32[8,128]{1,0:T(8,128)S(1)} %slice_add_fusion), channel_id=1, source_target_pairs={{0,3},{7,4},{2,5},{5,2},{1,6},{6,1},{8,11},{15,12},{10,13},{13,10}... | collective-permute-start | bytes 12296 | tf_op jit(solution)/shard_map/ppermute | solution.py:637
  38.5 0.1 pad_maximum_fusion.4
  38.6 0.0 copy-done.1
  38.6 0.0 copy-done.2
  38.6 0.0 copy-start
  38.6 0.0 copy-start.3
  38.6 4.8 %sweeps.1 = f32[3,4,64,384]{3,2,1,0:T(8,128)} custom-call(f32[3,4,64,384]{3,2,1,0:T(8,128)S(1)} %copy-done.1, f32[3,4,64,384]{3,2,1,0:T(8,128)S(1)} %copy-done.2, f32[3,3,64,384]{3,2,1,0:T(8,128)S(1)} %collective-permute-done.3.lo, f32[3,3,64,384]{3,2,1,0:T(8,128)} %collective-permute-done.4.hi, f32[48,384]{1,0:T(8,128)S(1)} %collective-permute-done.got1, ...), custom_call_target="tpu_custom_call" | custom-call | tf_op jit(solution)/shard_map/sweeps/pallas_call | solution.py:639
  43.4 0.0 collective-permute-done.6
  43.4 0.0 copy-done
  43.4 0.0 copy-done.3
  43.4 1.8 %synthesis.1 = f32[2,64,384]{2,1,0:T(8,128)} custom-call(f32[8,128]{1,0:T(8,128)S(1)} %add.30.coef, f32[8,128]{1,0:T(8,128)S(1)} %get-tuple-element.58.gain_a, f32[8,128]{1,0:T(8,128)S(1)} %get-tuple-element.59.gain_b, s32[64,384]{1,0:T(8,128)S(1)} %copy-done.3, f32[12,512,128]{2,1,0:T(8,128)S(1)} %copy-done), custom_call_target="tpu_custom_call" | custom-call | tf_op jit(solution)/shard_map/synthesis/pallas_call | solution.py:658
  (17 shorter events, 0.1 us)
Async XLA Ops:
  0.6 17.9 %copy-start.4 = (f32[2,2,512]{2,1,0:T(2,128)S(1)}, f32[2,2,512]{2,1,0:T(2,128)}, u32[]{:S(2)}) copy-start(f32[2,2,512]{2,1,0:T(2,128)} %param.16) | copy-start | bytes 24580
  0.6 38.0 %copy-start.1 = (f32[3,4,64,384]{3,2,1,0:T(8,128)S(1)}, f32[3,4,64,384]{3,2,1,0:T(8,128)}, u32[]{:S(2)}) copy-start(f32[3,4,64,384]{3,2,1,0:T(8,128)} %u.1) | copy-start | bytes 3538948
  0.7 38.0 %copy-start.2 = (f32[3,4,64,384]{3,2,1,0:T(8,128)S(1)}, f32[3,4,64,384]{3,2,1,0:T(8,128)}, u32[]{:S(2)}) copy-start(f32[3,4,64,384]{3,2,1,0:T(8,128)} %f.1) | copy-start | bytes 3538948
  4.8 3.8 %collective-permute-start = (f32[48,384]{1,0:T(8,128)S(1)}, f32[48,384]{1,0:T(8,128)S(1)}, u32[]{:S(2)}, u32[]{:S(2)}) collective-permute-start(f32[48,384]{1,0:T(8,128)S(1)} %get-tuple-element.14), channel_id=1, source_target_pairs={{0,8},{8,0},{16,24},{24,16},{1,9},{9,1},{17,25},{25,17},{2,10},{10... | collective-permute-start | bytes 221192 | tf_op jit(solution)/shard_map/ppermute | solution.py:609
  8.6 9.6 %collective-permute-start.1 = (f32[48,384]{1,0:T(8,128)S(1)}, f32[48,384]{1,0:T(8,128)S(1)}, u32[]{:S(2)}, u32[]{:S(2)}) collective-permute-start(f32[48,384]{1,0:T(8,128)S(1)} %select_maximum_fusion), channel_id=1, source_target_pairs={{8,16},{16,8},{24,0},{0,24},{9,17},{17,9},{25,1},{1,25},{10,18},{1... | collective-permute-start | bytes 221192 | tf_op jit(solution)/shard_map/ppermute | solution.py:615
  11.1 15.7 %collective-permute-start.3 = (f32[3,3,64,384]{3,2,1,0:T(8,128)}, f32[3,3,64,384]{3,2,1,0:T(8,128)S(1)}, u32[]{:S(2)}, u32[]{:S(2)}) collective-permute-start(f32[3,3,64,384]{3,2,1,0:T(8,128)} %get-tuple-element.18), channel_id=1, source_target_pairs={{0,1},{1,2},{2,3},{3,4},{4,5},{5,6},{6,7},{8,9},{9,10},{10,11},{11... | collective-permute-start | bytes 2654216 | tf_op jit(solution)/shard_map/ppermute | solution.py:604
  16.3 14.9 %collective-permute-start.4 = (f32[3,3,64,384]{3,2,1,0:T(8,128)}, f32[3,3,64,384]{3,2,1,0:T(8,128)}, u32[]{:S(2)}, u32[]{:S(2)}) collective-permute-start(f32[3,3,64,384]{3,2,1,0:T(8,128)} %get-tuple-element.19), channel_id=1, source_target_pairs={{1,0},{2,1},{3,2},{4,3},{5,4},{6,5},{7,6},{9,8},{10,9},{11,10},{12... | collective-permute-start | bytes 2654216 | tf_op jit(solution)/shard_map/ppermute | solution.py:605
  18.5 1.9 %collective-permute-start.2 = (f32[48,128]{1,0:T(8,128)S(1)}, f32[48,128]{1,0:T(8,128)S(1)}, u32[]{:S(2)}, u32[]{:S(2)}) collective-permute-start(f32[48,128]{1,0:T(8,128)S(1)} %pad_maximum_fusion), channel_id=1, source_target_pairs={{0,1},{1,0},{2,3},{3,2},{4,5},{5,4},{6,7},{7,6},{8,9},{9,8},{10,11... | collective-permute-start | bytes 73736 | tf_op jit(solution)/shard_map/ppermute | solution.py:629
  31.3 3.3 %collective-permute-start.5 = (f32[48,128]{1,0:T(8,128)S(1)}, f32[48,128]{1,0:T(8,128)S(1)}, u32[]{:S(2)}, u32[]{:S(2)}) collective-permute-start(f32[48,128]{1,0:T(8,128)S(1)} %pad_maximum_fusion.1), channel_id=1, source_target_pairs={{1,2},{2,1},{3,4},{4,3},{5,6},{6,5},{7,0},{0,7},{9,10},{10,9},{11,... | collective-permute-start | bytes 73736 | tf_op jit(solution)/shard_map/ppermute | solution.py:634
  34.5 8.9 %collective-permute-start.6 = (f32[8,128]{1,0:T(8,128)S(1)}, f32[8,128]{1,0:T(8,128)S(1)}, u32[]{:S(2)}, u32[]{:S(2)}) collective-permute-start(f32[8,128]{1,0:T(8,128)S(1)} %slice_add_fusion), channel_id=1, source_target_pairs={{0,3},{7,4},{2,5},{5,2},{1,6},{6,1},{8,11},{15,12},{10,13},{13,10}... | collective-permute-start | bytes 12296 | tf_op jit(solution)/shard_map/ppermute | solution.py:637
  38.6 4.8 %copy-start = (f32[12,512,128]{2,1,0:T(8,128)S(1)}, f32[12,512,128]{2,1,0:T(8,128)}, u32[]{:S(2)}) copy-start(f32[12,512,128]{2,1,0:T(8,128)} %constant.35.clone.tbl.tab) | copy-start | bytes 9437188
  38.6 4.8 %copy-start.3 = (s32[64,384]{1,0:T(8,128)S(1)}, s32[64,384]{1,0:T(8,128)}, u32[]{:S(2)}) copy-start(s32[64,384]{1,0:T(8,128)} %ids.3) | copy-start | bytes 294916

commit v3 on v2

--- a/solution.py
+++ b/solution.py
@@ -106,12 +106,89 @@
     return values
 
 
-def analysis_kernel(
-    disp, forc, lid, stiff, coup, ids, cnt, tbl,
-    up, dn, pay, held, send1, send2, every,
-    u, f, cyc, num, tab, mat, s, windows, lids, stiffs, coups, first_ids, last_ids, near_sem, far_sem, tab_sem,
+def first_sweep_kernel(
+    disp, forc, lid, stiff, coup,
+    u, f, s, kept, up, dn, every,
+    lids, stiffs, coups, u_sem, f_sem, small_sem, face_sem, kept_sem,
 ):
     layers, rows, width = disp.shape[1:]
+    per_row = width // LANES
+    total = rows // SUB
+    small = [
+        pltpu.make_async_copy(lid, lids, small_sem.at[0]),
+        pltpu.make_async_copy(stiff, stiffs, small_sem.at[1]),
+        pltpu.make_async_copy(coup, coups, small_sem.at[2]),
+    ]
+    loads_u = [pltpu.make_async_copy(disp.at[:, r], u.at[:, r], u_sem.at[r]) for r in range(layers)]
+    loads_f = [pltpu.make_async_copy(forc.at[:, r], f.at[:, r], f_sem.at[r]) for r in range(layers)]
+    for copy in small:
+        copy.start()
+    for r in range(layers):
+        loads_u[r].start()
+        loads_f[r].start()
+    for copy in small:
+        copy.wait()
+    for r in range(layers):
+        every[r] = coefficient_rows(*layer_scalars(r, lids, stiffs, coups))
+    none = jnp.zeros((1, LANES), jnp.float32)
+
+    def sweep(layer, lower, upper):
+        coef = [jnp.broadcast_to(every[layer, j:j + 1, :], (SUB, LANES)) for j in range(12)]
+        for g in range(total):
+            here = slice(SUB * g, SUB * g + SUB)
+            values = [spans(per_row, u, c, layer, here) for c in range(3)]
+            for c in range(3):
+                aside = roll_columns(values[c])
+                for j in range(per_row):
+                    at = (c, layer)
+                    before = u[at + (slice(SUB * g - 1, SUB * g), chunk(j))] if g > 0 else none
+                    after = u[at + (slice(SUB * g + SUB, SUB * g + SUB + 1), chunk(j))] if g < total - 1 else none
+                    near = roll_rows(values[c][j], before, after) + aside[j]
+                    if lower is not None:
+                        near = near + u[c, lower, here, chunk(j)]
+                    if upper is not None:
+                        near = near + u[c, upper, here, chunk(j)]
+                    value = relax(c, [values[d][j] for d in range(3)], near, f[c, layer, here, chunk(j)], coef)
+                    s[c, layer, here, chunk(j)] = value
+
+    loads_u[0].wait()
+    loads_f[0].wait()
+    loads_u[1].wait()
+    faces = [pltpu.make_async_copy(u.at[:, 0], dn.at[0], face_sem.at[0])]
+    faces[0].start()
+    sweep(0, None, 1)
+    faces.append(pltpu.make_async_copy(s.at[:, 0], dn.at[1], face_sem.at[1]))
+    faces[1].start()
+    keeps = [pltpu.make_async_copy(s.at[:, r], kept.at[:, r], kept_sem.at[r]) for r in range(layers)]
+    keeps[0].start()
+    top = layers - 1
+    for r in range(2, layers):
+        loads_u[r].wait()
+    for r in range(1, layers):
+        loads_f[r].wait()
+    faces.append(pltpu.make_async_copy(u.at[:, top], up.at[0], face_sem.at[2]))
+    faces[2].start()
+    sweep(top, top - 1, None)
+    faces.append(pltpu.make_async_copy(s.at[:, top], up.at[1], face_sem.at[3]))
+    faces[3].start()
+    keeps[top].start()
+
+    def middle(r, carry):
+        sweep(r, r - 1, r + 1)
+        pltpu.make_async_copy(s.at[:, r], kept.at[:, r], kept_sem.at[r]).start()
+        return carry
+
+    lax.fori_loop(1, top, middle, 0)
+    for copy in faces + keeps:
+        copy.wait()
+
+
+def analysis_kernel(
+    u, f, s, every, ids, cnt, tbl,
+    pay, held, send1, send2,
+    cyc, num, tab, mat, windows, first_ids, last_ids, near_sem, tab_sem,
+):
+    layers, rows, width = u.shape[1:]
     chunks = cnt.shape[0]
     groups = tbl.shape[1] // SUB
     per_row = width // LANES
@@ -121,40 +198,20 @@
     at_end = jnp.logical_or(bottom, rad == rads - 1)
     edge = jnp.where(bottom, 0, layers - 1)
     inner = jnp.where(bottom, 1, layers - 2)
-    deep = jnp.where(bottom, 2, layers - 3)
     total = rows // SUB
 
     small = [
-        pltpu.make_async_copy(lid, lids, near_sem.at[0]),
-        pltpu.make_async_copy(stiff, stiffs, near_sem.at[1]),
-        pltpu.make_async_copy(coup, coups, near_sem.at[2]),
-        pltpu.make_async_copy(ids.at[pl.ds(0, SUB), pl.ds(0, LANES)], first_ids, near_sem.at[3]),
+        pltpu.make_async_copy(ids.at[pl.ds(0, SUB), pl.ds(0, LANES)], first_ids, near_sem.at[0]),
         pltpu.make_async_copy(
-            ids.at[pl.ds(rows - SUB, SUB), pl.ds(width - LANES, LANES)], last_ids, near_sem.at[4]
+            ids.at[pl.ds(rows - SUB, SUB), pl.ds(width - LANES, LANES)], last_ids, near_sem.at[1]
         ),
-        pltpu.make_async_copy(cnt, num, near_sem.at[5]),
-        pltpu.make_async_copy(ids, cyc, near_sem.at[6]),
-    ]
-    large = [
-        pltpu.make_async_copy(disp, u, near_sem.at[7]),
-        pltpu.make_async_copy(forc, f, near_sem.at[8]),
+        pltpu.make_async_copy(cnt, num, near_sem.at[2]),
+        pltpu.make_async_copy(ids, cyc, near_sem.at[3]),
     ]
     table = [pltpu.make_async_copy(tbl.at[q], tab.at[q], tab_sem.at[q]) for q in range(chunks)]
-    for copy in small + large + table:
+    for copy in small + table:
         copy.start()
-    bulk = [
-        pltpu.make_async_copy(u.at[:, layers - 1], up.at[0], far_sem.at[0]),
-        pltpu.make_async_copy(u.at[:, layers - 2], up.at[1], far_sem.at[1]),
-        pltpu.make_async_copy(f.at[:, layers - 1], up.at[2], far_sem.at[2]),
-        pltpu.make_async_copy(u.at[:, 0], dn.at[0], far_sem.at[3]),
-        pltpu.make_async_copy(u.at[:, 1], dn.at[1], far_sem.at[4]),
-        pltpu.make_async_copy(f.at[:, 0], dn.at[2], far_sem.at[5]),
-    ]
-    for copy in small:
-        copy.wait()
-
-    for r in range(layers):
-        every[r] = coefficient_rows(*layer_scalars(r, lids, stiffs, coups))
+
     odd = lax.rem(rad, 2) == 1
     send1[...] = every[jnp.where(odd, 0, layers - 1)]
     send2[...] = every[jnp.where(odd, layers - 1, 0)]
@@ -163,12 +220,9 @@
     before = sub8 < 2
     zero = jnp.zeros((SUB, LANES), jnp.float32)
     reach = 2 * width // LEAST_COUNT + 2
+    for copy in small:
+        copy.wait()
     first, last = first_ids[0, 0], last_ids[SUB - 1, LANES - 1]
-
-    for copy in large:
-        copy.wait()
-    for copy in bulk:
-        copy.start()
     pay[0:SUB, :] = jnp.zeros((SUB, width), jnp.float32)
 
     @pl.when(at_end)
@@ -213,8 +267,6 @@
         def rows_of(g):
             return slice(SUB * g, SUB * g + SUB)
 
-        none = jnp.zeros((1, LANES), jnp.float32)
-
         def lateral(ref, g, index, ends):
             values = spans(per_row, ref, *index, rows_of(g))
             aside = roll_columns(values)
@@ -225,25 +277,6 @@
                 out.append(roll_rows(values[j], above, under) + aside[j])
             return out
 
-        nothing = [[none] * per_row] * 2
-        for g in range(total):
-            here = rows_of(g)
-            tops = [spans(per_row, u, c, edge, here) for c in range(3)]
-            unders = [spans(per_row, u, c, inner, here) for c in range(3)]
-            deeper = spans(per_row, u, 0, deep, here)
-            for c in range(3):
-                near = lateral(u, g, (c, edge), nothing)
-                force = spans(per_row, f, c, edge, here)
-                for j in range(per_row):
-                    s[c, here, chunk(j)] = relax(
-                        c, [top[j] for top in tops], near[j] + unders[c][j], force[j], outer
-                    )
-            near = lateral(u, g, (0, inner), nothing)
-            force = spans(per_row, f, 0, inner, here)
-            for j in range(per_row):
-                s[3, here, chunk(j)] = relax(
-                    0, [under[j] for under in unders], near[j] + tops[0][j] + deeper[j], force[j], below
-                )
         low_in = jnp.where(lat > 0, 1.0, 0.0)
         high_in = jnp.where(lat < lats - 1, 1.0, 0.0)
         weight = jnp.where(sub8 == 1, low_in, jnp.where(sub8 == 2, high_in, 0.0))
@@ -260,7 +293,7 @@
         for j in range(per_row):
             shifted = jnp.where(sub8 == 0, pltpu.roll(over[0][j], SUB - 1, 0),
                                 jnp.where(sub8 == 3, pltpu.roll(over[0][j], 1, 0), 0.0))
-            near = over_inner[j] + aside[j] + shifted + ends_of(s, (0,), j)
+            near = over_inner[j] + aside[j] + shifted + ends_of(s, (0, edge), j)
             value = relax(0, [over[c][j] for c in range(3)], near, zero, outer)
             spill.append(value * jnp.where(before, low_in, high_in))
         ends = [[over[0][j][1:2, :] for j in range(per_row)], [over[0][j][2:3, :] for j in range(per_row)]]
@@ -280,9 +313,9 @@
         windowed = [window_of(spill, spill_ids)]
         for g in range(total):
             here = rows_of(g)
-            centers = [spans(per_row, s, c, here) for c in range(3)]
-            near = lateral(s, g, (0,), ends)
-            inners = spans(per_row, s, 3, here)
+            centers = [spans(per_row, s, c, edge, here) for c in range(3)]
+            near = lateral(s, g, (0, edge), ends)
+            inners = spans(per_row, s, 0, inner, here)
             force = spans(per_row, f, 0, edge, here)
             values = [
                 relax(0, [center[j] for center in centers], near[j] + inners[j], force[j], outer)
@@ -349,19 +382,27 @@
         pack(pay, SUB, 0, 1)
         pack(held, 0, rows - 1, rows - 2)
 
-    for copy in bulk:
-        copy.wait()
-
 
 def sweep_kernel(
-    u, f, lo, hi, got1, got2, got3, got4, every,
+    disp, forc, first, lo, hi, got1, got2, got3, got4, every,
     out,
-    s, rim, edges, cf,
+    s, f, face, fringe, rim, done, cf, in_sem, out_sem,
 ):
-    layers, rows, width = u.shape[1:]
+    layers, rows, width = disp.shape[1:]
     per_row = width // LANES
     total = rows // SUB
     tall = 3 * layers
+    top = layers - 1
+    loads = [
+        pltpu.make_async_copy(disp.at[:, :, pl.ds(0, SUB)], fringe.at[0], in_sem.at[0]),
+        pltpu.make_async_copy(disp.at[:, :, pl.ds(rows - SUB, SUB)], fringe.at[1], in_sem.at[1]),
+        pltpu.make_async_copy(disp.at[:, 0], face.at[0], in_sem.at[2]),
+        pltpu.make_async_copy(disp.at[:, top], face.at[1], in_sem.at[3]),
+        pltpu.make_async_copy(first, s.at[:, pl.ds(1, layers)], in_sem.at[4]),
+        pltpu.make_async_copy(forc, f, in_sem.at[5]),
+    ]
+    for copy in loads:
+        copy.start()
     lat, lats = lax.axis_index("lat"), lax.axis_size("lat")
     rad, rads = lax.axis_index("rad"), lax.axis_size("rad")
     lat_odd, rad_odd = lax.rem(lat, 2) == 1, lax.rem(rad, 2) == 1
@@ -395,6 +436,8 @@
             here = jnp.broadcast_to(cf[1 + r, i:i + 1, :], (SUB, LANES))
             row = jnp.where(jnp.logical_or(sub8 == r, sub8 == layers + r), here, row)
         mixed.append(row)
+    loads[0].wait()
+    loads[1].wait()
     keep = jnp.where(sub8 < layers, jnp.where(low_in, 1.0, 0.0), jnp.where(high_in, 1.0, 0.0))
     for c in range(3):
         aside = roll_columns(near_rows[c])
@@ -410,77 +453,80 @@
             rise = jnp.where(sub8 == SUB - 1, jnp.broadcast_to(last_high, rise.shape), rise)
             within = jnp.zeros((SUB, LANES), jnp.float32)
             for r in range(layers):
-                head = jnp.broadcast_to(u[c, r, 0:1, chunk(j)], within.shape)
-                tail = jnp.broadcast_to(u[c, r, rows - 1:rows, chunk(j)], within.shape)
+                head = jnp.broadcast_to(fringe[0, c, r, 0:1, chunk(j)], within.shape)
+                tail = jnp.broadcast_to(fringe[1, c, r, SUB - 1:SUB, chunk(j)], within.shape)
                 within = jnp.where(sub8 == r, head, jnp.where(sub8 == layers + r, tail, within))
             near = aside[j] + down + rise + within + side_rows(tall + c * layers, j)
             force = side_rows(2 * tall + c * layers, j)
-            value = relax(c, [near_rows[d][j] for d in range(3)], near, force, mixed)
-            value = value * keep
+            value = relax(c, [near_rows[d][j] for d in range(3)], near, force, mixed) * keep
             for i in range(2 * layers):
                 rim[i, c, :, chunk(j)] = jnp.broadcast_to(value[i:i + 1, :], (SUB, LANES))
-                edges[i, c, :, chunk(j)] = jnp.broadcast_to(near_rows[c][j][i:i + 1, :], (SUB, LANES))
-
-    def update(layer, g, center, lower, upper, force, ends):
-        rows_here = slice(SUB * g, SUB * g + SUB)
+
+    def beyond(layer, side, c, j):
+        if layer == 0:
+            return corner_low[j][3 * side + c:3 * side + c + 1, :]
+        if layer == layers + 1:
+            return corner_high[j][3 * side + c:3 * side + c + 1, :]
+        at = layers * side + layer - 1
+        return near_rows[c][j][at:at + 1, :]
+
+    for copy in loads[2:5]:
+        copy.wait()
+    for layer in range(layers + 2):
+        for c in range(3):
+            gain = jnp.broadcast_to(cf[layer, 3 + c:4 + c, :], (SUB, LANES))
+            for j in range(per_row):
+                for g in range(total):
+                    at = (slice(SUB * g, SUB * g + SUB), chunk(j))
+                    value = None
+                    if layer == 0:
+                        value = lo[(1, c) + at] + gain * face[(0, c) + at]
+                    elif layer == layers + 1:
+                        value = hi[(1, c) + at] + gain * face[(1, c) + at]
+                    elif layer in (1, layers) or g in (0, total - 1):
+                        value = s[(c, layer) + at]
+                    if layer == 1:
+                        value = value + gain * lo[(0, c) + at]
+                    if layer == layers:
+                        value = value + gain * hi[(0, c) + at]
+                    if value is None:
+                        continue
+                    if g == 0:
+                        row = jnp.broadcast_to(beyond(layer, 0, c, j), value.shape)
+                        value = value + jnp.where(sub8 == 0, gain * row, 0.0)
+                    if g == total - 1:
+                        row = jnp.broadcast_to(beyond(layer, 1, c, j), value.shape)
+                        value = value + jnp.where(sub8 == SUB - 1, gain * row, 0.0)
+                    s[(c, layer) + at] = value
+
+    loads[5].wait()
+    stores = [pltpu.make_async_copy(done.at[:, r], out.at[:, r], out_sem.at[r]) for r in range(layers)]
+    for r in range(layers):
+        layer = r + 1
         coef = coefficients(layer)
-        values = [[center(c, rows_here, j) for j in range(per_row)] for c in range(3)]
-        result = []
-        for c in range(3):
-            aside = roll_columns(values[c])
-            line = []
-            for j in range(per_row):
-                before = center(c, slice(SUB * g - 1, SUB * g), j) if g > 0 else ends(c, 0, j)
-                after = center(c, slice(SUB * g + SUB, SUB * g + SUB + 1), j) if g < total - 1 else ends(c, 1, j)
-                near = roll_rows(values[c][j], before, after) + aside[j]
-                near = near + (lower(c, rows_here, j) + upper(c, rows_here, j))
-                line.append(relax(c, [values[d][j] for d in range(3)], near, force(c, rows_here, j), coef))
-            result.append(line)
-        return rows_here, result
-
-    def reader(ref, *index):
-        def read(c, at, j):
-            full = tuple(c if i is None else i for i in index)
-            return ref[full + (at, chunk(j))]
-        return read
-
-    def first(layer, center, lower, upper, force, ends):
         for g in range(total):
-            at, result = update(layer, g, center, lower, upper, force, ends)
+            here = slice(SUB * g, SUB * g + SUB)
+            values = [spans(per_row, s, c, layer, here) for c in range(3)]
             for c in range(3):
+                aside = roll_columns(values[c])
                 for j in range(per_row):
-                    s[c, layer, at, chunk(j)] = result[c][j]
-
-    def rows_beside(layer):
-        return lambda c, side, j: edges[layer + layers * side, c, :, chunk(j)]
-
-    def corner_rows(which):
-        return lambda c, side, j: (corner_low, corner_high)[which][j][3 * side + c:3 * side + c + 1, :]
-
-    top = layers - 1
-    first(0, reader(lo, 0, None), reader(lo, 1, None), reader(u, None, 0), reader(lo, 2, None), corner_rows(0))
-    first(1, reader(u, None, 0), reader(lo, 0, None), reader(u, None, 1), reader(f, None, 0), rows_beside(0))
-
-    def middle(r, carry):
-        first(r + 1, reader(u, None, r), reader(u, None, r - 1), reader(u, None, r + 1), reader(f, None, r), rows_beside(r))
-        return carry
-
-    lax.fori_loop(1, top, middle, 0)
-    first(layers, reader(u, None, top), reader(u, None, top - 1), reader(hi, 0, None), reader(f, None, top), rows_beside(top))
-    first(layers + 1, reader(hi, 0, None), reader(u, None, top), reader(hi, 1, None), reader(hi, 2, None), corner_rows(1))
-
-    def last(r, carry):
-        ends = lambda c, side, j: rim[r + layers * side, c, :, chunk(j)]
-        for g in range(total):
-            at, result = update(
-                r + 1, g, reader(s, None, r + 1), reader(s, None, r), reader(s, None, r + 2), reader(f, None, r), ends
-            )
-            for c in range(3):
-                for j in range(per_row):
-                    out[c, r, at, chunk(j)] = result[c][j]
-        return carry
-
-    lax.fori_loop(0, layers, last, 0)
+                    at = (c, layer)
+                    if g > 0:
+                        before = s[at + (slice(SUB * g - 1, SUB * g), chunk(j))]
+                    else:
+                        before = rim[r, c, :, chunk(j)]
+                    if g < total - 1:
+                        after = s[at + (slice(SUB * g + SUB, SUB * g + SUB + 1), chunk(j))]
+                    else:
+                        after = rim[layers + r, c, :, chunk(j)]
+                    near = roll_rows(values[c][j], before, after) + aside[j]
+                    near = near + (s[c, layer - 1, here, chunk(j)] + s[c, layer + 1, here, chunk(j)])
+                    done[c, r, here, chunk(j)] = relax(
+                        c, [values[d][j] for d in range(3)], near, f[c, r, here, chunk(j)], coef
+                    )
+        stores[r].start()
+    for copy in stores:
+        copy.wait()
 
 
 def synthesis_kernel(scale, coef, gain_a, gain_b, ids, tab, out, factors):
@@ -556,53 +602,62 @@
     per_row = width // LANES
     tall = 3 * layers
     edge_rows = -(-3 * tall // SUB) * SUB
-    face = jax.ShapeDtypeStruct((3, 3, rows, width), f32)
-    grid = (3, layers, rows, width)
-
-    up, dn, pay, held, mine1, mine2, every = pl.pallas_call(
+    face = jax.ShapeDtypeStruct((2, 3, rows, width), f32)
+
+    whole = jax.ShapeDtypeStruct(displacement.shape, f32)
+    pinned = [
+        pltpu.with_memory_space_constraint(value, pltpu.HBM)
+        for value in (
+            displacement, forcing, layer_id, stiffness, jnp.transpose(coupling, (1, 2, 0)), cycle_id,
+            cycle_count.reshape(chunks, LANES), table,
+        )
+    ]
+    u, f, swept, kept, up, dn, every = pl.pallas_call(
+        first_sweep_kernel,
+        out_shape=(whole, whole, whole, whole, face, face, jax.ShapeDtypeStruct((layers, COEFS, LANES), f32)),
+        in_specs=[HBM] * 5,
+        out_specs=(VMEM,) * 3 + (HBM,) + (VMEM,) * 3,
+        scratch_shapes=[
+            pltpu.SMEM(layer_id.shape, jnp.int32),
+            pltpu.SMEM(stiffness.shape, f32),
+            pltpu.SMEM(coupling.shape[1:] + coupling.shape[:1], f32),
+            pltpu.SemaphoreType.DMA((layers,)),
+            pltpu.SemaphoreType.DMA((layers,)),
+            pltpu.SemaphoreType.DMA((3,)),
+            pltpu.SemaphoreType.DMA((4,)),
+            pltpu.SemaphoreType.DMA((layers,)),
+        ],
+        compiler_params=pltpu.CompilerParams(vmem_limit_bytes=VMEM_LIMIT),
+        name="first_sweep",
+    )(*pinned[:5])
+
+    low_far = lax.ppermute(up, "rad", [(i, i + 1) for i in range(rads - 1)])
+    high_far = lax.ppermute(dn, "rad", [(i + 1, i) for i in range(rads - 1)])
+
+    pay, held, mine1, mine2 = pl.pallas_call(
         analysis_kernel,
         out_shape=(
-            face, face,
             jax.ShapeDtypeStruct((SUB + edge_rows, width), f32),
             jax.ShapeDtypeStruct((edge_rows, width), f32),
             jax.ShapeDtypeStruct((COEFS, LANES), f32),
             jax.ShapeDtypeStruct((COEFS, LANES), f32),
-            jax.ShapeDtypeStruct((layers, COEFS, LANES), f32),
         ),
-        in_specs=[HBM] * 8,
-        out_specs=(ANY, ANY) + (VMEM,) * 5,
+        in_specs=[VMEM] * 4 + [HBM] * 3,
+        out_specs=(VMEM,) * 4,
         scratch_shapes=[
-            pltpu.VMEM(grid, f32),
-            pltpu.VMEM(grid, f32),
             pltpu.VMEM(cycle_id.shape, jnp.int32),
             pltpu.VMEM((chunks, LANES), jnp.int32),
             pltpu.VMEM((chunks, degrees, LANES), f32),
             pltpu.VMEM((2, COEFS, LANES), f32),
-            pltpu.VMEM((4, rows, width), f32),
             pltpu.VMEM((2, rows // SUB + 1, SUB, LANES), f32),
-            pltpu.SMEM(layer_id.shape, jnp.int32),
-            pltpu.SMEM(stiffness.shape, f32),
-            pltpu.SMEM(coupling.shape[1:] + coupling.shape[:1], f32),
             pltpu.SMEM((SUB, LANES), jnp.int32),
             pltpu.SMEM((SUB, LANES), jnp.int32),
-            pltpu.SemaphoreType.DMA((9,)),
-            pltpu.SemaphoreType.DMA((6,)),
+            pltpu.SemaphoreType.DMA((4,)),
             pltpu.SemaphoreType.DMA((chunks,)),
         ],
         compiler_params=pltpu.CompilerParams(vmem_limit_bytes=VMEM_LIMIT),
         name="analysis",
-    )(
-        *(
-            pltpu.with_memory_space_constraint(value, pltpu.HBM)
-            for value in (
-                displacement, forcing, layer_id, stiffness, jnp.transpose(coupling, (1, 2, 0)), cycle_id,
-                cycle_count.reshape(chunks, LANES), table,
-            )
-        )
-    )
-
-    low_far = lax.ppermute(up, "rad", [(i, i + 1) for i in range(rads - 1)])
-    high_far = lax.ppermute(dn, "rad", [(i + 1, i) for i in range(rads - 1)])
+    )(u, f, swept, every, *pinned[5:])
 
     butterfly = lats == 4 and rads == 8
     coef = pay[:SUB, :LANES]
@@ -612,7 +667,9 @@
     else:
         coef = lax.psum(coef, ("lat", "rad"))
     strip = jnp.concatenate([coef, jnp.zeros((SUB, width - LANES), f32)], axis=1)
-    got2 = lax.ppermute(jnp.concatenate([strip, held], axis=0), "lat", odd_pairs(lats))
+    ahead = jnp.concatenate([strip, held], axis=0)
+    ahead, low_far, high_far = lax.optimization_barrier((ahead, low_far, high_far))
+    got2 = lax.ppermute(ahead, "lat", odd_pairs(lats))
     if butterfly:
         coef = coef + got2[:SUB, :LANES]
     low = jnp.where(lat > 0, jnp.where(lat_odd, got1[SUB:SUB + tall], got2[SUB:SUB + tall]), 0.0)
@@ -629,27 +686,30 @@
     got3 = lax.ppermute(jnp.concatenate([coef, mine1, send1], axis=0), "rad", even_pairs(rads))
     if butterfly:
         coef = coef + got3[:SUB]
-    far = jnp.concatenate([coef, mine2, send2], axis=0)
-    far, low_far, high_far = lax.optimization_barrier((far, low_far, high_far))
-    got4 = lax.ppermute(far, "rad", odd_pairs(rads))
+    got4 = lax.ppermute(jnp.concatenate([coef, mine2, send2], axis=0), "rad", odd_pairs(rads))
     if butterfly:
         coef = coef + got4[:SUB]
         coef = coef + lax.ppermute(coef, "rad", [(0, 3), (7, 4), (2, 5), (5, 2), (1, 6), (6, 1)])
 
     smoothed = pl.pallas_call(
         sweep_kernel,
-        out_shape=jax.ShapeDtypeStruct(displacement.shape, f32),
-        in_specs=[VMEM] * 9,
-        out_specs=VMEM,
+        out_shape=whole,
+        in_specs=[HBM] * 3 + [VMEM] * 7,
+        out_specs=HBM,
         scratch_shapes=[
             pltpu.VMEM((3, layers + 2, rows, width), f32),
+            pltpu.VMEM((3, layers, rows, width), f32),
+            pltpu.VMEM((2, 3, rows, width), f32),
+            pltpu.VMEM((2, 3, layers, SUB, width), f32),
             pltpu.VMEM((2 * layers, 3, SUB, width), f32),
-            pltpu.VMEM((2 * layers, 3, SUB, width), f32),
+            pltpu.VMEM((3, layers, rows, width), f32),
             pltpu.VMEM((layers + 2, COEFS, LANES), f32),
+            pltpu.SemaphoreType.DMA((6,)),
+            pltpu.SemaphoreType.DMA((layers,)),
         ],
         compiler_params=pltpu.CompilerParams(vmem_limit_bytes=VMEM_LIMIT),
         name="sweeps",
-    )(displacement, forcing, low_far, high_far, got1, got2, got3, got4, every)
+    )(*pinned[:2], kept, low_far, high_far, got1, got2, got3, got4, every)
     coef, smoothed = lax.optimization_barrier((coef, smoothed))
 
     shaped = gravity.reshape(2, 2, SUB, groups)

time: 45.4 us -> 38.3 us (0.84)
  waiting for transfers between devices: 17.6 us -> 10.9 us
  Pallas kernels: 10.6 us -> 9.87 us
  starting transfers between devices: 15.8 us -> 16.3 us
    ppermute x1, waiting for transfers between devices: 6.54 us -> 0.01 us  [local(): low_far = lax.ppermute(up, 'rad', [(i, i + 1) for i in range(rads - 1)])]
    ppermute x2, starting transfers between devices: 2.48 us -> 3.51 us  [the longest x1 2.17 us: local(): got2 = lax.ppermute(ahead, 'lat', odd_pairs(lats))]
    ppermute x1, starting transfers between devices: 4.02 us -> 4.91 us  [local(): lax.ppermute(coef, 'rad', [(0, 3), (7, 4), (2, 5), (5, 2), (1, 6), (6, 1)])]
    pallas_call x2 -> x3, Pallas kernels: 8.88 us -> 8.04 us  [the longest x1 3.42 us: local(): pl.pallas_call(sweep_kernel, out_shape=whole, in_specs=[HBM] * 3 + [VMEM]...]
    ppermute x1, starting transfers between devices: 2.11 us -> 1.28 us  [local(): got1 = lax.ppermute(pay, 'lat', even_pairs(lats))]
    ppermute x1, waiting for transfers between devices: 4.4 us -> 3.71 us  [local(): high_far = lax.ppermute(dn, 'rad', [(i + 1, i) for i in range(rads - 1)])]
    ppermute x1, waiting for transfers between devices: 1.68 us -> 1.09 us  [local(): lax.ppermute(jnp.concatenate([coef, mine1, send1], axis=0), 'rad', even_p...]
    ppermute x2, waiting for transfers between devices: 3.25 us -> 3.84 us  [the longest x1 1.94 us: local(): got2 = lax.ppermute(ahead, 'lat', odd_pairs(lats))]
  transfers between devices with their start and end apart: 7 -> 7, of which waited for: 5 -> 5; matrix products, arithmetic and copies ran while one was open for 1% -> 0% of each run, Pallas kernels for 11% -> 14%
where the time goes in v3:
time: 38.3 us; the launch traced here: 38.1 us
  starting transfers between devices  16.3 us (43%)
  waiting for transfers between devices  10.9 us (28%)
  Pallas kernels  9.87 us (26%)
  between operations  0.8 us (2%)
    ppermute x1, starting transfers between devices, local(): lax.ppermute(coef, 'rad', [(0, 3), (7, 4), (2, 5), (5, 2), (1, 6), (6, 1)])  4.91 us
    ppermute x1, starting transfers between devices, local(): low_far = lax.ppermute(up, 'rad', [(i, i + 1) for i in range(rads - 1)])  4.59 us
    ppermute x1, waiting for transfers between devices, local(): high_far = lax.ppermute(dn, 'rad', [(i + 1, i) for i in range(rads - 1)])  3.71 us
    pallas_call x1, Pallas kernels, local(): pl.pallas_call(sweep_kernel, out_shape=whole, in_specs=[HBM] * 3 + [VMEM]...  3.42 us
    pallas_call x1, Pallas kernels, local(): pl.pallas_call(first_sweep_kernel, out_shape=(whole, whole, whole, whole,...  2.59 us
    ppermute x1, waiting for transfers between devices, local(): got1 = lax.ppermute(pay, 'lat', even_pairs(lats))  2.2 us
    ppermute x1, starting transfers between devices, local(): got2 = lax.ppermute(ahead, 'lat', odd_pairs(lats))  2.17 us
    pallas_call x1, Pallas kernels, local(): pl.pallas_call(analysis_kernel, out_shape=(jax.ShapeDtypeStruct((SUB + ed...  2.04 us
  transfers between devices with their start and end apart: 7, of which 5 were waited for; matrix products, arithmetic and copies ran while one was open for 0% of the time, Pallas kernels for 14%

profile of v3, /device:TPU:1, one launch (start us, length us, event | category | flops | bytes accessed | tf_op | source)
XLA Modules:
  0.0 38.1 jit_solution(7059346660238894265)
XLA Ops:
  0.6 2.6 %first_sweep.1 = (f32[3,4,64,384]{3,2,1,0:T(8,128)S(1)}, f32[3,4,64,384]{3,2,1,0:T(8,128)S(1)}, f32[3,4,64,384]{3,2,1,0:T(8,128)S(1)}, f32[3,4,64,384]{3,2,1,0:T...) custom-call(f32[3,4,64,384]{3,2,1,0:T(8,128)} %disp.3, ...), custom_call_target="tpu_custom_call" | custom-call | tf_op jit(solution)/shard_map/first_sweep/pallas_call | solution.py:615
  3.2 4.6 %collective-permute-start.1 = (f32[2,3,64,384]{3,2,1,0:T(8,128)S(1)}, f32[2,3,64,384]{3,2,1,0:T(8,128)S(1)}, u32[]{:S(2)}, u32[]{:S(2)}) collective-permute-start(f32[2,3,64,384]{3,2,1,0:T(8,128)S(1)} %get-tuple-element.24), channel_id=1, source_target_pairs={{0,1},{1,2},{2,3},{3,4},{4,5},{5,6},{6,7},{8,9},{9,10},{10,11},{11... | collective-permute-start | bytes 1769480 | tf_op jit(solution)/shard_map/ppermute | solution.py:634
  7.8 1.9 %collective-permute-start.2 = (f32[2,3,64,384]{3,2,1,0:T(8,128)S(1)}, f32[2,3,64,384]{3,2,1,0:T(8,128)S(1)}, u32[]{:S(2)}, u32[]{:S(2)}) collective-permute-start(f32[2,3,64,384]{3,2,1,0:T(8,128)S(1)} %get-tuple-element.25), channel_id=1, source_target_pairs={{1,0},{2,1},{3,2},{4,3},{5,4},{6,5},{7,6},{9,8},{10,9},{11,10},{12... | collective-permute-start | bytes 1769480 | tf_op jit(solution)/shard_map/ppermute | solution.py:635
  9.8 0.0 copy-start.2
  9.8 2.0 %analysis.1 = (f32[48,384]{1,0:T(8,128)S(1)}, f32[40,384]{1,0:T(8,128)S(1)}, f32[16,128]{1,0:T(8,128)S(1)}, f32[16,128]{1,0:T(8,128)S(1)}) custom-call(f32[3,4,64,384]{3,2,1,0:T(8,128)S(1)} %get-tuple-element.18.u, f32[3,4,64,384]{3,2,1,0:T(8,128)S(1)} %get-tuple-element.19.f, f32[3,4,64,384]{3,2,1,0:T(8,128)S(1)} %get-tuple-element.20.s, ...), custom_call_target="tpu_custom_call" | custom-call | tf_op jit(solution)/shard_map/analysis/pallas_call | solution.py:637
  11.8 1.3 %collective-permute-start = (f32[48,384]{1,0:T(8,128)S(1)}, f32[48,384]{1,0:T(8,128)S(1)}, u32[]{:S(2)}, u32[]{:S(2)}) collective-permute-start(f32[48,384]{1,0:T(8,128)S(1)} %get-tuple-element.22), channel_id=1, source_target_pairs={{0,8},{8,0},{16,24},{24,16},{1,9},{9,1},{17,25},{25,17},{2,10},{10... | collective-permute-start | bytes 221192 | tf_op jit(solution)/shard_map/ppermute | solution.py:664
  13.1 2.2 %collective-permute-done.got1 = f32[48,384]{1,0:T(8,128)S(1)} collective-permute-done((f32[48,384]{1,0:T(8,128)S(1)}, f32[48,384]{1,0:T(8,128)S(1)}, u32[]{:S(2)}, u32[]{:S(2)}) %collective-permute-start) | collective-permute-done | bytes 73760 | tf_op jit(solution)/shard_map/ppermute | solution.py:664
  15.3 0.0 collective-permute-done.1.lo
  15.3 3.7 %collective-permute-done.2.hi = f32[2,3,64,384]{3,2,1,0:T(8,128)S(1)} collective-permute-done((f32[2,3,64,384]{3,2,1,0:T(8,128)S(1)}, f32[2,3,64,384]{3,2,1,0:T(8,128)S(1)}, u32[]{:S(2)}, u32[]{:S(2)}) %collective-permute-start.2) | collective-permute-done | bytes 589856 | tf_op jit(solution)/shard_map/ppermute | solution.py:635
  19.0 2.2 %collective-permute-start.3 = (f32[48,384]{1,0:T(8,128)S(1)}, f32[48,384]{1,0:T(8,128)S(1)}, u32[]{:S(2)}, u32[]{:S(2)}) collective-permute-start(f32[48,384]{1,0:T(8,128)S(1)} %select_maximum_fusion), channel_id=1, source_target_pairs={{8,16},{16,8},{24,0},{0,24},{9,17},{17,9},{25,1},{1,25},{10,18},{1... | collective-permute-start | bytes 221192 | tf_op jit(solution)/shard_map/ppermute | solution.py:672
  21.2 1.9 %collective-permute-done.3.got2 = f32[48,384]{1,0:T(8,128)S(1)} collective-permute-done((f32[48,384]{1,0:T(8,128)S(1)}, f32[48,384]{1,0:T(8,128)S(1)}, u32[]{:S(2)}, u32[]{:S(2)}) %collective-permute-start.3) | collective-permute-done | bytes 73760 | tf_op jit(solution)/shard_map/ppermute | solution.py:672
  23.3 0.1 collective-permute-start.4
  23.4 0.0 copy-done.2
  23.4 0.1 reshape.11
  23.5 1.1 %collective-permute-done.4.got3 = f32[48,128]{1,0:T(8,128)S(1)} collective-permute-done((f32[48,128]{1,0:T(8,128)S(1)}, f32[48,128]{1,0:T(8,128)S(1)}, u32[]{:S(2)}, u32[]{:S(2)}) %collective-permute-start.4) | collective-permute-done | bytes 24608 | tf_op jit(solution)/shard_map/ppermute | solution.py:686
  24.6 1.3 %collective-permute-start.5 = (f32[48,128]{1,0:T(8,128)S(1)}, f32[48,128]{1,0:T(8,128)S(1)}, u32[]{:S(2)}, u32[]{:S(2)}) collective-permute-start(f32[48,128]{1,0:T(8,128)S(1)} %pad_maximum_fusion.1), channel_id=1, source_target_pairs={{1,2},{2,1},{3,4},{4,3},{5,6},{6,5},{7,0},{0,7},{9,10},{10,9},{11,... | collective-permute-start | bytes 73736 | tf_op jit(solution)/shard_map/ppermute | solution.py:689
  25.9 1.9 %collective-permute-done.5.got4 = f32[48,128]{1,0:T(8,128)S(1)} collective-permute-done((f32[48,128]{1,0:T(8,128)S(1)}, f32[48,128]{1,0:T(8,128)S(1)}, u32[]{:S(2)}, u32[]{:S(2)}) %collective-permute-start.5) | collective-permute-done | bytes 24608 | tf_op jit(solution)/shard_map/ppermute | solution.py:689
  27.8 4.9 %collective-permute-start.6 = (f32[8,128]{1,0:T(8,128)S(1)}, f32[8,128]{1,0:T(8,128)S(1)}, u32[]{:S(2)}, u32[]{:S(2)}) collective-permute-start(f32[8,128]{1,0:T(8,128)S(1)} %slice_add_fusion), channel_id=1, source_target_pairs={{0,3},{7,4},{2,5},{5,2},{1,6},{6,1},{8,11},{15,12},{10,13},{13,10}... | collective-permute-start | bytes 12296 | tf_op jit(solution)/shard_map/ppermute | solution.py:692
  32.7 0.1 pad_maximum_fusion.4
  32.8 0.0 copy-start
  32.8 0.0 copy-start.1
  32.8 3.4 %sweeps.1 = f32[3,4,64,384]{3,2,1,0:T(8,128)} custom-call(f32[3,4,64,384]{3,2,1,0:T(8,128)} %disp.3, f32[3,4,64,384]{3,2,1,0:T(8,128)} %forc.3, f32[3,4,64,384]{3,2,1,0:T(8,128)S(1)} %get-tuple-element.29.first, f32[2,3,64,384]{3,2,1,0:T(8,128)S(1)} %collective-permute-done.1.lo, f32[2,3,64,384]{3,2,1,0:T(8,128)S(1)} %collective-permute-done.2.hi, ...), custom_call_target="tpu_custom_call" | custom-call | tf_op jit(solution)/shard_map/sweeps/pallas_call | solution.py:694
  36.3 0.0 collective-permute-done.6
  36.3 0.0 copy-done
  36.3 0.0 copy-done.1
  36.3 1.8 %synthesis.1 = f32[2,64,384]{2,1,0:T(8,128)} custom-call(f32[8,128]{1,0:T(8,128)S(1)} %add.30.coef, f32[8,128]{1,0:T(8,128)S(1)} %get-tuple-element.66.gain_a, f32[8,128]{1,0:T(8,128)S(1)} %get-tuple-element.67.gain_b, s32[64,384]{1,0:T(8,128)S(1)} %copy-done.1, f32[12,512,128]{2,1,0:T(8,128)S(1)} %copy-done), custom_call_target="tpu_custom_call" | custom-call | tf_op jit(solution)/shard_map/synthesis/pallas_call | solution.py:718
  (17 shorter events, 0.1 us)
Async XLA Ops:
  3.2 12.1 %collective-permute-start.1 = (f32[2,3,64,384]{3,2,1,0:T(8,128)S(1)}, f32[2,3,64,384]{3,2,1,0:T(8,128)S(1)}, u32[]{:S(2)}, u32[]{:S(2)}) collective-permute-start(f32[2,3,64,384]{3,2,1,0:T(8,128)S(1)} %get-tuple-element.24), channel_id=1, source_target_pairs={{0,1},{1,2},{2,3},{3,4},{4,5},{5,6},{6,7},{8,9},{9,10},{10,11},{11... | collective-permute-start | bytes 1769480 | tf_op jit(solution)/shard_map/ppermute | solution.py:634
  7.8 11.2 %collective-permute-start.2 = (f32[2,3,64,384]{3,2,1,0:T(8,128)S(1)}, f32[2,3,64,384]{3,2,1,0:T(8,128)S(1)}, u32[]{:S(2)}, u32[]{:S(2)}) collective-permute-start(f32[2,3,64,384]{3,2,1,0:T(8,128)S(1)} %get-tuple-element.25), channel_id=1, source_target_pairs={{1,0},{2,1},{3,2},{4,3},{5,4},{6,5},{7,6},{9,8},{10,9},{11,10},{12... | collective-permute-start | bytes 1769480 | tf_op jit(solution)/shard_map/ppermute | solution.py:635
  9.8 13.6 %copy-start.2 = (f32[2,2,512]{2,1,0:T(2,128)S(1)}, f32[2,2,512]{2,1,0:T(2,128)}, u32[]{:S(2)}) copy-start(f32[2,2,512]{2,1,0:T(2,128)} %param.16) | copy-start | bytes 24580
  11.8 3.5 %collective-permute-start = (f32[48,384]{1,0:T(8,128)S(1)}, f32[48,384]{1,0:T(8,128)S(1)}, u32[]{:S(2)}, u32[]{:S(2)}) collective-permute-start(f32[48,384]{1,0:T(8,128)S(1)} %get-tuple-element.22), channel_id=1, source_target_pairs={{0,8},{8,0},{16,24},{24,16},{1,9},{9,1},{17,25},{25,17},{2,10},{10... | collective-permute-start | bytes 221192 | tf_op jit(solution)/shard_map/ppermute | solution.py:664
  19.0 4.1 %collective-permute-start.3 = (f32[48,384]{1,0:T(8,128)S(1)}, f32[48,384]{1,0:T(8,128)S(1)}, u32[]{:S(2)}, u32[]{:S(2)}) collective-permute-start(f32[48,384]{1,0:T(8,128)S(1)} %select_maximum_fusion), channel_id=1, source_target_pairs={{8,16},{16,8},{24,0},{0,24},{9,17},{17,9},{25,1},{1,25},{10,18},{1... | collective-permute-start | bytes 221192 | tf_op jit(solution)/shard_map/ppermute | solution.py:672
  23.3 1.3 %collective-permute-start.4 = (f32[48,128]{1,0:T(8,128)S(1)}, f32[48,128]{1,0:T(8,128)S(1)}, u32[]{:S(2)}, u32[]{:S(2)}) collective-permute-start(f32[48,128]{1,0:T(8,128)S(1)} %pad_maximum_fusion), channel_id=1, source_target_pairs={{0,1},{1,0},{2,3},{3,2},{4,5},{5,4},{6,7},{7,6},{8,9},{9,8},{10,11... | collective-permute-start | bytes 73736 | tf_op jit(solution)/shard_map/ppermute | solution.py:686
  24.6 3.3 %collective-permute-start.5 = (f32[48,128]{1,0:T(8,128)S(1)}, f32[48,128]{1,0:T(8,128)S(1)}, u32[]{:S(2)}, u32[]{:S(2)}) collective-permute-start(f32[48,128]{1,0:T(8,128)S(1)} %pad_maximum_fusion.1), channel_id=1, source_target_pairs={{1,2},{2,1},{3,4},{4,3},{5,6},{6,5},{7,0},{0,7},{9,10},{10,9},{11,... | collective-permute-start | bytes 73736 | tf_op jit(solution)/shard_map/ppermute | solution.py:689
  27.8 8.4 %collective-permute-start.6 = (f32[8,128]{1,0:T(8,128)S(1)}, f32[8,128]{1,0:T(8,128)S(1)}, u32[]{:S(2)}, u32[]{:S(2)}) collective-permute-start(f32[8,128]{1,0:T(8,128)S(1)} %slice_add_fusion), channel_id=1, source_target_pairs={{0,3},{7,4},{2,5},{5,2},{1,6},{6,1},{8,11},{15,12},{10,13},{13,10}... | collective-permute-start | bytes 12296 | tf_op jit(solution)/shard_map/ppermute | solution.py:692
  32.8 3.5 %copy-start = (f32[12,512,128]{2,1,0:T(8,128)S(1)}, f32[12,512,128]{2,1,0:T(8,128)}, u32[]{:S(2)}) copy-start(f32[12,512,128]{2,1,0:T(8,128)} %constant.35.clone.tbl.tab) | copy-start | bytes 9437188
  32.8 3.5 %copy-start.1 = (s32[64,384]{1,0:T(8,128)S(1)}, s32[64,384]{1,0:T(8,128)}, u32[]{:S(2)}) copy-start(s32[64,384]{1,0:T(8,128)} %ids.3) | copy-start | bytes 294916

commit v4 on v3

--- a/solution.py
+++ b/solution.py
@@ -106,89 +106,13 @@
     return values
 
 
-def first_sweep_kernel(
-    disp, forc, lid, stiff, coup,
-    u, f, s, kept, up, dn, every,
-    lids, stiffs, coups, u_sem, f_sem, small_sem, face_sem, kept_sem,
+def analysis_kernel(
+    disp, forc, lid, stiff, coup, ids, cnt, tbl,
+    kept, face1, face2, pay, send1, send2, every,
+    u, f, s, cyc, num, tab, mat, windows, lids, stiffs, coups, first_ids, last_ids,
+    small_sem, near_sem, u_sem, f_sem, face_sem, kept_sem, tab_sem,
 ):
     layers, rows, width = disp.shape[1:]
-    per_row = width // LANES
-    total = rows // SUB
-    small = [
-        pltpu.make_async_copy(lid, lids, small_sem.at[0]),
-        pltpu.make_async_copy(stiff, stiffs, small_sem.at[1]),
-        pltpu.make_async_copy(coup, coups, small_sem.at[2]),
-    ]
-    loads_u = [pltpu.make_async_copy(disp.at[:, r], u.at[:, r], u_sem.at[r]) for r in range(layers)]
-    loads_f = [pltpu.make_async_copy(forc.at[:, r], f.at[:, r], f_sem.at[r]) for r in range(layers)]
-    for copy in small:
-        copy.start()
-    for r in range(layers):
-        loads_u[r].start()
-        loads_f[r].start()
-    for copy in small:
-        copy.wait()
-    for r in range(layers):
-        every[r] = coefficient_rows(*layer_scalars(r, lids, stiffs, coups))
-    none = jnp.zeros((1, LANES), jnp.float32)
-
-    def sweep(layer, lower, upper):
-        coef = [jnp.broadcast_to(every[layer, j:j + 1, :], (SUB, LANES)) for j in range(12)]
-        for g in range(total):
-            here = slice(SUB * g, SUB * g + SUB)
-            values = [spans(per_row, u, c, layer, here) for c in range(3)]
-            for c in range(3):
-                aside = roll_columns(values[c])
-                for j in range(per_row):
-                    at = (c, layer)
-                    before = u[at + (slice(SUB * g - 1, SUB * g), chunk(j))] if g > 0 else none
-                    after = u[at + (slice(SUB * g + SUB, SUB * g + SUB + 1), chunk(j))] if g < total - 1 else none
-                    near = roll_rows(values[c][j], before, after) + aside[j]
-                    if lower is not None:
-                        near = near + u[c, lower, here, chunk(j)]
-                    if upper is not None:
-                        near = near + u[c, upper, here, chunk(j)]
-                    value = relax(c, [values[d][j] for d in range(3)], near, f[c, layer, here, chunk(j)], coef)
-                    s[c, layer, here, chunk(j)] = value
-
-    loads_u[0].wait()
-    loads_f[0].wait()
-    loads_u[1].wait()
-    faces = [pltpu.make_async_copy(u.at[:, 0], dn.at[0], face_sem.at[0])]
-    faces[0].start()
-    sweep(0, None, 1)
-    faces.append(pltpu.make_async_copy(s.at[:, 0], dn.at[1], face_sem.at[1]))
-    faces[1].start()
-    keeps = [pltpu.make_async_copy(s.at[:, r], kept.at[:, r], kept_sem.at[r]) for r in range(layers)]
-    keeps[0].start()
-    top = layers - 1
-    for r in range(2, layers):
-        loads_u[r].wait()
-    for r in range(1, layers):
-        loads_f[r].wait()
-    faces.append(pltpu.make_async_copy(u.at[:, top], up.at[0], face_sem.at[2]))
-    faces[2].start()
-    sweep(top, top - 1, None)
-    faces.append(pltpu.make_async_copy(s.at[:, top], up.at[1], face_sem.at[3]))
-    faces[3].start()
-    keeps[top].start()
-
-    def middle(r, carry):
-        sweep(r, r - 1, r + 1)
-        pltpu.make_async_copy(s.at[:, r], kept.at[:, r], kept_sem.at[r]).start()
-        return carry
-
-    lax.fori_loop(1, top, middle, 0)
-    for copy in faces + keeps:
-        copy.wait()
-
-
-def analysis_kernel(
-    u, f, s, every, ids, cnt, tbl,
-    pay, held, send1, send2,
-    cyc, num, tab, mat, windows, first_ids, last_ids, near_sem, tab_sem,
-):
-    layers, rows, width = u.shape[1:]
     chunks = cnt.shape[0]
     groups = tbl.shape[1] // SUB
     per_row = width // LANES
@@ -200,7 +124,14 @@
     inner = jnp.where(bottom, 1, layers - 2)
     total = rows // SUB
 
+    top = layers - 1
+    odd = lax.rem(rad, 2) == 1
     small = [
+        pltpu.make_async_copy(lid, lids, small_sem.at[0]),
+        pltpu.make_async_copy(stiff, stiffs, small_sem.at[1]),
+        pltpu.make_async_copy(coup, coups, small_sem.at[2]),
+    ]
+    cycles = [
         pltpu.make_async_copy(ids.at[pl.ds(0, SUB), pl.ds(0, LANES)], first_ids, near_sem.at[0]),
         pltpu.make_async_copy(
             ids.at[pl.ds(rows - SUB, SUB), pl.ds(width - LANES, LANES)], last_ids, near_sem.at[1]
@@ -208,25 +139,95 @@
         pltpu.make_async_copy(cnt, num, near_sem.at[2]),
         pltpu.make_async_copy(ids, cyc, near_sem.at[3]),
     ]
-    table = [pltpu.make_async_copy(tbl.at[q], tab.at[q], tab_sem.at[q]) for q in range(chunks)]
-    for copy in small + table:
+    loads_u = [pltpu.make_async_copy(disp.at[:, r], u.at[:, r], u_sem.at[r]) for r in range(layers)]
+    loads_f = [pltpu.make_async_copy(forc.at[:, r], f.at[:, r], f_sem.at[r]) for r in range(layers)]
+    order = [0, 1, top] + list(range(top - 1, 1, -1))
+    for copy in small:
         copy.start()
-
-    odd = lax.rem(rad, 2) == 1
-    send1[...] = every[jnp.where(odd, 0, layers - 1)]
-    send2[...] = every[jnp.where(odd, layers - 1, 0)]
+    for r in order:
+        loads_u[r].start()
+        loads_f[r].start()
+    for copy in cycles:
+        copy.start()
+    for copy in small:
+        copy.wait()
+
+    for r in range(layers):
+        every[r] = coefficient_rows(*layer_scalars(r, lids, stiffs, coups))
+    send1[...] = every[jnp.where(odd, 0, top)]
+    send2[...] = every[jnp.where(odd, top, 0)]
+
+    def local_sweep(layer, lower, upper):
+        coef = [jnp.broadcast_to(every[layer, j:j + 1, :], (SUB, LANES)) for j in range(12)]
+        none = jnp.zeros((1, LANES), jnp.float32)
+        for g in range(total):
+            here = slice(SUB * g, SUB * g + SUB)
+            values = [spans(per_row, u, c, layer, here) for c in range(3)]
+            for c in range(3):
+                aside = roll_columns(values[c])
+                for j in range(per_row):
+                    at = (c, layer)
+                    above = u[at + (slice(SUB * g - 1, SUB * g), chunk(j))] if g > 0 else none
+                    under = u[at + (slice(SUB * g + SUB, SUB * g + SUB + 1), chunk(j))] if g < total - 1 else none
+                    near = roll_rows(values[c][j], above, under) + aside[j]
+                    if lower is not None:
+                        near = near + u[c, lower, here, chunk(j)]
+                    if upper is not None:
+                        near = near + u[c, upper, here, chunk(j)]
+                    value = relax(c, [values[d][j] for d in range(3)], near, f[c, layer, here, chunk(j)], coef)
+                    s[c, layer, here, chunk(j)] = value
+
+    keeps = [pltpu.make_async_copy(s.at[:, r], kept.at[:, r], kept_sem.at[r]) for r in range(layers)]
+    loads_u[0].wait()
+    loads_f[0].wait()
+    loads_u[1].wait()
+    local_sweep(0, None, 1)
+    keeps[0].start()
+    for r in range(2, layers):
+        loads_u[r].wait()
+    loads_f[top].wait()
+    faces = []
+    for n, (face, layer) in enumerate(((face1, jnp.where(odd, 0, top)), (face2, jnp.where(odd, top, 0)))):
+        faces.append(pltpu.make_async_copy(u.at[:, layer], face.at[0], face_sem.at[2 * n]))
+        faces.append(pltpu.make_async_copy(s.at[:, layer], face.at[1], face_sem.at[2 * n + 1]))
+    faces[0].start()
+    faces[2].start()
+    local_sweep(top, top - 1, None)
+    keeps[top].start()
+    faces[1].start()
+    faces[3].start()
+    for r in range(1, top):
+        loads_f[r].wait()
+
+    def middle(r, carry):
+        local_sweep(r, r - 1, r + 1)
+        pltpu.make_async_copy(s.at[:, r], kept.at[:, r], kept_sem.at[r]).start()
+        return carry
+
+    lax.fori_loop(1, top, middle, 0)
 
     sub8, lane8 = iota((SUB, LANES), 0), iota((SUB, LANES), 1)
     before = sub8 < 2
     zero = jnp.zeros((SUB, LANES), jnp.float32)
     reach = 2 * width // LEAST_COUNT + 2
-    for copy in small:
+    for copy in cycles:
         copy.wait()
     first, last = first_ids[0, 0], last_ids[SUB - 1, LANES - 1]
+    low_part = jnp.right_shift(jnp.maximum(first - reach, 0), 7)
+    high_part = jnp.minimum(jnp.right_shift(last + reach, 7), chunks - 1)
     pay[0:SUB, :] = jnp.zeros((SUB, width), jnp.float32)
+
+    def table(b):
+        return [
+            pltpu.make_async_copy(tbl.at[jnp.minimum(low_part + b * BATCH + i, chunks - 1)], tab.at[i], tab_sem.at[i])
+            for i in range(BATCH)
+        ]
 
     @pl.when(at_end)
     def _():
+        for copy in table(0):
+            copy.start()
+
         own_first = jnp.zeros((SUB, LANES), jnp.int32)
         own_last = own_first
         for j in range(per_row):
@@ -326,19 +327,18 @@
             windows[0, i] = window
             windows[1, i] = start.astype(jnp.float32)
 
-        for copy in table:
-            copy.wait()
         half = jnp.where(bottom, groups, 0)
-        low_part = jnp.right_shift(jnp.maximum(first - reach, 0), 7)
-        high_part = jnp.minimum(jnp.right_shift(last + reach, 7), chunks - 1)
 
         def batch(b, result):
+            @pl.when(b > 0)
+            def _():
+                for copy in table(b):
+                    copy.start()
+
             means = []
-            parts = []
             for i in range(BATCH):
                 q = low_part + b * BATCH + i
                 part = jnp.minimum(q, chunks - 1)
-                parts.append(part)
                 acc = zero
                 for w in range(total + 1):
                     at = q * LANES + lane8 - windows[1, w].astype(jnp.int32)
@@ -347,44 +347,36 @@
                 mean = jnp.sum(acc, axis=0, keepdims=True) / num[pl.ds(part, 1), :].astype(jnp.float32)
                 mean = jnp.where(q < chunks, mean, 0.0)
                 means.append(jnp.broadcast_to(mean, (SUB, LANES)))
+            for copy in table(b):
+                copy.wait()
             for g in range(groups):
-                acc = tab[parts[0], SUB * g:SUB * g + SUB, :] * means[0]
+                acc = tab[0, SUB * g:SUB * g + SUB, :] * means[0]
                 for i in range(1, BATCH):
-                    acc = acc + tab[parts[i], SUB * g:SUB * g + SUB, :] * means[i]
+                    acc = acc + tab[i, SUB * g:SUB * g + SUB, :] * means[i]
                 column = jnp.broadcast_to(jnp.sum(acc, axis=1, keepdims=True), (SUB, LANES))
                 result = jnp.where(lane8 == g + half, result + column, result)
             return result
 
         pay[0:SUB, 0:LANES] = lax.fori_loop(0, (high_part - low_part) // BATCH + 1, batch, zero)
 
-    @pl.when(jnp.logical_not(at_end))
-    def _():
-        for copy in table:
-            copy.wait()
-
     tall = 3 * layers
 
-    def pack(ref, base, near, far):
+    def pack(ref, base, near):
         for c in range(3):
             for r in range(layers):
                 at = base + c * layers + r
                 ref[at:at + 1, :] = u[c, r, near:near + 1, :]
-                ref[at + tall:at + tall + 1, :] = u[c, r, far:far + 1, :]
-                ref[at + 2 * tall:at + 2 * tall + 1, :] = f[c, r, near:near + 1, :]
-
-    @pl.when(lax.rem(lat, 2) == 0)
-    def _():
-        pack(pay, SUB, rows - 1, rows - 2)
-        pack(held, 0, 0, 1)
-
-    @pl.when(lax.rem(lat, 2) == 1)
-    def _():
-        pack(pay, SUB, 0, 1)
-        pack(held, 0, rows - 1, rows - 2)
+                ref[at + tall:at + tall + 1, :] = s[c, r, near:near + 1, :]
+
+    pack(pay, SUB, 0)
+    pack(pay, SUB + 2 * tall, rows - 1)
+
+    for copy in faces + keeps:
+        copy.wait()
 
 
 def sweep_kernel(
-    disp, forc, first, lo, hi, got1, got2, got3, got4, every,
+    disp, forc, first, face1, face2, ring, got3, got4, every,
     out,
     s, f, face, fringe, rim, done, cf, in_sem, out_sem,
 ):
@@ -405,15 +397,16 @@
         copy.start()
     lat, lats = lax.axis_index("lat"), lax.axis_size("lat")
     rad, rads = lax.axis_index("rad"), lax.axis_size("rad")
-    lat_odd, rad_odd = lax.rem(lat, 2) == 1, lax.rem(rad, 2) == 1
+    rad_odd = lax.rem(rad, 2) == 1
+    before, after = jnp.maximum(lat - 1, 0), jnp.minimum(lat + 1, lats - 1)
     low_in, high_in = lat > 0, lat < lats - 1
     sub8 = iota((SUB, LANES), 0)
 
     def side_rows(base, j):
-        at = (slice(SUB + base, SUB + base + layers), chunk(j))
-        one, two = got1[at], got2[at]
-        low = jnp.where(low_in, jnp.where(lat_odd, one, two), 0.0)
-        high = jnp.where(high_in, jnp.where(lat_odd, two, one), 0.0)
+        at = SUB + base
+        low = ring[before, at + 2 * tall:at + 2 * tall + layers, chunk(j)]
+        high = ring[after, at:at + layers, chunk(j)]
+        low, high = jnp.where(low_in, low, 0.0), jnp.where(high_in, high, 0.0)
         return jnp.concatenate([low, high], axis=0)
 
     below = lambda at: jnp.where(rad > 0, jnp.where(rad_odd, got3[at], got4[at]), 0.0)
@@ -429,36 +422,27 @@
         return [jnp.broadcast_to(cf[layer, j:j + 1, :], (SUB, LANES)) for j in range(12)]
 
     near_rows = [[side_rows(c * layers, j) for j in range(per_row)] for c in range(3)]
-    mixed = []
-    for i in range(12):
-        row = jnp.zeros((SUB, LANES), jnp.float32)
-        for r in range(layers):
-            here = jnp.broadcast_to(cf[1 + r, i:i + 1, :], (SUB, LANES))
-            row = jnp.where(jnp.logical_or(sub8 == r, sub8 == layers + r), here, row)
-        mixed.append(row)
     loads[0].wait()
     loads[1].wait()
     keep = jnp.where(sub8 < layers, jnp.where(low_in, 1.0, 0.0), jnp.where(high_in, 1.0, 0.0))
     for c in range(3):
-        aside = roll_columns(near_rows[c])
+        gain = jnp.zeros((SUB, LANES), jnp.float32)
+        for r in range(layers):
+            here = jnp.broadcast_to(cf[1 + r, 3 + c:4 + c, :], (SUB, LANES))
+            gain = jnp.where(jnp.logical_or(sub8 == r, sub8 == layers + r), here, gain)
         for j in range(per_row):
-            value = near_rows[c][j]
-            first_low, first_high = corner_low[j][c:c + 1, :], corner_low[j][3 + c:4 + c, :]
-            last_low, last_high = corner_high[j][c:c + 1, :], corner_high[j][3 + c:4 + c, :]
-            down = pltpu.roll(value, 1, 0)
-            down = jnp.where(sub8 == 0, jnp.broadcast_to(first_low, down.shape), down)
-            down = jnp.where(sub8 == layers, jnp.broadcast_to(first_high, down.shape), down)
-            rise = pltpu.roll(value, SUB - 1, 0)
-            rise = jnp.where(sub8 == layers - 1, jnp.broadcast_to(last_low, rise.shape), rise)
-            rise = jnp.where(sub8 == SUB - 1, jnp.broadcast_to(last_high, rise.shape), rise)
-            within = jnp.zeros((SUB, LANES), jnp.float32)
+            near = jnp.zeros((SUB, LANES), jnp.float32)
             for r in range(layers):
-                head = jnp.broadcast_to(fringe[0, c, r, 0:1, chunk(j)], within.shape)
-                tail = jnp.broadcast_to(fringe[1, c, r, SUB - 1:SUB, chunk(j)], within.shape)
-                within = jnp.where(sub8 == r, head, jnp.where(sub8 == layers + r, tail, within))
-            near = aside[j] + down + rise + within + side_rows(tall + c * layers, j)
-            force = side_rows(2 * tall + c * layers, j)
-            value = relax(c, [near_rows[d][j] for d in range(3)], near, force, mixed) * keep
+                head = jnp.broadcast_to(fringe[0, c, r, 0:1, chunk(j)], near.shape)
+                tail = jnp.broadcast_to(fringe[1, c, r, SUB - 1:SUB, chunk(j)], near.shape)
+                near = jnp.where(sub8 == r, head, jnp.where(sub8 == layers + r, tail, near))
+            ends = (
+                (0, corner_low[j][c:c + 1, :]), (layers, corner_low[j][3 + c:4 + c, :]),
+                (layers - 1, corner_high[j][c:c + 1, :]), (SUB - 1, corner_high[j][3 + c:4 + c, :]),
+            )
+            for row, corner in ends:
+                near = near + jnp.where(sub8 == row, jnp.broadcast_to(corner, near.shape), 0.0)
+            value = (side_rows(tall + c * layers, j) + gain * near) * keep
             for i in range(2 * layers):
                 rim[i, c, :, chunk(j)] = jnp.broadcast_to(value[i:i + 1, :], (SUB, LANES))
 
@@ -469,6 +453,12 @@
             return corner_high[j][3 * side + c:3 * side + c + 1, :]
         at = layers * side + layer - 1
         return near_rows[c][j][at:at + 1, :]
+
+    def lo(index):
+        return jnp.where(rad_odd, face1[index], face2[index])
+
+    def hi(index):
+        return jnp.where(rad_odd, face2[index], face1[index])
 
     for copy in loads[2:5]:
         copy.wait()
@@ -480,15 +470,15 @@
                     at = (slice(SUB * g, SUB * g + SUB), chunk(j))
                     value = None
                     if layer == 0:
-                        value = lo[(1, c) + at] + gain * face[(0, c) + at]
+                        value = lo((1, c) + at) + gain * face[(0, c) + at]
                     elif layer == layers + 1:
-                        value = hi[(1, c) + at] + gain * face[(1, c) + at]
+                        value = hi((1, c) + at) + gain * face[(1, c) + at]
                     elif layer in (1, layers) or g in (0, total - 1):
                         value = s[(c, layer) + at]
                     if layer == 1:
-                        value = value + gain * lo[(0, c) + at]
+                        value = value + gain * lo((0, c) + at)
                     if layer == layers:
-                        value = value + gain * hi[(0, c) + at]
+                        value = value + gain * hi((0, c) + at)
                     if value is None:
                         continue
                     if g == 0:
@@ -512,14 +502,14 @@
                 for j in range(per_row):
                     at = (c, layer)
                     if g > 0:
-                        before = s[at + (slice(SUB * g - 1, SUB * g), chunk(j))]
+                        above_row = s[at + (slice(SUB * g - 1, SUB * g), chunk(j))]
                     else:
-                        before = rim[r, c, :, chunk(j)]
+                        above_row = rim[r, c, :, chunk(j)]
                     if g < total - 1:
-                        after = s[at + (slice(SUB * g + SUB, SUB * g + SUB + 1), chunk(j))]
+                        under_row = s[at + (slice(SUB * g + SUB, SUB * g + SUB + 1), chunk(j))]
                     else:
-                        after = rim[layers + r, c, :, chunk(j)]
-                    near = roll_rows(values[c][j], before, after) + aside[j]
+                        under_row = rim[layers + r, c, :, chunk(j)]
+                    near = roll_rows(values[c][j], above_row, under_row) + aside[j]
                     near = near + (s[c, layer - 1, here, chunk(j)] + s[c, layer + 1, here, chunk(j)])
                     done[c, r, here, chunk(j)] = relax(
                         c, [values[d][j] for d in range(3)], near, f[c, r, here, chunk(j)], coef
@@ -596,12 +586,11 @@
         raise ValueError("unsupported sizes")
     lat, lats = lax.axis_index("lat"), lax.axis_size("lat")
     rad, rads = lax.axis_index("rad"), lax.axis_size("rad")
-    lat_odd, rad_odd = lat % 2 == 1, rad % 2 == 1
+    rad_odd = rad % 2 == 1
     f32 = jnp.float32
     table = jnp.asarray(basis_table(degrees, cycles))
     per_row = width // LANES
     tall = 3 * layers
-    edge_rows = -(-3 * tall // SUB) * SUB
     face = jax.ShapeDtypeStruct((2, 3, rows, width), f32)
 
     whole = jax.ShapeDtypeStruct(displacement.shape, f32)
@@ -612,68 +601,54 @@
             cycle_count.reshape(chunks, LANES), table,
         )
     ]
-    u, f, swept, kept, up, dn, every = pl.pallas_call(
-        first_sweep_kernel,
-        out_shape=(whole, whole, whole, whole, face, face, jax.ShapeDtypeStruct((layers, COEFS, LANES), f32)),
-        in_specs=[HBM] * 5,
-        out_specs=(VMEM,) * 3 + (HBM,) + (VMEM,) * 3,
+    kept, face1, face2, pay, mine1, mine2, every = pl.pallas_call(
+        analysis_kernel,
+        out_shape=(
+            whole, face, face,
+            jax.ShapeDtypeStruct((SUB + 4 * tall, width), f32),
+            jax.ShapeDtypeStruct((COEFS, LANES), f32),
+            jax.ShapeDtypeStruct((COEFS, LANES), f32),
+            jax.ShapeDtypeStruct((layers, COEFS, LANES), f32),
+        ),
+        in_specs=[HBM] * 8,
+        out_specs=(HBM,) + (VMEM,) * 6,
         scratch_shapes=[
+            pltpu.VMEM(displacement.shape, f32),
+            pltpu.VMEM(displacement.shape, f32),
+            pltpu.VMEM(displacement.shape, f32),
+            pltpu.VMEM(cycle_id.shape, jnp.int32),
+            pltpu.VMEM((chunks, LANES), jnp.int32),
+            pltpu.VMEM((BATCH, degrees, LANES), f32),
+            pltpu.VMEM((2, COEFS, LANES), f32),
+            pltpu.VMEM((2, rows // SUB + 1, SUB, LANES), f32),
             pltpu.SMEM(layer_id.shape, jnp.int32),
             pltpu.SMEM(stiffness.shape, f32),
             pltpu.SMEM(coupling.shape[1:] + coupling.shape[:1], f32),
-            pltpu.SemaphoreType.DMA((layers,)),
-            pltpu.SemaphoreType.DMA((layers,)),
+            pltpu.SMEM((SUB, LANES), jnp.int32),
+            pltpu.SMEM((SUB, LANES), jnp.int32),
             pltpu.SemaphoreType.DMA((3,)),
             pltpu.SemaphoreType.DMA((4,)),
             pltpu.SemaphoreType.DMA((layers,)),
-        ],
-        compiler_params=pltpu.CompilerParams(vmem_limit_bytes=VMEM_LIMIT),
-        name="first_sweep",
-    )(*pinned[:5])
-
-    low_far = lax.ppermute(up, "rad", [(i, i + 1) for i in range(rads - 1)])
-    high_far = lax.ppermute(dn, "rad", [(i + 1, i) for i in range(rads - 1)])
-
-    pay, held, mine1, mine2 = pl.pallas_call(
-        analysis_kernel,
-        out_shape=(
-            jax.ShapeDtypeStruct((SUB + edge_rows, width), f32),
-            jax.ShapeDtypeStruct((edge_rows, width), f32),
-            jax.ShapeDtypeStruct((COEFS, LANES), f32),
-            jax.ShapeDtypeStruct((COEFS, LANES), f32),
-        ),
-        in_specs=[VMEM] * 4 + [HBM] * 3,
-        out_specs=(VMEM,) * 4,
-        scratch_shapes=[
-            pltpu.VMEM(cycle_id.shape, jnp.int32),
-            pltpu.VMEM((chunks, LANES), jnp.int32),
-            pltpu.VMEM((chunks, degrees, LANES), f32),
-            pltpu.VMEM((2, COEFS, LANES), f32),
-            pltpu.VMEM((2, rows // SUB + 1, SUB, LANES), f32),
-            pltpu.SMEM((SUB, LANES), jnp.int32),
-            pltpu.SMEM((SUB, LANES), jnp.int32),
+            pltpu.SemaphoreType.DMA((layers,)),
             pltpu.SemaphoreType.DMA((4,)),
-            pltpu.SemaphoreType.DMA((chunks,)),
+            pltpu.SemaphoreType.DMA((layers,)),
+            pltpu.SemaphoreType.DMA((BATCH,)),
         ],
         compiler_params=pltpu.CompilerParams(vmem_limit_bytes=VMEM_LIMIT),
         name="analysis",
-    )(u, f, swept, every, *pinned[5:])
-
-    butterfly = lats == 4 and rads == 8
-    coef = pay[:SUB, :LANES]
-    got1 = lax.ppermute(pay, "lat", even_pairs(lats))
-    if butterfly:
-        coef = coef + got1[:SUB, :LANES]
-    else:
-        coef = lax.psum(coef, ("lat", "rad"))
-    strip = jnp.concatenate([coef, jnp.zeros((SUB, width - LANES), f32)], axis=1)
-    ahead = jnp.concatenate([strip, held], axis=0)
-    ahead, low_far, high_far = lax.optimization_barrier((ahead, low_far, high_far))
-    got2 = lax.ppermute(ahead, "lat", odd_pairs(lats))
-    if butterfly:
-        coef = coef + got2[:SUB, :LANES]
-    low = jnp.where(lat > 0, jnp.where(lat_odd, got1[SUB:SUB + tall], got2[SUB:SUB + tall]), 0.0)
-    high = jnp.where(lat < lats - 1, jnp.where(lat_odd, got2[SUB:SUB + tall], got1[SUB:SUB + tall]), 0.0)
+    )(*pinned)
+
+    beside2 = lax.ppermute(face2, "rad", odd_pairs(rads)[:-2])
+    beside1 = lax.ppermute(face1, "rad", even_pairs(rads))
+
+    ring = lax.all_gather(pay, "lat")
+    coef = jnp.sum(ring[:, :SUB, :LANES], axis=0)
+    butterfly = rads == 8
+    if not butterfly:
+        coef = lax.psum(coef, "rad")
+    low = lax.dynamic_index_in_dim(ring, jnp.maximum(lat - 1, 0), keepdims=False)[SUB + 2 * tall:SUB + 3 * tall]
+    high = lax.dynamic_index_in_dim(ring, jnp.minimum(lat + 1, lats - 1), keepdims=False)[SUB:SUB + tall]
+    low, high = jnp.where(lat > 0, low, 0.0), jnp.where(lat < lats - 1, high, 0.0)
 
     def corners(layer):
         picks = [side[c * layers + layer][None] for side in (low, high) for c in range(3)]
@@ -683,7 +658,9 @@
     corner_low, corner_high = corners(0), corners(layers - 1)
     send1 = jnp.where(rad_odd, corner_low, corner_high)
     send2 = jnp.where(rad_odd, corner_high, corner_low)
-    got3 = lax.ppermute(jnp.concatenate([coef, mine1, send1], axis=0), "rad", even_pairs(rads))
+    first = jnp.concatenate([coef, mine1, send1], axis=0)
+    first, beside1, beside2 = lax.optimization_barrier((first, beside1, beside2))
+    got3 = lax.ppermute(first, "rad", even_pairs(rads))
     if butterfly:
         coef = coef + got3[:SUB]
     got4 = lax.ppermute(jnp.concatenate([coef, mine2, send2], axis=0), "rad", odd_pairs(rads))
@@ -694,7 +671,7 @@
     smoothed = pl.pallas_call(
         sweep_kernel,
         out_shape=whole,
-        in_specs=[HBM] * 3 + [VMEM] * 7,
+        in_specs=[HBM] * 3 + [VMEM] * 6,
         out_specs=HBM,
         scratch_shapes=[
             pltpu.VMEM((3, layers + 2, rows, width), f32),
@@ -709,7 +686,7 @@
         ],
         compiler_params=pltpu.CompilerParams(vmem_limit_bytes=VMEM_LIMIT),
         name="sweeps",
-    )(*pinned[:2], kept, low_far, high_far, got1, got2, got3, got4, every)
+    )(*pinned[:2], kept, beside1, beside2, ring, got3, got4, every)
     coef, smoothed = lax.optimization_barrier((coef, smoothed))
 
     shaped = gravity.reshape(2, 2, SUB, groups)

time: 38.3 us -> 34.5 us (0.901)
  blocking collectives: 0 us -> 9.45 us
  waiting for transfers between devices: 10.9 us -> 2.58 us
  starting transfers between devices: 16.3 us -> 12.4 us
  Pallas kernels: 9.87 us -> 8.77 us
    all_gather x0 -> x1, blocking collectives: none -> 9.45 us  [local(): ring = lax.all_gather(pay, 'lat')]
    ppermute x5 -> x3, waiting for transfers between devices: 8.94 us -> 0.77 us  [the longest x1 0.77 us: local(): got3 = lax.ppermute(first, 'rad', even_pairs(rads))]
    ppermute x5 -> x3, starting transfers between devices: 10 us -> 5.27 us  [the longest x1 2.4 us: local(): beside2 = lax.ppermute(face2, 'rad', odd_pairs(rads)[:-2])]
    pallas_call x2 -> x1, Pallas kernels: 4.63 us -> 3.53 us  [local(): pl.pallas_call(analysis_kernel, out_shape=(whole, face, face, jax.ShapeDt...]
    ppermute x1, starting transfers between devices: 1.35 us -> 2.44 us  [local(): lax.ppermute(jnp.concatenate([coef, mine2, send2], axis=0), 'rad', odd_pa...]
  transfers between devices with their start and end apart: 7 -> 5, of which waited for: 5 -> 2; matrix products, arithmetic and copies ran while one was open for 0% -> 1% of each run, Pallas kernels for 14% -> 10%
where the time goes in v4:
time: 34.5 us; the launch traced here: 34.3 us
  starting transfers between devices  12.4 us (36%)
  blocking collectives  9.45 us (27%)
  Pallas kernels  8.77 us (25%)
  waiting for transfers between devices  2.58 us (7%)
  between operations  0.81 us (2%)
    all_gather x1, blocking collectives, local(): ring = lax.all_gather(pay, 'lat')  9.45 us
    ppermute x1, starting transfers between devices, local(): lax.ppermute(coef, 'rad', [(0, 3), (7, 4), (2, 5), (5, 2), (1, 6), (6, 1)])  4.65 us
    pallas_call x1, Pallas kernels, local(): pl.pallas_call(analysis_kernel, out_shape=(whole, face, face, jax.ShapeDt...  3.53 us
    pallas_call x1, Pallas kernels, local(): pl.pallas_call(sweep_kernel, out_shape=whole, in_specs=[HBM] * 3 + [VMEM]...  3.42 us
    ppermute x1, starting transfers between devices, local(): lax.ppermute(jnp.concatenate([coef, mine2, send2], axis=0), 'rad', odd_pa...  2.44 us
    ppermute x1, starting transfers between devices, local(): beside2 = lax.ppermute(face2, 'rad', odd_pairs(rads)[:-2])  2.4 us
    ppermute x1, starting transfers between devices, local(): beside1 = lax.ppermute(face1, 'rad', even_pairs(rads))  2.27 us
    pallas_call x1, Pallas kernels, local(): pl.pallas_call(functools.partial(synthesis_kernel, 2.0 / cycles), out_sha...  1.83 us
  transfers between devices with their start and end apart: 5, of which 2 were waited for; matrix products, arithmetic and copies ran while one was open for 1% of the time, Pallas kernels for 10%

profile of v4, /device:TPU:1, one launch (start us, length us, event | category | flops | bytes accessed | tf_op | source)
XLA Modules:
  0.0 34.3 jit_solution(2271084352499363257)
XLA Ops:
  0.6 0.0 copy-start.2
  0.6 3.5 %analysis.1 = (f32[3,4,64,384]{3,2,1,0:T(8,128)S(1)}, f32[2,3,64,384]{3,2,1,0:T(8,128)}, f32[2,3,64,384]{3,2,1,0:T(8,128)S(1)}, f32[56,384]{1,0:T(8,128)S(1)}, f...) custom-call(f32[3,4,64,384]{3,2,1,0:T(8,128)} %disp.3, f32[3,4,64,384]{3,2,1,0:T(8,128)} %forc.3, ...), custom_call_target="tpu_custom_call" | custom-call | tf_op jit(solution)/shard_map/analysis/pallas_call | solution.py:604
  4.2 2.3 %collective-permute-start = (f32[2,3,64,384]{3,2,1,0:T(8,128)}, f32[2,3,64,384]{3,2,1,0:T(8,128)S(1)}, u32[]{:S(2)}, u32[]{:S(2)}) collective-permute-start(f32[2,3,64,384]{3,2,1,0:T(8,128)} %get-tuple-element.16), channel_id=1, source_target_pairs={{0,1},{1,0},{2,3},{3,2},{4,5},{5,4},{6,7},{7,6},{8,9},{9,8},{10,11... | collective-permute-start | bytes 1769480 | tf_op jit(solution)/shard_map/ppermute | solution.py:642
  6.4 2.4 %collective-permute-start.1 = (f32[2,3,64,384]{3,2,1,0:T(8,128)S(1)}, f32[2,3,64,384]{3,2,1,0:T(8,128)S(1)}, u32[]{:S(2)}, u32[]{:S(2)}) collective-permute-start(f32[2,3,64,384]{3,2,1,0:T(8,128)S(1)} %get-tuple-element.17), channel_id=1, source_target_pairs={{1,2},{2,1},{3,4},{4,3},{5,6},{6,5},{9,10},{10,9},{11,12},{12,11},... | collective-permute-start | bytes 1769480 | tf_op jit(solution)/shard_map/ppermute | solution.py:641
  8.9 9.4 %all-gather = f32[224,384]{1,0:T(8,128)S(1)} all-gather(f32[56,384]{1,0:T(8,128)S(1)} %get-tuple-element.14), channel_id=2, replica_groups=mesh['lat'=4,'rad'=8] {'lat'}, dimensions={0}, use_global_device_ids=true | all-gather | bytes 430080 | tf_op jit(solution)/shard_map/all_gather | solution.py:644
  18.5 0.0 collective-permute-done.face1
  18.5 0.0 collective-permute-done.1.face2
  18.5 0.6 %collective-permute-start.2 = (f32[48,128]{1,0:T(8,128)S(1)}, f32[48,128]{1,0:T(8,128)S(1)}, u32[]{:S(2)}, u32[]{:S(2)}) collective-permute-start(f32[48,128]{1,0:T(8,128)S(1)} %pad_maximum_fusion), channel_id=1, source_target_pairs={{0,1},{1,0},{2,3},{3,2},{4,5},{5,4},{6,7},{7,6},{8,9},{9,8},{10,11... | collective-permute-start | bytes 73736 | tf_op jit(solution)/shard_map/ppermute | solution.py:663
  19.1 0.0 copy-done.2
  19.1 0.1 reshape.31
  19.2 0.8 %collective-permute-done.2.got3 = f32[48,128]{1,0:T(8,128)S(1)} collective-permute-done((f32[48,128]{1,0:T(8,128)S(1)}, f32[48,128]{1,0:T(8,128)S(1)}, u32[]{:S(2)}, u32[]{:S(2)}) %collective-permute-start.2) | collective-permute-done | bytes 24608 | tf_op jit(solution)/shard_map/ppermute | solution.py:663
  20.0 2.4 %collective-permute-start.3 = (f32[48,128]{1,0:T(8,128)S(1)}, f32[48,128]{1,0:T(8,128)S(1)}, u32[]{:S(2)}, u32[]{:S(2)}) collective-permute-start(f32[48,128]{1,0:T(8,128)S(1)} %pad_maximum_fusion.1), channel_id=1, source_target_pairs={{1,2},{2,1},{3,4},{4,3},{5,6},{6,5},{7,0},{0,7},{9,10},{10,9},{11,... | collective-permute-start | bytes 73736 | tf_op jit(solution)/shard_map/ppermute | solution.py:666
  22.4 1.8 %collective-permute-done.3.got4 = f32[48,128]{1,0:T(8,128)S(1)} collective-permute-done((f32[48,128]{1,0:T(8,128)S(1)}, f32[48,128]{1,0:T(8,128)S(1)}, u32[]{:S(2)}, u32[]{:S(2)}) %collective-permute-start.3) | collective-permute-done | bytes 24608 | tf_op jit(solution)/shard_map/ppermute | solution.py:666
  24.2 4.7 %collective-permute-start.4 = (f32[8,128]{1,0:T(8,128)S(1)}, f32[8,128]{1,0:T(8,128)S(1)}, u32[]{:S(2)}, u32[]{:S(2)}) collective-permute-start(f32[8,128]{1,0:T(8,128)S(1)} %slice_add_fusion), channel_id=1, source_target_pairs={{0,3},{7,4},{2,5},{5,2},{1,6},{6,1},{8,11},{15,12},{10,13},{13,10}... | collective-permute-start | bytes 12296 | tf_op jit(solution)/shard_map/ppermute | solution.py:669
  28.9 0.1 pad_maximum_fusion.4
  29.0 0.0 copy-start
  29.0 0.0 copy-start.1
  29.0 3.4 %sweeps.1 = f32[3,4,64,384]{3,2,1,0:T(8,128)} custom-call(f32[3,4,64,384]{3,2,1,0:T(8,128)} %disp.3, f32[3,4,64,384]{3,2,1,0:T(8,128)} %forc.3, f32[3,4,64,384]{3,2,1,0:T(8,128)S(1)} %get-tuple-element.20.first, f32[2,3,64,384]{3,2,1,0:T(8,128)S(1)} %collective-permute-done.face1, f32[2,3,64,384]{3,2,1,0:T(8,128)S(1)} %collective-permute-done.1.face2, ...), custom_call_target="tpu_custom_call" | custom-call | tf_op jit(solution)/shard_map/sweeps/pallas_call | solution.py:671
  32.4 0.0 collective-permute-done.4
  32.4 0.0 copy-done
  32.4 0.0 copy-done.1
  32.4 1.8 %synthesis.1 = f32[2,64,384]{2,1,0:T(8,128)} custom-call(f32[8,128]{1,0:T(8,128)S(1)} %add.27.coef, f32[8,128]{1,0:T(8,128)S(1)} %get-tuple-element.58.gain_a, f32[8,128]{1,0:T(8,128)S(1)} %get-tuple-element.59.gain_b, s32[64,384]{1,0:T(8,128)S(1)} %copy-done.1, f32[12,512,128]{2,1,0:T(8,128)S(1)} %copy-done), custom_call_target="tpu_custom_call" | custom-call | tf_op jit(solution)/shard_map/synthesis/pallas_call | solution.py:695
  (15 shorter events, 0.1 us)
Async XLA Ops:
  0.6 18.5 %copy-start.2 = (f32[2,2,512]{2,1,0:T(2,128)S(1)}, f32[2,2,512]{2,1,0:T(2,128)}, u32[]{:S(2)}) copy-start(f32[2,2,512]{2,1,0:T(2,128)} %param.16) | copy-start | bytes 24580
  4.2 14.3 %collective-permute-start = (f32[2,3,64,384]{3,2,1,0:T(8,128)}, f32[2,3,64,384]{3,2,1,0:T(8,128)S(1)}, u32[]{:S(2)}, u32[]{:S(2)}) collective-permute-start(f32[2,3,64,384]{3,2,1,0:T(8,128)} %get-tuple-element.16), channel_id=1, source_target_pairs={{0,1},{1,0},{2,3},{3,2},{4,5},{5,4},{6,7},{7,6},{8,9},{9,8},{10,11... | collective-permute-start | bytes 1769480 | tf_op jit(solution)/shard_map/ppermute | solution.py:642
  6.4 12.1 %collective-permute-start.1 = (f32[2,3,64,384]{3,2,1,0:T(8,128)S(1)}, f32[2,3,64,384]{3,2,1,0:T(8,128)S(1)}, u32[]{:S(2)}, u32[]{:S(2)}) collective-permute-start(f32[2,3,64,384]{3,2,1,0:T(8,128)S(1)} %get-tuple-element.17), channel_id=1, source_target_pairs={{1,2},{2,1},{3,4},{4,3},{5,6},{6,5},{9,10},{10,9},{11,12},{12,11},... | collective-permute-start | bytes 1769480 | tf_op jit(solution)/shard_map/ppermute | solution.py:641
  18.5 1.4 %collective-permute-start.2 = (f32[48,128]{1,0:T(8,128)S(1)}, f32[48,128]{1,0:T(8,128)S(1)}, u32[]{:S(2)}, u32[]{:S(2)}) collective-permute-start(f32[48,128]{1,0:T(8,128)S(1)} %pad_maximum_fusion), channel_id=1, source_target_pairs={{0,1},{1,0},{2,3},{3,2},{4,5},{5,4},{6,7},{7,6},{8,9},{9,8},{10,11... | collective-permute-start | bytes 73736 | tf_op jit(solution)/shard_map/ppermute | solution.py:663
  20.0 4.2 %collective-permute-start.3 = (f32[48,128]{1,0:T(8,128)S(1)}, f32[48,128]{1,0:T(8,128)S(1)}, u32[]{:S(2)}, u32[]{:S(2)}) collective-permute-start(f32[48,128]{1,0:T(8,128)S(1)} %pad_maximum_fusion.1), channel_id=1, source_target_pairs={{1,2},{2,1},{3,4},{4,3},{5,6},{6,5},{7,0},{0,7},{9,10},{10,9},{11,... | collective-permute-start | bytes 73736 | tf_op jit(solution)/shard_map/ppermute | solution.py:666
  24.2 8.2 %collective-permute-start.4 = (f32[8,128]{1,0:T(8,128)S(1)}, f32[8,128]{1,0:T(8,128)S(1)}, u32[]{:S(2)}, u32[]{:S(2)}) collective-permute-start(f32[8,128]{1,0:T(8,128)S(1)} %slice_add_fusion), channel_id=1, source_target_pairs={{0,3},{7,4},{2,5},{5,2},{1,6},{6,1},{8,11},{15,12},{10,13},{13,10}... | collective-permute-start | bytes 12296 | tf_op jit(solution)/shard_map/ppermute | solution.py:669
  29.0 3.5 %copy-start = (f32[12,512,128]{2,1,0:T(8,128)S(1)}, f32[12,512,128]{2,1,0:T(8,128)}, u32[]{:S(2)}) copy-start(f32[12,512,128]{2,1,0:T(8,128)} %constant.40.clone.tbl.tab) | copy-start | bytes 9437188
  29.0 3.5 %copy-start.1 = (s32[64,384]{1,0:T(8,128)S(1)}, s32[64,384]{1,0:T(8,128)}, u32[]{:S(2)}) copy-start(s32[64,384]{1,0:T(8,128)} %ids.3) | copy-start | bytes 294916

commit v5 on v4

--- a/solution.py
+++ b/solution.py
@@ -107,10 +107,10 @@
 
 
 def analysis_kernel(
-    disp, forc, lid, stiff, coup, ids, cnt, tbl,
-    kept, face1, face2, pay, send1, send2, every,
-    u, f, s, cyc, num, tab, mat, windows, lids, stiffs, coups, first_ids, last_ids,
-    small_sem, near_sem, u_sem, f_sem, face_sem, kept_sem, tab_sem,
+    disp, forc, lid, stiff, coup, ids, cnt, grav, tbl,
+    u, f, s, face1, face2, pay, send, every, gains,
+    cyc, num, tab, mat, windows, gain_in, lids, stiffs, coups, first_ids, last_ids,
+    small_sem, near_sem, u_sem, f_sem, face_sem, tab_sem,
 ):
     layers, rows, width = disp.shape[1:]
     chunks = cnt.shape[0]
@@ -138,6 +138,7 @@
         ),
         pltpu.make_async_copy(cnt, num, near_sem.at[2]),
         pltpu.make_async_copy(ids, cyc, near_sem.at[3]),
+        pltpu.make_async_copy(grav, gain_in, near_sem.at[4]),
     ]
     loads_u = [pltpu.make_async_copy(disp.at[:, r], u.at[:, r], u_sem.at[r]) for r in range(layers)]
     loads_f = [pltpu.make_async_copy(forc.at[:, r], f.at[:, r], f_sem.at[r]) for r in range(layers)]
@@ -154,8 +155,8 @@
 
     for r in range(layers):
         every[r] = coefficient_rows(*layer_scalars(r, lids, stiffs, coups))
-    send1[...] = every[jnp.where(odd, 0, top)]
-    send2[...] = every[jnp.where(odd, top, 0)]
+    send[...] = every[jnp.where(odd, top, 0)]
+    at_core = every[jnp.where(odd, 0, top)]
 
     def local_sweep(layer, lower, upper):
         coef = [jnp.broadcast_to(every[layer, j:j + 1, :], (SUB, LANES)) for j in range(12)]
@@ -177,12 +178,10 @@
                     value = relax(c, [values[d][j] for d in range(3)], near, f[c, layer, here, chunk(j)], coef)
                     s[c, layer, here, chunk(j)] = value
 
-    keeps = [pltpu.make_async_copy(s.at[:, r], kept.at[:, r], kept_sem.at[r]) for r in range(layers)]
     loads_u[0].wait()
     loads_f[0].wait()
     loads_u[1].wait()
     local_sweep(0, None, 1)
-    keeps[0].start()
     for r in range(2, layers):
         loads_u[r].wait()
     loads_f[top].wait()
@@ -193,7 +192,6 @@
     faces[0].start()
     faces[2].start()
     local_sweep(top, top - 1, None)
-    keeps[top].start()
     faces[1].start()
     faces[3].start()
     for r in range(1, top):
@@ -201,7 +199,6 @@
 
     def middle(r, carry):
         local_sweep(r, r - 1, r + 1)
-        pltpu.make_async_copy(s.at[:, r], kept.at[:, r], kept_sem.at[r]).start()
         return carry
 
     lax.fori_loop(1, top, middle, 0)
@@ -215,7 +212,16 @@
     first, last = first_ids[0, 0], last_ids[SUB - 1, LANES - 1]
     low_part = jnp.right_shift(jnp.maximum(first - reach, 0), 7)
     high_part = jnp.minimum(jnp.right_shift(last + reach, 7), chunks - 1)
-    pay[0:SUB, :] = jnp.zeros((SUB, width), jnp.float32)
+    pay[0:SUB, 0:LANES] = jnp.zeros((SUB, LANES), jnp.float32)
+    pay[0:SUB, LANES:2 * LANES] = at_core[0:SUB]
+    pay[0:SUB, 2 * LANES:3 * LANES] = at_core[SUB:]
+
+    lane1 = iota((1, LANES), 1)
+    for load in range(2):
+        for m in range(groups * SUB // LANES):
+            one, two = gain_in[0, load:load + 1, chunk(m)], gain_in[1, load:load + 1, chunk(m)]
+            gains[load, 2 * m:2 * m + 1, :] = jnp.where(lane1 < groups, one, pltpu.roll(two, groups, 1))
+            gains[load, 2 * m + 1:2 * m + 2, :] = jnp.where(lane1 < groups, pltpu.roll(one, groups, 1), two)
 
     def table(b):
         return [
@@ -371,59 +377,89 @@
     pack(pay, SUB, 0)
     pack(pay, SUB + 2 * tall, rows - 1)
 
-    for copy in faces + keeps:
+    for copy in faces:
         copy.wait()
 
 
+def relay_kernel(ring, send, out):
+    cores = 2
+    lat, lats = lax.axis_index("lat"), lax.axis_size("lat")
+    core = lax.rem(lax.axis_index("rad"), cores)
+    members, _, width = ring.shape
+    tall = (ring.shape[1] - SUB) // 4
+    layers = tall // 3
+    coef = ring[0, 0:SUB, 0:LANES]
+    for i in range(1, members):
+        coef = coef + ring[i, 0:SUB, 0:LANES]
+    out[0:SUB, :] = coef
+    out[SUB:SUB + COEFS, :] = send[...]
+    before, after = cores * jnp.maximum(lat - 1, 0) + core, cores * jnp.minimum(lat + 1, lats - 1) + core
+    low_in, high_in = lat > 0, lat < lats - 1
+    for j in range(width // LANES):
+        base = SUB + COEFS + SUB * j
+        out[base:base + SUB, :] = jnp.zeros((SUB, LANES), jnp.float32)
+        for c in range(3):
+            for at, member, valid, start in ((c, before, low_in, 2 * tall), (3 + c, after, high_in, 0)):
+                row = SUB + start + c * layers
+                bottom, top = ring[member, row:row + 1, chunk(j)], ring[member, row + layers - 1:row + layers, chunk(j)]
+                out[base + at:base + at + 1, :] = jnp.where(valid, jnp.where(core == 1, top, bottom), 0.0)
+
+
 def sweep_kernel(
-    disp, forc, first, face1, face2, ring, got3, got4, every,
+    u, f, first, face1, face2, ring, got, every,
     out,
-    s, f, face, fringe, rim, done, cf, in_sem, out_sem,
+    s, rim, done, cf, out_sem,
 ):
-    layers, rows, width = disp.shape[1:]
+    layers, rows, width = u.shape[1:]
     per_row = width // LANES
     total = rows // SUB
     tall = 3 * layers
     top = layers - 1
-    loads = [
-        pltpu.make_async_copy(disp.at[:, :, pl.ds(0, SUB)], fringe.at[0], in_sem.at[0]),
-        pltpu.make_async_copy(disp.at[:, :, pl.ds(rows - SUB, SUB)], fringe.at[1], in_sem.at[1]),
-        pltpu.make_async_copy(disp.at[:, 0], face.at[0], in_sem.at[2]),
-        pltpu.make_async_copy(disp.at[:, top], face.at[1], in_sem.at[3]),
-        pltpu.make_async_copy(first, s.at[:, pl.ds(1, layers)], in_sem.at[4]),
-        pltpu.make_async_copy(forc, f, in_sem.at[5]),
-    ]
-    for copy in loads:
-        copy.start()
     lat, lats = lax.axis_index("lat"), lax.axis_size("lat")
     rad, rads = lax.axis_index("rad"), lax.axis_size("rad")
     rad_odd = lax.rem(rad, 2) == 1
-    before, after = jnp.maximum(lat - 1, 0), jnp.minimum(lat + 1, lats - 1)
+    cores = 2
+    core = lax.rem(rad, cores)
+    lower, upper = cores * jnp.maximum(lat - 1, 0), cores * jnp.minimum(lat + 1, lats - 1)
     low_in, high_in = lat > 0, lat < lats - 1
     sub8 = iota((SUB, LANES), 0)
 
     def side_rows(base, j):
         at = SUB + base
-        low = ring[before, at + 2 * tall:at + 2 * tall + layers, chunk(j)]
-        high = ring[after, at:at + layers, chunk(j)]
+        low = ring[lower + core, at + 2 * tall:at + 2 * tall + layers, chunk(j)]
+        high = ring[upper + core, at:at + layers, chunk(j)]
         low, high = jnp.where(low_in, low, 0.0), jnp.where(high_in, high, 0.0)
         return jnp.concatenate([low, high], axis=0)
 
-    below = lambda at: jnp.where(rad > 0, jnp.where(rad_odd, got3[at], got4[at]), 0.0)
-    above = lambda at: jnp.where(rad < rads - 1, jnp.where(rad_odd, got4[at], got3[at]), 0.0)
-    cf[0] = below(slice(SUB, SUB + COEFS))
-    cf[layers + 1] = above(slice(SUB, SUB + COEFS))
+    mate = 1 - core
+    own_chip = jnp.concatenate(
+        [ring[cores * lat + mate, 0:SUB, LANES:2 * LANES], ring[cores * lat + mate, 0:SUB, 2 * LANES:3 * LANES]], axis=0
+    )
+    other_chip = got[SUB:SUB + COEFS, :]
+    lowest, highest = rad == 0, rad == rads - 1
+    cf[0] = jnp.where(rad_odd, own_chip, jnp.where(lowest, 0.0, other_chip))
+    cf[layers + 1] = jnp.where(rad_odd, jnp.where(highest, 0.0, other_chip), own_chip)
     for r in range(layers):
         cf[1 + r] = every[r]
-    corner_low = [below(slice(SUB + COEFS + SUB * j, SUB + COEFS + SUB * j + SUB)) for j in range(per_row)]
-    corner_high = [above(slice(SUB + COEFS + SUB * j, SUB + COEFS + SUB * j + SUB)) for j in range(per_row)]
+    corner_low, corner_high = [], []
+    for j in range(per_row):
+        base = SUB + COEFS + SUB * j
+        other = got[base:base + SUB, :]
+        rows_own = []
+        for member, valid, start in ((lower + mate, low_in, 2 * tall), (upper + mate, high_in, 0)):
+            for c in range(3):
+                row = SUB + start + c * layers
+                near_end, far_end = ring[member, row:row + 1, chunk(j)], ring[member, row + top:row + top + 1, chunk(j)]
+                rows_own.append(jnp.where(valid, jnp.where(rad_odd, far_end, near_end), 0.0))
+        rows_own.append(jnp.zeros((SUB - 6, LANES), jnp.float32))
+        own = jnp.concatenate(rows_own, axis=0)
+        corner_low.append(jnp.where(rad_odd, own, jnp.where(lowest, 0.0, other)))
+        corner_high.append(jnp.where(rad_odd, jnp.where(highest, 0.0, other), own))
 
     def coefficients(layer):
         return [jnp.broadcast_to(cf[layer, j:j + 1, :], (SUB, LANES)) for j in range(12)]
 
     near_rows = [[side_rows(c * layers, j) for j in range(per_row)] for c in range(3)]
-    loads[0].wait()
-    loads[1].wait()
     keep = jnp.where(sub8 < layers, jnp.where(low_in, 1.0, 0.0), jnp.where(high_in, 1.0, 0.0))
     for c in range(3):
         gain = jnp.zeros((SUB, LANES), jnp.float32)
@@ -433,8 +469,8 @@
         for j in range(per_row):
             near = jnp.zeros((SUB, LANES), jnp.float32)
             for r in range(layers):
-                head = jnp.broadcast_to(fringe[0, c, r, 0:1, chunk(j)], near.shape)
-                tail = jnp.broadcast_to(fringe[1, c, r, SUB - 1:SUB, chunk(j)], near.shape)
+                head = jnp.broadcast_to(u[c, r, 0:1, chunk(j)], near.shape)
+                tail = jnp.broadcast_to(u[c, r, rows - 1:rows, chunk(j)], near.shape)
                 near = jnp.where(sub8 == r, head, jnp.where(sub8 == layers + r, tail, near))
             ends = (
                 (0, corner_low[j][c:c + 1, :]), (layers, corner_low[j][3 + c:4 + c, :]),
@@ -460,27 +496,22 @@
     def hi(index):
         return jnp.where(rad_odd, face2[index], face1[index])
 
-    for copy in loads[2:5]:
-        copy.wait()
     for layer in range(layers + 2):
         for c in range(3):
             gain = jnp.broadcast_to(cf[layer, 3 + c:4 + c, :], (SUB, LANES))
             for j in range(per_row):
                 for g in range(total):
                     at = (slice(SUB * g, SUB * g + SUB), chunk(j))
-                    value = None
                     if layer == 0:
-                        value = lo((1, c) + at) + gain * face[(0, c) + at]
+                        value = lo((1, c) + at) + gain * u[(c, 0) + at]
                     elif layer == layers + 1:
-                        value = hi((1, c) + at) + gain * face[(1, c) + at]
-                    elif layer in (1, layers) or g in (0, total - 1):
-                        value = s[(c, layer) + at]
+                        value = hi((1, c) + at) + gain * u[(c, top) + at]
+                    else:
+                        value = first[(c, layer - 1) + at]
                     if layer == 1:
                         value = value + gain * lo((0, c) + at)
                     if layer == layers:
                         value = value + gain * hi((0, c) + at)
-                    if value is None:
-                        continue
                     if g == 0:
                         row = jnp.broadcast_to(beyond(layer, 0, c, j), value.shape)
                         value = value + jnp.where(sub8 == 0, gain * row, 0.0)
@@ -489,7 +520,6 @@
                         value = value + jnp.where(sub8 == SUB - 1, gain * row, 0.0)
                     s[(c, layer) + at] = value
 
-    loads[5].wait()
     stores = [pltpu.make_async_copy(done.at[:, r], out.at[:, r], out_sem.at[r]) for r in range(layers)]
     for r in range(layers):
         layer = r + 1
@@ -519,18 +549,18 @@
         copy.wait()
 
 
-def synthesis_kernel(scale, coef, gain_a, gain_b, ids, tab, out, factors):
+def synthesis_kernel(scale, coef, rest, gains, ids, tab, out, factors):
     rows, width = ids.shape
     chunks = tab.shape[0]
     groups = tab.shape[1] // SUB
     per_row = width // LANES
     lane8 = iota((SUB, LANES), 1)
-    here = coef[...]
+    here = coef[...] + rest[...]
     other = pltpu.roll(here, groups, 1)
     left = lane8 < groups
     surface = jnp.where(left, here, other)
     core = jnp.where(left, other, here)
-    modes = (gain_a[...] * surface + gain_b[...] * core) * scale
+    modes = (gains[0] * surface + gains[1] * core) * scale
     zero = jnp.zeros((SUB, LANES), jnp.float32)
     for i in range(2 * groups):
         factors[i] = jnp.broadcast_to(modes[:, i:i + 1], (SUB, LANES))
@@ -582,11 +612,9 @@
     _, layers, rows, width = displacement.shape
     cycles, degrees = cycle_count.shape[0], gravity.shape[2]
     chunks, groups = cycles // LANES, degrees // SUB
-    if 2 * groups != LANES or 2 * layers != SUB:
+    lats, rads, cores = lax.axis_size("lat"), lax.axis_size("rad"), 2
+    if 2 * groups != LANES or 2 * layers != SUB or rads % cores or width < 3 * LANES:
         raise ValueError("unsupported sizes")
-    lat, lats = lax.axis_index("lat"), lax.axis_size("lat")
-    rad, rads = lax.axis_index("rad"), lax.axis_size("rad")
-    rad_odd = rad % 2 == 1
     f32 = jnp.float32
     table = jnp.asarray(basis_table(degrees, cycles))
     per_row = width // LANES
@@ -598,40 +626,37 @@
         pltpu.with_memory_space_constraint(value, pltpu.HBM)
         for value in (
             displacement, forcing, layer_id, stiffness, jnp.transpose(coupling, (1, 2, 0)), cycle_id,
-            cycle_count.reshape(chunks, LANES), table,
+            cycle_count.reshape(chunks, LANES), gravity, table,
         )
     ]
-    kept, face1, face2, pay, mine1, mine2, every = pl.pallas_call(
+    u, f, swept, face1, face2, pay, mine, every, gains = pl.pallas_call(
         analysis_kernel,
         out_shape=(
-            whole, face, face,
+            whole, whole, whole, face, face,
             jax.ShapeDtypeStruct((SUB + 4 * tall, width), f32),
             jax.ShapeDtypeStruct((COEFS, LANES), f32),
-            jax.ShapeDtypeStruct((COEFS, LANES), f32),
             jax.ShapeDtypeStruct((layers, COEFS, LANES), f32),
+            jax.ShapeDtypeStruct((2, SUB, LANES), f32),
         ),
-        in_specs=[HBM] * 8,
-        out_specs=(HBM,) + (VMEM,) * 6,
+        in_specs=[HBM] * 9,
+        out_specs=(VMEM,) * 9,
         scratch_shapes=[
-            pltpu.VMEM(displacement.shape, f32),
-            pltpu.VMEM(displacement.shape, f32),
-            pltpu.VMEM(displacement.shape, f32),
             pltpu.VMEM(cycle_id.shape, jnp.int32),
             pltpu.VMEM((chunks, LANES), jnp.int32),
             pltpu.VMEM((BATCH, degrees, LANES), f32),
             pltpu.VMEM((2, COEFS, LANES), f32),
             pltpu.VMEM((2, rows // SUB + 1, SUB, LANES), f32),
+            pltpu.VMEM(gravity.shape, f32),
             pltpu.SMEM(layer_id.shape, jnp.int32),
             pltpu.SMEM(stiffness.shape, f32),
             pltpu.SMEM(coupling.shape[1:] + coupling.shape[:1], f32),
             pltpu.SMEM((SUB, LANES), jnp.int32),
             pltpu.SMEM((SUB, LANES), jnp.int32),
             pltpu.SemaphoreType.DMA((3,)),
-            pltpu.SemaphoreType.DMA((4,)),
+            pltpu.SemaphoreType.DMA((5,)),
             pltpu.SemaphoreType.DMA((layers,)),
             pltpu.SemaphoreType.DMA((layers,)),
             pltpu.SemaphoreType.DMA((4,)),
-            pltpu.SemaphoreType.DMA((layers,)),
             pltpu.SemaphoreType.DMA((BATCH,)),
         ],
         compiler_params=pltpu.CompilerParams(vmem_limit_bytes=VMEM_LIMIT),
@@ -641,57 +666,43 @@
     beside2 = lax.ppermute(face2, "rad", odd_pairs(rads)[:-2])
     beside1 = lax.ppermute(face1, "rad", even_pairs(rads))
 
-    ring = lax.all_gather(pay, "lat")
-    coef = jnp.sum(ring[:, :SUB, :LANES], axis=0)
-    butterfly = rads == 8
-    if not butterfly:
-        coef = lax.psum(coef, "rad")
-    low = lax.dynamic_index_in_dim(ring, jnp.maximum(lat - 1, 0), keepdims=False)[SUB + 2 * tall:SUB + 3 * tall]
-    high = lax.dynamic_index_in_dim(ring, jnp.minimum(lat + 1, lats - 1), keepdims=False)[SUB:SUB + tall]
-    low, high = jnp.where(lat > 0, low, 0.0), jnp.where(lat < lats - 1, high, 0.0)
-
-    def corners(layer):
-        picks = [side[c * layers + layer][None] for side in (low, high) for c in range(3)]
-        block = jnp.concatenate(picks + [jnp.zeros((SUB - 6, width), f32)], axis=0)
-        return jnp.concatenate(jnp.split(block, per_row, axis=1), axis=0)
-
-    corner_low, corner_high = corners(0), corners(layers - 1)
-    send1 = jnp.where(rad_odd, corner_low, corner_high)
-    send2 = jnp.where(rad_odd, corner_high, corner_low)
-    first = jnp.concatenate([coef, mine1, send1], axis=0)
-    first, beside1, beside2 = lax.optimization_barrier((first, beside1, beside2))
-    got3 = lax.ppermute(first, "rad", even_pairs(rads))
-    if butterfly:
-        coef = coef + got3[:SUB]
-    got4 = lax.ppermute(jnp.concatenate([coef, mine2, send2], axis=0), "rad", odd_pairs(rads))
-    if butterfly:
-        coef = coef + got4[:SUB]
-        coef = coef + lax.ppermute(coef, "rad", [(0, 3), (7, 4), (2, 5), (5, 2), (1, 6), (6, 1)])
+    chips = [[a * rads + b + c for a in range(lats) for c in range(cores)] for b in range(0, rads, cores)]
+    ring = lax.all_gather(pay, ("lat", "rad"), axis_index_groups=chips)
+    outward = pl.pallas_call(
+        relay_kernel,
+        out_shape=jax.ShapeDtypeStruct((SUB + COEFS + SUB * per_row, LANES), f32),
+        in_specs=[VMEM] * 2,
+        out_specs=VMEM,
+        compiler_params=pltpu.CompilerParams(vmem_limit_bytes=VMEM_LIMIT),
+        name="relay",
+    )(ring, mine)
+    outward, beside1, beside2 = lax.optimization_barrier((outward, beside1, beside2))
+    got = lax.ppermute(outward, "rad", odd_pairs(rads))
+    coef = outward[:SUB]
+    if rads == 8:
+        coef = coef + got[:SUB]
+        rest = lax.ppermute(coef, "rad", [(0, 3), (7, 4), (2, 5), (5, 2), (1, 6), (6, 1)])
+    else:
+        coef = lax.psum(coef, "rad") * (1.0 / cores)
+        rest = jnp.zeros_like(coef)
 
     smoothed = pl.pallas_call(
         sweep_kernel,
         out_shape=whole,
-        in_specs=[HBM] * 3 + [VMEM] * 6,
+        in_specs=[VMEM] * 8,
         out_specs=HBM,
         scratch_shapes=[
             pltpu.VMEM((3, layers + 2, rows, width), f32),
-            pltpu.VMEM((3, layers, rows, width), f32),
-            pltpu.VMEM((2, 3, rows, width), f32),
-            pltpu.VMEM((2, 3, layers, SUB, width), f32),
             pltpu.VMEM((2 * layers, 3, SUB, width), f32),
             pltpu.VMEM((3, layers, rows, width), f32),
             pltpu.VMEM((layers + 2, COEFS, LANES), f32),
-            pltpu.SemaphoreType.DMA((6,)),
             pltpu.SemaphoreType.DMA((layers,)),
         ],
         compiler_params=pltpu.CompilerParams(vmem_limit_bytes=VMEM_LIMIT),
         name="sweeps",
-    )(*pinned[:2], kept, beside1, beside2, ring, got3, got4, every)
+    )(u, f, swept, beside1, beside2, ring, got, every)
     coef, smoothed = lax.optimization_barrier((coef, smoothed))
 
-    shaped = gravity.reshape(2, 2, SUB, groups)
-    gain_a = jnp.concatenate([shaped[0, 0], shaped[1, 0]], axis=1)
-    gain_b = jnp.concatenate([shaped[0, 1], shaped[1, 1]], axis=1)
     potential = pl.pallas_call(
         functools.partial(synthesis_kernel, 2.0 / cycles),
         out_shape=jax.ShapeDtypeStruct((2, rows, width), f32),
@@ -700,7 +711,7 @@
         scratch_shapes=[pltpu.VMEM((2 * groups, SUB, LANES), f32)],
         compiler_params=pltpu.CompilerParams(vmem_limit_bytes=VMEM_LIMIT),
         name="synthesis",
-    )(coef, gain_a, gain_b, cycle_id, table)
+    )(coef, rest, gains, cycle_id, table)
     return smoothed, potential
 
 

time: 34.5 us -> 32.2 us (0.933)
  Pallas kernels: 8.77 us -> 6.56 us
  blocking collectives: 9.45 us -> 11.3 us
  waiting for transfers between devices: 2.58 us -> 1.52 us
  starting transfers between devices: 12.4 us -> 11.5 us
    pallas_call x2 -> x3, Pallas kernels: 6.94 us -> 4.72 us  [the longest x1 2.81 us: local(): pl.pallas_call(analysis_kernel, out_shape=(whole, whole, whole, face, fac...]
    all_gather x1, blocking collectives: 9.45 us -> 11.3 us  [local(): ring = lax.all_gather(pay, ('lat', 'rad'), axis_index_groups=chips)]
    ppermute x2 -> x1, starting transfers between devices: 3.04 us -> 1.86 us  [local(): got = lax.ppermute(outward, 'rad', odd_pairs(rads))]
    ppermute x2 -> x1, waiting for transfers between devices: 2.57 us -> 1.51 us  [local(): got = lax.ppermute(outward, 'rad', odd_pairs(rads))]
    unnamed x6 -> x4, local copies, waits for them, and re-layouts: 0.01 us -> 0.41 us
  transfers between devices with their start and end apart: 5 -> 4, of which waited for: 2 -> 1; matrix products, arithmetic and copies ran while one was open for 1% -> 0% of each run, Pallas kernels for 10% -> 6%
where the time goes in v5:
time: 32.2 us; the launch traced here: 32 us
  starting transfers between devices  11.5 us (36%)
  blocking collectives  11.3 us (35%)
  Pallas kernels  6.56 us (20%)
  waiting for transfers between devices  1.52 us (5%)
  between operations  0.71 us (2%)
  local copies, waits for them, and re-layouts  0.41 us (1%)
    all_gather x1, blocking collectives, local(): ring = lax.all_gather(pay, ('lat', 'rad'), axis_index_groups=chips)  11.3 us
    ppermute x1, starting transfers between devices, local(): lax.ppermute(coef, 'rad', [(0, 3), (7, 4), (2, 5), (5, 2), (1, 6), (6, 1)])  4.94 us
    pallas_call x1, Pallas kernels, local(): pl.pallas_call(analysis_kernel, out_shape=(whole, whole, whole, face, fac...  2.81 us
    ppermute x1, starting transfers between devices, local(): beside1 = lax.ppermute(face1, 'rad', even_pairs(rads))  2.4 us
    ppermute x1, starting transfers between devices, local(): beside2 = lax.ppermute(face2, 'rad', odd_pairs(rads)[:-2])  2.28 us
    pallas_call x1, Pallas kernels, local(): pl.pallas_call(sweep_kernel, out_shape=whole, in_specs=[VMEM] * 8, out_sp...  1.88 us
    ppermute x1, starting transfers between devices, local(): got = lax.ppermute(outward, 'rad', odd_pairs(rads))  1.86 us
    pallas_call x1, Pallas kernels, local(): pl.pallas_call(functools.partial(synthesis_kernel, 2.0 / cycles), out_sha...  1.84 us
  transfers between devices with their start and end apart: 4, of which 1 were waited for; matrix products, arithmetic and copies ran while one was open for 0% of the time, Pallas kernels for 6%

profile of v5, /device:TPU:1, one launch (start us, length us, event | category | flops | bytes accessed | tf_op | source)
XLA Modules:
  0.0 32.0 jit_solution(12245126662007700131)
XLA Ops:
  0.6 2.8 %analysis.1 = (f32[3,4,64,384]{3,2,1,0:T(8,128)S(1)}, f32[3,4,64,384]{3,2,1,0:T(8,128)S(1)}, f32[3,4,64,384]{3,2,1,0:T(8,128)S(1)}, f32[2,3,64,384]{3,2,1,0:T(8,...) custom-call(f32[3,4,64,384]{3,2,1,0:T(8,128)} %disp.1, ...), custom_call_target="tpu_custom_call" | custom-call | tf_op jit(solution)/shard_map/analysis/pallas_call | solution.py:632
  3.5 2.4 %collective-permute-start = (f32[2,3,64,384]{3,2,1,0:T(8,128)S(1)}, f32[2,3,64,384]{3,2,1,0:T(8,128)S(1)}, u32[]{:S(2)}, u32[]{:S(2)}) collective-permute-start(f32[2,3,64,384]{3,2,1,0:T(8,128)S(1)} %get-tuple-element.18), channel_id=1, source_target_pairs={{0,1},{1,0},{2,3},{3,2},{4,5},{5,4},{6,7},{7,6},{8,9},{9,8},{10,11... | collective-permute-start | bytes 1769480 | tf_op jit(solution)/shard_map/ppermute | solution.py:667
  5.9 2.3 %collective-permute-start.1 = (f32[2,3,64,384]{3,2,1,0:T(8,128)S(1)}, f32[2,3,64,384]{3,2,1,0:T(8,128)S(1)}, u32[]{:S(2)}, u32[]{:S(2)}) collective-permute-start(f32[2,3,64,384]{3,2,1,0:T(8,128)S(1)} %get-tuple-element.19), channel_id=1, source_target_pairs={{1,2},{2,1},{3,4},{4,3},{5,6},{6,5},{9,10},{10,9},{11,12},{12,11},... | collective-permute-start | bytes 1769480 | tf_op jit(solution)/shard_map/ppermute | solution.py:666
  8.1 11.3 %all-gather = f32[448,384]{1,0:T(8,128)S(1)} all-gather(f32[56,384]{1,0:T(8,128)S(1)} %get-tuple-element.16), channel_id=2, replica_groups={{0,1,8,9,16,17,24,25},{2,3,10,11,18,19,26,27},{4,5,12,13,20,21,28,29},{..., dimensions={0}, use_global_device_ids=true | all-gather | bytes 774144 | tf_op jit(solution)/shard_map/all_gather | solution.py:670
  19.5 0.0 collective-permute-done.face1
  19.5 0.0 collective-permute-done.1.face2
  19.5 1.9 %collective-permute-start.2 = (f32[48,128]{1,0:T(8,128)S(1)}, f32[48,128]{1,0:T(8,128)S(1)}, u32[]{:S(2)}, u32[]{:S(2)}) collective-permute-start(f32[48,128]{1,0:T(8,128)S(1)} %relay.1), channel_id=1, source_target_pairs={{1,2},{2,1},{3,4},{4,3},{5,6},{6,5},{7,0},{0,7},{9,10},{10,9},{11,... | collective-permute-start | bytes 73736 | tf_op jit(solution)/shard_map/ppermute | solution.py:680
  21.3 1.5 %collective-permute-done.2.got = f32[48,128]{1,0:T(8,128)S(1)} collective-permute-done((f32[48,128]{1,0:T(8,128)S(1)}, f32[48,128]{1,0:T(8,128)S(1)}, u32[]{:S(2)}, u32[]{:S(2)}) %collective-permute-start.2) | collective-permute-done | bytes 24608 | tf_op jit(solution)/shard_map/ppermute | solution.py:680
  22.9 4.9 %collective-permute-start.3 = (f32[8,128]{1,0:T(8,128)S(1)}, f32[8,128]{1,0:T(8,128)S(1)}, u32[]{:S(2)}, u32[]{:S(2)}) collective-permute-start(f32[8,128]{1,0:T(8,128)S(1)} %slice_add_fusion.coef), channel_id=1, source_target_pairs={{0,3},{7,4},{2,5},{5,2},{1,6},{6,1},{8,11},{15,12},{10,13},{13,10}... | collective-permute-start | bytes 12296 | tf_op jit(solution)/shard_map/ppermute | solution.py:684
  27.8 0.0 copy-start
  27.8 0.0 copy-start.1
  27.8 1.9 %sweeps.1 = f32[3,4,64,384]{3,2,1,0:T(8,128)} custom-call(f32[3,4,64,384]{3,2,1,0:T(8,128)S(1)} %get-tuple-element.21.u, f32[3,4,64,384]{3,2,1,0:T(8,128)S(1)} %get-tuple-element.22.f, f32[3,4,64,384]{3,2,1,0:T(8,128)S(1)} %get-tuple-element.23.first, f32[2,3,64,384]{3,2,1,0:T(8,128)S(1)} %collective-permute-done.face1, ...), custom_call_target="tpu_custom_call" | custom-call | tf_op jit(solution)/shard_map/sweeps/pallas_call | solution.py:689
  29.7 0.0 collective-permute-done.3.rest
  29.7 0.4 %copy-done = f32[12,512,128]{2,1,0:T(8,128)S(1)} copy-done((f32[12,512,128]{2,1,0:T(8,128)S(1)}, f32[12,512,128]{2,1,0:T(8,128)}, u32[]{:S(2)}) %copy-start) | copy-done | bytes 3145752
  30.1 0.0 copy-done.1
  30.1 1.8 %synthesis.1 = f32[2,64,384]{2,1,0:T(8,128)} custom-call(f32[8,128]{1,0:T(8,128)S(1)} %slice_add_fusion.coef, f32[8,128]{1,0:T(8,128)S(1)} %collective-permute-done.3.rest, f32[2,8,128]{2,1,0:T(8,128)S(1)} %get-tuple-element.29.gains, s32[64,384]{1,0:T(8,128)S(1)} %copy-done.1, f32[12,512,128]{2,1,0:T(8,128)S(1)} %copy-done), custom_call_target="tpu_custom_call" | custom-call | tf_op jit(solution)/shard_map/synthesis/pallas_call | solution.py:706
  (2 shorter events, 0.0 us)
Async XLA Ops:
  3.5 16.0 %collective-permute-start = (f32[2,3,64,384]{3,2,1,0:T(8,128)S(1)}, f32[2,3,64,384]{3,2,1,0:T(8,128)S(1)}, u32[]{:S(2)}, u32[]{:S(2)}) collective-permute-start(f32[2,3,64,384]{3,2,1,0:T(8,128)S(1)} %get-tuple-element.18), channel_id=1, source_target_pairs={{0,1},{1,0},{2,3},{3,2},{4,5},{5,4},{6,7},{7,6},{8,9},{9,8},{10,11... | collective-permute-start | bytes 1769480 | tf_op jit(solution)/shard_map/ppermute | solution.py:667
  5.9 13.6 %collective-permute-start.1 = (f32[2,3,64,384]{3,2,1,0:T(8,128)S(1)}, f32[2,3,64,384]{3,2,1,0:T(8,128)S(1)}, u32[]{:S(2)}, u32[]{:S(2)}) collective-permute-start(f32[2,3,64,384]{3,2,1,0:T(8,128)S(1)} %get-tuple-element.19), channel_id=1, source_target_pairs={{1,2},{2,1},{3,4},{4,3},{5,6},{6,5},{9,10},{10,9},{11,12},{12,11},... | collective-permute-start | bytes 1769480 | tf_op jit(solution)/shard_map/ppermute | solution.py:666
  19.5 3.4 %collective-permute-start.2 = (f32[48,128]{1,0:T(8,128)S(1)}, f32[48,128]{1,0:T(8,128)S(1)}, u32[]{:S(2)}, u32[]{:S(2)}) collective-permute-start(f32[48,128]{1,0:T(8,128)S(1)} %relay.1), channel_id=1, source_target_pairs={{1,2},{2,1},{3,4},{4,3},{5,6},{6,5},{7,0},{0,7},{9,10},{10,9},{11,... | collective-permute-start | bytes 73736 | tf_op jit(solution)/shard_map/ppermute | solution.py:680
  22.9 6.9 %collective-permute-start.3 = (f32[8,128]{1,0:T(8,128)S(1)}, f32[8,128]{1,0:T(8,128)S(1)}, u32[]{:S(2)}, u32[]{:S(2)}) collective-permute-start(f32[8,128]{1,0:T(8,128)S(1)} %slice_add_fusion.coef), channel_id=1, source_target_pairs={{0,3},{7,4},{2,5},{5,2},{1,6},{6,1},{8,11},{15,12},{10,13},{13,10}... | collective-permute-start | bytes 12296 | tf_op jit(solution)/shard_map/ppermute | solution.py:684
  27.8 2.3 %copy-start = (f32[12,512,128]{2,1,0:T(8,128)S(1)}, f32[12,512,128]{2,1,0:T(8,128)}, u32[]{:S(2)}) copy-start(f32[12,512,128]{2,1,0:T(8,128)} %constant.2.clone.tbl.tab) | copy-start | bytes 9437188
  27.8 2.3 %copy-start.1 = (s32[64,384]{1,0:T(8,128)S(1)}, s32[64,384]{1,0:T(8,128)}, u32[]{:S(2)}) copy-start(s32[64,384]{1,0:T(8,128)} %ids.3) | copy-start | bytes 294916

commit v6 on v5

--- a/solution.py
+++ b/solution.py
@@ -106,99 +106,116 @@
     return values
 
 
+def local_sweep(u, f, every, layer, lower, upper, result, at_layer):
+    rows, width = u.shape[2:]
+    per_row, total = width // LANES, rows // SUB
+    coef = [jnp.broadcast_to(every[layer, j:j + 1, :], (SUB, LANES)) for j in range(12)]
+    none = jnp.zeros((1, LANES), jnp.float32)
+    for g in range(total):
+        here = slice(SUB * g, SUB * g + SUB)
+        values = [spans(per_row, u, c, layer, here) for c in range(3)]
+        for c in range(3):
+            aside = roll_columns(values[c])
+            for j in range(per_row):
+                at = (c, layer)
+                above = u[at + (slice(SUB * g - 1, SUB * g), chunk(j))] if g > 0 else none
+                under = u[at + (slice(SUB * g + SUB, SUB * g + SUB + 1), chunk(j))] if g < total - 1 else none
+                near = roll_rows(values[c][j], above, under) + aside[j]
+                if lower is not None:
+                    near = near + u[c, lower, here, chunk(j)]
+                if upper is not None:
+                    near = near + u[c, upper, here, chunk(j)]
+                value = relax(c, [values[d][j] for d in range(3)], near, f[c, layer, here, chunk(j)], coef)
+                result[c, at_layer, here, chunk(j)] = value
+
+
+def faces_kernel(
+    disp, forc, lid, stiff, coup, ids, cnt,
+    u, f, outer_s, face1, face2, send, every, cyc, num,
+    lids, stiffs, coups, small_sem, near_sem, u_sem, f_sem, face_sem,
+):
+    layers = disp.shape[1]
+    top = layers - 1
+    odd = lax.rem(lax.axis_index("rad"), 2) == 1
+    small = [
+        pltpu.make_async_copy(lid, lids, small_sem.at[0]),
+        pltpu.make_async_copy(stiff, stiffs, small_sem.at[1]),
+        pltpu.make_async_copy(coup, coups, small_sem.at[2]),
+    ]
+    cycles = [
+        pltpu.make_async_copy(cnt, num, near_sem.at[0]),
+        pltpu.make_async_copy(ids, cyc, near_sem.at[1]),
+    ]
+    loads_u = [pltpu.make_async_copy(disp.at[:, r], u.at[:, r], u_sem.at[r]) for r in range(layers)]
+    loads_f = [pltpu.make_async_copy(forc.at[:, r], f.at[:, r], f_sem.at[r]) for r in range(layers)]
+    for copy in small:
+        copy.start()
+    for r in [0, 1, top] + list(range(top - 1, 1, -1)):
+        loads_u[r].start()
+        if r in (0, top):
+            loads_f[r].start()
+    for r in range(1, top):
+        loads_f[r].start()
+    for copy in cycles:
+        copy.start()
+    for copy in small:
+        copy.wait()
+    for r in range(layers):
+        every[r] = coefficient_rows(*layer_scalars(r, lids, stiffs, coups))
+    send[...] = every[jnp.where(odd, top, 0)]
+
+    loads_u[0].wait()
+    loads_f[0].wait()
+    loads_u[1].wait()
+    local_sweep(u, f, every, 0, None, 1, outer_s, 0)
+    for r in range(2, layers):
+        loads_u[r].wait()
+    loads_f[top].wait()
+    faces = []
+    for n, (face, high) in enumerate(((face1, jnp.logical_not(odd)), (face2, odd))):
+        source = jnp.where(high, top, 0)
+        swept = jnp.where(high, 1, 0)
+        faces.append(pltpu.make_async_copy(u.at[:, source], face.at[0], face_sem.at[2 * n]))
+        faces.append(pltpu.make_async_copy(outer_s.at[:, swept], face.at[1], face_sem.at[2 * n + 1]))
+    faces[0].start()
+    faces[2].start()
+    local_sweep(u, f, every, top, top - 1, None, outer_s, 1)
+    faces[1].start()
+    faces[3].start()
+    for copy in loads_f[1:top] + cycles + faces:
+        copy.wait()
+
+
 def analysis_kernel(
-    disp, forc, lid, stiff, coup, ids, cnt, grav, tbl,
-    u, f, s, face1, face2, pay, send, every, gains,
-    cyc, num, tab, mat, windows, gain_in, lids, stiffs, coups, first_ids, last_ids,
-    small_sem, near_sem, u_sem, f_sem, face_sem, tab_sem,
+    u, f, outer_s, every, cyc, num, ids, grav, tbl,
+    inner_s, pay, gains,
+    tab, mat, windows, gain_in, first_ids, last_ids, near_sem, tab_sem,
 ):
-    layers, rows, width = disp.shape[1:]
-    chunks = cnt.shape[0]
+    layers, rows, width = u.shape[1:]
+    chunks = num.shape[0]
     groups = tbl.shape[1] // SUB
     per_row = width // LANES
     lat, lats = lax.axis_index("lat"), lax.axis_size("lat")
     rad, rads = lax.axis_index("rad"), lax.axis_size("rad")
     bottom = rad == 0
     at_end = jnp.logical_or(bottom, rad == rads - 1)
-    edge = jnp.where(bottom, 0, layers - 1)
-    inner = jnp.where(bottom, 1, layers - 2)
+    top = layers - 1
+    edge, inner = jnp.where(bottom, 0, top), jnp.where(bottom, 1, top - 1)
+    edge_s, inner_at = jnp.where(bottom, 0, 1), jnp.where(bottom, 0, top - 2)
     total = rows // SUB
-
-    top = layers - 1
-    odd = lax.rem(rad, 2) == 1
-    small = [
-        pltpu.make_async_copy(lid, lids, small_sem.at[0]),
-        pltpu.make_async_copy(stiff, stiffs, small_sem.at[1]),
-        pltpu.make_async_copy(coup, coups, small_sem.at[2]),
-    ]
+    at_core = every[jnp.where(lax.rem(rad, 2) == 1, 0, top)]
     cycles = [
         pltpu.make_async_copy(ids.at[pl.ds(0, SUB), pl.ds(0, LANES)], first_ids, near_sem.at[0]),
         pltpu.make_async_copy(
             ids.at[pl.ds(rows - SUB, SUB), pl.ds(width - LANES, LANES)], last_ids, near_sem.at[1]
         ),
-        pltpu.make_async_copy(cnt, num, near_sem.at[2]),
-        pltpu.make_async_copy(ids, cyc, near_sem.at[3]),
-        pltpu.make_async_copy(grav, gain_in, near_sem.at[4]),
+        pltpu.make_async_copy(grav, gain_in, near_sem.at[2]),
     ]
-    loads_u = [pltpu.make_async_copy(disp.at[:, r], u.at[:, r], u_sem.at[r]) for r in range(layers)]
-    loads_f = [pltpu.make_async_copy(forc.at[:, r], f.at[:, r], f_sem.at[r]) for r in range(layers)]
-    order = [0, 1, top] + list(range(top - 1, 1, -1))
-    for copy in small:
-        copy.start()
-    for r in order:
-        loads_u[r].start()
-        loads_f[r].start()
     for copy in cycles:
         copy.start()
-    for copy in small:
-        copy.wait()
-
-    for r in range(layers):
-        every[r] = coefficient_rows(*layer_scalars(r, lids, stiffs, coups))
-    send[...] = every[jnp.where(odd, top, 0)]
-    at_core = every[jnp.where(odd, 0, top)]
-
-    def local_sweep(layer, lower, upper):
-        coef = [jnp.broadcast_to(every[layer, j:j + 1, :], (SUB, LANES)) for j in range(12)]
-        none = jnp.zeros((1, LANES), jnp.float32)
-        for g in range(total):
-            here = slice(SUB * g, SUB * g + SUB)
-            values = [spans(per_row, u, c, layer, here) for c in range(3)]
-            for c in range(3):
-                aside = roll_columns(values[c])
-                for j in range(per_row):
-                    at = (c, layer)
-                    above = u[at + (slice(SUB * g - 1, SUB * g), chunk(j))] if g > 0 else none
-                    under = u[at + (slice(SUB * g + SUB, SUB * g + SUB + 1), chunk(j))] if g < total - 1 else none
-                    near = roll_rows(values[c][j], above, under) + aside[j]
-                    if lower is not None:
-                        near = near + u[c, lower, here, chunk(j)]
-                    if upper is not None:
-                        near = near + u[c, upper, here, chunk(j)]
-                    value = relax(c, [values[d][j] for d in range(3)], near, f[c, layer, here, chunk(j)], coef)
-                    s[c, layer, here, chunk(j)] = value
-
-    loads_u[0].wait()
-    loads_f[0].wait()
-    loads_u[1].wait()
-    local_sweep(0, None, 1)
-    for r in range(2, layers):
-        loads_u[r].wait()
-    loads_f[top].wait()
-    faces = []
-    for n, (face, layer) in enumerate(((face1, jnp.where(odd, 0, top)), (face2, jnp.where(odd, top, 0)))):
-        faces.append(pltpu.make_async_copy(u.at[:, layer], face.at[0], face_sem.at[2 * n]))
-        faces.append(pltpu.make_async_copy(s.at[:, layer], face.at[1], face_sem.at[2 * n + 1]))
-    faces[0].start()
-    faces[2].start()
-    local_sweep(top, top - 1, None)
-    faces[1].start()
-    faces[3].start()
-    for r in range(1, top):
-        loads_f[r].wait()
 
     def middle(r, carry):
-        local_sweep(r, r - 1, r + 1)
+        local_sweep(u, f, every, r, r - 1, r + 1, inner_s, r - 1)
         return carry
 
     lax.fori_loop(1, top, middle, 0)
@@ -300,7 +317,7 @@
         for j in range(per_row):
             shifted = jnp.where(sub8 == 0, pltpu.roll(over[0][j], SUB - 1, 0),
                                 jnp.where(sub8 == 3, pltpu.roll(over[0][j], 1, 0), 0.0))
-            near = over_inner[j] + aside[j] + shifted + ends_of(s, (0, edge), j)
+            near = over_inner[j] + aside[j] + shifted + ends_of(outer_s, (0, edge_s), j)
             value = relax(0, [over[c][j] for c in range(3)], near, zero, outer)
             spill.append(value * jnp.where(before, low_in, high_in))
         ends = [[over[0][j][1:2, :] for j in range(per_row)], [over[0][j][2:3, :] for j in range(per_row)]]
@@ -320,9 +337,9 @@
         windowed = [window_of(spill, spill_ids)]
         for g in range(total):
             here = rows_of(g)
-            centers = [spans(per_row, s, c, edge, here) for c in range(3)]
-            near = lateral(s, g, (0, edge), ends)
-            inners = spans(per_row, s, 0, inner, here)
+            centers = [spans(per_row, outer_s, c, edge_s, here) for c in range(3)]
+            near = lateral(outer_s, g, (0, edge_s), ends)
+            inners = spans(per_row, inner_s, 0, inner_at, here)
             force = spans(per_row, f, 0, edge, here)
             values = [
                 relax(0, [center[j] for center in centers], near[j] + inners[j], force[j], outer)
@@ -372,13 +389,11 @@
             for r in range(layers):
                 at = base + c * layers + r
                 ref[at:at + 1, :] = u[c, r, near:near + 1, :]
-                ref[at + tall:at + tall + 1, :] = s[c, r, near:near + 1, :]
+                source, layer = (outer_s, r // top) if r in (0, top) else (inner_s, r - 1)
+                ref[at + tall:at + tall + 1, :] = source[c, layer, near:near + 1, :]
 
     pack(pay, SUB, 0)
     pack(pay, SUB + 2 * tall, rows - 1)
-
-    for copy in faces:
-        copy.wait()
 
 
 def relay_kernel(ring, send, out):
@@ -406,7 +421,7 @@
 
 
 def sweep_kernel(
-    u, f, first, face1, face2, ring, got, every,
+    u, f, outer_s, inner_s, face1, face2, ring, got, every,
     out,
     s, rim, done, cf, out_sem,
 ):
@@ -506,8 +521,10 @@
                         value = lo((1, c) + at) + gain * u[(c, 0) + at]
                     elif layer == layers + 1:
                         value = hi((1, c) + at) + gain * u[(c, top) + at]
+                    elif layer in (1, layers):
+                        value = outer_s[(c, layer // layers) + at]
                     else:
-                        value = first[(c, layer - 1) + at]
+                        value = inner_s[(c, layer - 2) + at]
                     if layer == 1:
                         value = value + gain * lo((0, c) + at)
                     if layer == layers:
@@ -629,42 +646,58 @@
             cycle_count.reshape(chunks, LANES), gravity, table,
         )
     ]
-    u, f, swept, face1, face2, pay, mine, every, gains = pl.pallas_call(
+    u, f, outer_s, face1, face2, mine, every, cyc, num = pl.pallas_call(
+        faces_kernel,
+        out_shape=(
+            whole, whole,
+            jax.ShapeDtypeStruct((3, 2, rows, width), f32),
+            face, face,
+            jax.ShapeDtypeStruct((COEFS, LANES), f32),
+            jax.ShapeDtypeStruct((layers, COEFS, LANES), f32),
+            jax.ShapeDtypeStruct(cycle_id.shape, jnp.int32),
+            jax.ShapeDtypeStruct((chunks, LANES), jnp.int32),
+        ),
+        in_specs=[HBM] * 7,
+        out_specs=(VMEM,) * 9,
+        scratch_shapes=[
+            pltpu.SMEM(layer_id.shape, jnp.int32),
+            pltpu.SMEM(stiffness.shape, f32),
+            pltpu.SMEM(coupling.shape[1:] + coupling.shape[:1], f32),
+            pltpu.SemaphoreType.DMA((3,)),
+            pltpu.SemaphoreType.DMA((2,)),
+            pltpu.SemaphoreType.DMA((layers,)),
+            pltpu.SemaphoreType.DMA((layers,)),
+            pltpu.SemaphoreType.DMA((4,)),
+        ],
+        compiler_params=pltpu.CompilerParams(vmem_limit_bytes=VMEM_LIMIT),
+        name="faces",
+    )(*pinned[:7])
+
+    beside2 = lax.ppermute(face2, "rad", odd_pairs(rads)[:-2])
+    beside1 = lax.ppermute(face1, "rad", even_pairs(rads))
+
+    inner_s, pay, gains = pl.pallas_call(
         analysis_kernel,
         out_shape=(
-            whole, whole, whole, face, face,
+            jax.ShapeDtypeStruct((3, layers - 2, rows, width), f32),
             jax.ShapeDtypeStruct((SUB + 4 * tall, width), f32),
-            jax.ShapeDtypeStruct((COEFS, LANES), f32),
-            jax.ShapeDtypeStruct((layers, COEFS, LANES), f32),
             jax.ShapeDtypeStruct((2, SUB, LANES), f32),
         ),
-        in_specs=[HBM] * 9,
-        out_specs=(VMEM,) * 9,
+        in_specs=[VMEM] * 6 + [HBM] * 3,
+        out_specs=(VMEM,) * 3,
         scratch_shapes=[
-            pltpu.VMEM(cycle_id.shape, jnp.int32),
-            pltpu.VMEM((chunks, LANES), jnp.int32),
             pltpu.VMEM((BATCH, degrees, LANES), f32),
             pltpu.VMEM((2, COEFS, LANES), f32),
             pltpu.VMEM((2, rows // SUB + 1, SUB, LANES), f32),
             pltpu.VMEM(gravity.shape, f32),
-            pltpu.SMEM(layer_id.shape, jnp.int32),
-            pltpu.SMEM(stiffness.shape, f32),
-            pltpu.SMEM(coupling.shape[1:] + coupling.shape[:1], f32),
             pltpu.SMEM((SUB, LANES), jnp.int32),
             pltpu.SMEM((SUB, LANES), jnp.int32),
             pltpu.SemaphoreType.DMA((3,)),
-            pltpu.SemaphoreType.DMA((5,)),
-            pltpu.SemaphoreType.DMA((layers,)),
-            pltpu.SemaphoreType.DMA((layers,)),
-            pltpu.SemaphoreType.DMA((4,)),
             pltpu.SemaphoreType.DMA((BATCH,)),
         ],
         compiler_params=pltpu.CompilerParams(vmem_limit_bytes=VMEM_LIMIT),
         name="analysis",
-    )(*pinned)
-
-    beside2 = lax.ppermute(face2, "rad", odd_pairs(rads)[:-2])
-    beside1 = lax.ppermute(face1, "rad", even_pairs(rads))
+    )(u, f, outer_s, every, cyc, num, pinned[5], *pinned[7:])
 
     chips = [[a * rads + b + c for a in range(lats) for c in range(cores)] for b in range(0, rads, cores)]
     ring = lax.all_gather(pay, ("lat", "rad"), axis_index_groups=chips)
@@ -681,7 +714,7 @@
     coef = outward[:SUB]
     if rads == 8:
         coef = coef + got[:SUB]
-        rest = lax.ppermute(coef, "rad", [(0, 3), (7, 4), (2, 5), (5, 2), (1, 6), (6, 1)])
+        rest = lax.ppermute(coef, "rad", [(0, 3), (3, 0), (7, 4), (4, 7), (2, 5), (5, 2), (1, 6), (6, 1)])
     else:
         coef = lax.psum(coef, "rad") * (1.0 / cores)
         rest = jnp.zeros_like(coef)
@@ -689,7 +722,7 @@
     smoothed = pl.pallas_call(
         sweep_kernel,
         out_shape=whole,
-        in_specs=[VMEM] * 8,
+        in_specs=[VMEM] * 9,
         out_specs=HBM,
         scratch_shapes=[
             pltpu.VMEM((3, layers + 2, rows, width), f32),
@@ -700,7 +733,7 @@
         ],
         compiler_params=pltpu.CompilerParams(vmem_limit_bytes=VMEM_LIMIT),
         name="sweeps",
-    )(u, f, swept, beside1, beside2, ring, got, every)
+    )(u, f, outer_s, inner_s, beside1, beside2, ring, got, every)
     coef, smoothed = lax.optimization_barrier((coef, smoothed))
 
     potential = pl.pallas_call(
@@ -711,7 +744,7 @@
         scratch_shapes=[pltpu.VMEM((2 * groups, SUB, LANES), f32)],
         compiler_params=pltpu.CompilerParams(vmem_limit_bytes=VMEM_LIMIT),
         name="synthesis",
-    )(coef, rest, gains, cycle_id, table)
+    )(coef, rest, gains, cyc, table)
     return smoothed, potential
 
 

time: 32.2 us -> 29.7 us (0.922)
  starting transfers between devices: 11.5 us -> 9.53 us
  blocking collectives: 11.3 us -> 10.2 us
  waiting for transfers between devices: 1.52 us -> 1.88 us
    ppermute x1, starting transfers between devices: 2.4 us -> 0.12 us  [local(): beside1 = lax.ppermute(face1, 'rad', even_pairs(rads))]
    ppermute x1, starting transfers between devices: 2.28 us -> 4.55 us  [local(): beside2 = lax.ppermute(face2, 'rad', odd_pairs(rads)[:-2])]
    ppermute x1, starting transfers between devices: 4.94 us -> 3.41 us  [local(): lax.ppermute(coef, 'rad', [(0, 3), (3, 0), (7, 4), (4, 7), (2, 5), (5, 2)...]
    all_gather x1, blocking collectives: 11.3 us -> 10.2 us  [local(): ring = lax.all_gather(pay, ('lat', 'rad'), axis_index_groups=chips)]
    ppermute x1, starting transfers between devices: 1.86 us -> 1.45 us  [local(): got = lax.ppermute(outward, 'rad', odd_pairs(rads))]
    ppermute x1, waiting for transfers between devices: 1.51 us -> 1.87 us  [local(): got = lax.ppermute(outward, 'rad', odd_pairs(rads))]
    pallas_call x2 -> x3, Pallas kernels: 4.69 us -> 4.95 us  [the longest x1 2.02 us: local(): pl.pallas_call(faces_kernel, out_shape=(whole, whole, jax.ShapeDtypeStruc...]
  transfers between devices with their start and end apart: 4 -> 4, of which waited for: 1 -> 1; matrix products, arithmetic and copies ran while one was open for 0% -> 0% of each run, Pallas kernels for 6% -> 10%
where the time goes in v6:
time: 29.7 us; the launch traced here: 29.5 us
  blocking collectives  10.2 us (34%)
  starting transfers between devices  9.53 us (32%)
  Pallas kernels  6.82 us (23%)
  waiting for transfers between devices  1.88 us (6%)
  between operations  0.7 us (2%)
  local copies, waits for them, and re-layouts  0.35 us (1%)
    all_gather x1, blocking collectives, local(): ring = lax.all_gather(pay, ('lat', 'rad'), axis_index_groups=chips)  10.2 us
    ppermute x1, starting transfers between devices, local(): beside2 = lax.ppermute(face2, 'rad', odd_pairs(rads)[:-2])  4.55 us
    ppermute x1, starting transfers between devices, local(): lax.ppermute(coef, 'rad', [(0, 3), (3, 0), (7, 4), (4, 7), (2, 5), (5, 2)...  3.41 us
    pallas_call x1, Pallas kernels, local(): pl.pallas_call(faces_kernel, out_shape=(whole, whole, jax.ShapeDtypeStruc...  2.02 us
    pallas_call x1, Pallas kernels, local(): pl.pallas_call(sweep_kernel, out_shape=whole, in_specs=[VMEM] * 9, out_sp...  1.95 us
    ppermute x1, waiting for transfers between devices, local(): got = lax.ppermute(outward, 'rad', odd_pairs(rads))  1.87 us
    pallas_call x1, Pallas kernels, local(): pl.pallas_call(functools.partial(synthesis_kernel, 2.0 / cycles), out_sha...  1.84 us
    ppermute x1, starting transfers between devices, local(): got = lax.ppermute(outward, 'rad', odd_pairs(rads))  1.45 us
  transfers between devices with their start and end apart: 4, of which 1 were waited for; matrix products, arithmetic and copies ran while one was open for 0% of the time, Pallas kernels for 10%

profile of v6, /device:TPU:1, one launch (start us, length us, event | category | flops | bytes accessed | tf_op | source)
XLA Modules:
  0.0 29.5 jit_solution(51057949715913598)
XLA Ops:
  0.6 2.0 %faces.1 = (f32[3,4,64,384]{3,2,1,0:T(8,128)S(1)}, f32[3,4,64,384]{3,2,1,0:T(8,128)S(1)}, f32[3,2,64,384]{3,2,1,0:T(8,128)S(1)}, f32[2,3,64,384]{3,2,1,0:T(8,128...) custom-call(f32[3,4,64,384]{3,2,1,0:T(8,128)} %disp.1, ...), custom_call_target="tpu_custom_call" | custom-call | tf_op jit(solution)/shard_map/faces/pallas_call | solution.py:649
  2.7 0.1 collective-permute-start
  2.8 4.6 %collective-permute-start.1 = (f32[2,3,64,384]{3,2,1,0:T(8,128)S(1)}, f32[2,3,64,384]{3,2,1,0:T(8,128)S(1)}, u32[]{:S(2)}, u32[]{:S(2)}) collective-permute-start(f32[2,3,64,384]{3,2,1,0:T(8,128)S(1)} %get-tuple-element.28), channel_id=1, source_target_pairs={{1,2},{2,1},{3,4},{4,3},{5,6},{6,5},{9,10},{10,9},{11,12},{12,11},... | collective-permute-start | bytes 1769480 | tf_op jit(solution)/shard_map/ppermute | solution.py:676
  7.3 1.0 %analysis.1 = (f32[3,2,64,384]{3,2,1,0:T(8,128)S(1)}, f32[56,384]{1,0:T(8,128)S(1)}, f32[2,8,128]{2,1,0:T(8,128)S(1)}) custom-call(f32[3,4,64,384]{3,2,1,0:T(8,128)S(1)} %get-tuple-element.19.u, f32[3,4,64,384]{3,2,1,0:T(8,128)S(1)} %get-tuple-element.20.f, f32[3,2,64,384]{3,2,1,0:T(8,128)S(1)} %get-tuple-element.21.outer_s, ...), custom_call_target="tpu_custom_call" | custom-call | tf_op jit(solution)/shard_map/analysis/pallas_call | solution.py:679
  8.3 10.2 %all-gather = f32[448,384]{1,0:T(8,128)S(1)} all-gather(f32[56,384]{1,0:T(8,128)S(1)} %get-tuple-element.25), channel_id=2, replica_groups={{0,1,8,9,16,17,24,25},{2,3,10,11,18,19,26,27},{4,5,12,13,20,21,28,29},{..., dimensions={0}, use_global_device_ids=true | all-gather | bytes 774144 | tf_op jit(solution)/shard_map/all_gather | solution.py:703
  18.6 0.0 collective-permute-done.face1
  18.6 0.0 collective-permute-done.1.face2
  18.6 1.4 %collective-permute-start.2 = (f32[48,128]{1,0:T(8,128)S(1)}, f32[48,128]{1,0:T(8,128)S(1)}, u32[]{:S(2)}, u32[]{:S(2)}) collective-permute-start(f32[48,128]{1,0:T(8,128)S(1)} %relay.1), channel_id=1, source_target_pairs={{1,2},{2,1},{3,4},{4,3},{5,6},{6,5},{7,0},{0,7},{9,10},{10,9},{11,... | collective-permute-start | bytes 73736 | tf_op jit(solution)/shard_map/ppermute | solution.py:713
  20.0 1.9 %collective-permute-done.2.got = f32[48,128]{1,0:T(8,128)S(1)} collective-permute-done((f32[48,128]{1,0:T(8,128)S(1)}, f32[48,128]{1,0:T(8,128)S(1)}, u32[]{:S(2)}, u32[]{:S(2)}) %collective-permute-start.2) | collective-permute-done | bytes 24608 | tf_op jit(solution)/shard_map/ppermute | solution.py:713
  21.9 3.4 %collective-permute-start.3 = (f32[8,128]{1,0:T(8,128)S(1)}, f32[8,128]{1,0:T(8,128)S(1)}, u32[]{:S(2)}, u32[]{:S(2)}) collective-permute-start(f32[8,128]{1,0:T(8,128)S(1)} %slice_add_fusion.coef), channel_id=1, source_target_pairs={{0,3},{3,0},{7,4},{4,7},{2,5},{5,2},{1,6},{6,1},{8,11},{11,8},{15,... | collective-permute-start | bytes 12296 | tf_op jit(solution)/shard_map/ppermute | solution.py:717
  25.3 0.0 copy-start
  25.3 2.0 %sweeps.1 = f32[3,4,64,384]{3,2,1,0:T(8,128)} custom-call(f32[3,4,64,384]{3,2,1,0:T(8,128)S(1)} %get-tuple-element.19.u, f32[3,4,64,384]{3,2,1,0:T(8,128)S(1)} %get-tuple-element.20.f, f32[3,2,64,384]{3,2,1,0:T(8,128)S(1)} %get-tuple-element.21.outer_s, f32[3,2,64,384]{3,2,1,0:T(8,128)S(1)} %get-tuple-element.30.inner_s, ...), custom_call_target="tpu_custom_call" | custom-call | tf_op jit(solution)/shard_map/sweeps/pallas_call | solution.py:722
  27.3 0.0 collective-permute-done.3.rest
  27.3 0.3 %copy-done = f32[12,512,128]{2,1,0:T(8,128)S(1)} copy-done((f32[12,512,128]{2,1,0:T(8,128)S(1)}, f32[12,512,128]{2,1,0:T(8,128)}, u32[]{:S(2)}) %copy-start) | copy-done | bytes 3145752
  27.6 1.8 %synthesis.1 = f32[2,64,384]{2,1,0:T(8,128)} custom-call(f32[8,128]{1,0:T(8,128)S(1)} %slice_add_fusion.coef, f32[8,128]{1,0:T(8,128)S(1)} %collective-permute-done.3.rest, f32[2,8,128]{2,1,0:T(8,128)S(1)} %get-tuple-element.35.gains, s32[64,384]{1,0:T(8,128)S(1)} %get-tuple-element.23.cyc.ids, f32[12,512,128]{2,1,0:T(8,128)S(1)} %copy-done), custom_call_target="tpu_custom_call" | custom-call | tf_op jit(solution)/shard_map/synthesis/pallas_call | solution.py:739
  (2 shorter events, 0.0 us)
Async XLA Ops:
  2.7 15.9 %collective-permute-start = (f32[2,3,64,384]{3,2,1,0:T(8,128)S(1)}, f32[2,3,64,384]{3,2,1,0:T(8,128)S(1)}, u32[]{:S(2)}, u32[]{:S(2)}) collective-permute-start(f32[2,3,64,384]{3,2,1,0:T(8,128)S(1)} %get-tuple-element.27), channel_id=1, source_target_pairs={{0,1},{1,0},{2,3},{3,2},{4,5},{5,4},{6,7},{7,6},{8,9},{9,8},{10,11... | collective-permute-start | bytes 1769480 | tf_op jit(solution)/shard_map/ppermute | solution.py:677
  2.8 15.8 %collective-permute-start.1 = (f32[2,3,64,384]{3,2,1,0:T(8,128)S(1)}, f32[2,3,64,384]{3,2,1,0:T(8,128)S(1)}, u32[]{:S(2)}, u32[]{:S(2)}) collective-permute-start(f32[2,3,64,384]{3,2,1,0:T(8,128)S(1)} %get-tuple-element.28), channel_id=1, source_target_pairs={{1,2},{2,1},{3,4},{4,3},{5,6},{6,5},{9,10},{10,9},{11,12},{12,11},... | collective-permute-start | bytes 1769480 | tf_op jit(solution)/shard_map/ppermute | solution.py:676
  18.6 3.3 %collective-permute-start.2 = (f32[48,128]{1,0:T(8,128)S(1)}, f32[48,128]{1,0:T(8,128)S(1)}, u32[]{:S(2)}, u32[]{:S(2)}) collective-permute-start(f32[48,128]{1,0:T(8,128)S(1)} %relay.1), channel_id=1, source_target_pairs={{1,2},{2,1},{3,4},{4,3},{5,6},{6,5},{7,0},{0,7},{9,10},{10,9},{11,... | collective-permute-start | bytes 73736 | tf_op jit(solution)/shard_map/ppermute | solution.py:713
  21.9 5.4 %collective-permute-start.3 = (f32[8,128]{1,0:T(8,128)S(1)}, f32[8,128]{1,0:T(8,128)S(1)}, u32[]{:S(2)}, u32[]{:S(2)}) collective-permute-start(f32[8,128]{1,0:T(8,128)S(1)} %slice_add_fusion.coef), channel_id=1, source_target_pairs={{0,3},{3,0},{7,4},{4,7},{2,5},{5,2},{1,6},{6,1},{8,11},{11,8},{15,... | collective-permute-start | bytes 12296 | tf_op jit(solution)/shard_map/ppermute | solution.py:717
  25.3 2.3 %copy-start = (f32[12,512,128]{2,1,0:T(8,128)S(1)}, f32[12,512,128]{2,1,0:T(8,128)}, u32[]{:S(2)}) copy-start(f32[12,512,128]{2,1,0:T(8,128)} %constant.2.clone.tbl.tab) | copy-start | bytes 9437188

commit v7 on v6

--- a/solution.py
+++ b/solution.py
@@ -106,33 +106,31 @@
     return values
 
 
-def local_sweep(u, f, every, layer, lower, upper, result, at_layer):
+def local_sweep(u, f, every, layer, beside, store, groups=None, parts=(0, 1, 2)):
     rows, width = u.shape[2:]
     per_row, total = width // LANES, rows // SUB
     coef = [jnp.broadcast_to(every[layer, j:j + 1, :], (SUB, LANES)) for j in range(12)]
     none = jnp.zeros((1, LANES), jnp.float32)
-    for g in range(total):
+    for g in range(total) if groups is None else groups:
         here = slice(SUB * g, SUB * g + SUB)
         values = [spans(per_row, u, c, layer, here) for c in range(3)]
-        for c in range(3):
+        for c in parts:
             aside = roll_columns(values[c])
             for j in range(per_row):
                 at = (c, layer)
                 above = u[at + (slice(SUB * g - 1, SUB * g), chunk(j))] if g > 0 else none
                 under = u[at + (slice(SUB * g + SUB, SUB * g + SUB + 1), chunk(j))] if g < total - 1 else none
                 near = roll_rows(values[c][j], above, under) + aside[j]
-                if lower is not None:
-                    near = near + u[c, lower, here, chunk(j)]
-                if upper is not None:
-                    near = near + u[c, upper, here, chunk(j)]
+                for other in beside:
+                    near = near + u[c, other, here, chunk(j)]
                 value = relax(c, [values[d][j] for d in range(3)], near, f[c, layer, here, chunk(j)], coef)
-                result[c, at_layer, here, chunk(j)] = value
+                store(c, g, j, values[c][j], value)
 
 
 def faces_kernel(
     disp, forc, lid, stiff, coup, ids, cnt,
-    u, f, outer_s, face1, face2, send, every, cyc, num,
-    lids, stiffs, coups, small_sem, near_sem, u_sem, f_sem, face_sem,
+    u, f, face1, face2, send, every, cyc, num,
+    lids, stiffs, coups, small_sem, near_sem, u_sem, f_sem,
 ):
     layers = disp.shape[1]
     top = layers - 1
@@ -164,32 +162,46 @@
         every[r] = coefficient_rows(*layer_scalars(r, lids, stiffs, coups))
     send[...] = every[jnp.where(odd, top, 0)]
 
-    loads_u[0].wait()
-    loads_f[0].wait()
-    loads_u[1].wait()
-    local_sweep(u, f, every, 0, None, 1, outer_s, 0)
-    for r in range(2, layers):
-        loads_u[r].wait()
-    loads_f[top].wait()
-    faces = []
-    for n, (face, high) in enumerate(((face1, jnp.logical_not(odd)), (face2, odd))):
-        source = jnp.where(high, top, 0)
-        swept = jnp.where(high, 1, 0)
-        faces.append(pltpu.make_async_copy(u.at[:, source], face.at[0], face_sem.at[2 * n]))
-        faces.append(pltpu.make_async_copy(outer_s.at[:, swept], face.at[1], face_sem.at[2 * n + 1]))
-    faces[0].start()
-    faces[2].start()
-    local_sweep(u, f, every, top, top - 1, None, outer_s, 1)
-    faces[1].start()
-    faces[3].start()
-    for copy in loads_f[1:top] + cycles + faces:
+    for copy in loads_u + [loads_f[0], loads_f[top]]:
         copy.wait()
+    for face, layer in ((face1, jnp.where(odd, 0, top)), (face2, jnp.where(odd, top, 0))):
+        def store(c, g, j, value, swept, face=face):
+            at = (c, slice(SUB * g, SUB * g + SUB), chunk(j))
+            face[(0,) + at] = value
+            face[(1,) + at] = swept
+
+        local_sweep(u, f, every, layer, (jnp.where(layer == 0, 1, top - 1),), store)
+    for copy in loads_f[1:top] + cycles:
+        copy.wait()
+
+
+def inner_kernel(u, f, every, grav, inner_s, gains, gain_in, gain_sem):
+    groups = gain_in.shape[2] // SUB
+    load_gains = pltpu.make_async_copy(grav, gain_in, gain_sem.at[0])
+    load_gains.start()
+
+    def middle(r, carry):
+        def store(c, g, j, value, swept):
+            inner_s[c, r - 1, SUB * g:SUB * g + SUB, chunk(j)] = swept
+
+        local_sweep(u, f, every, r, (r - 1, r + 1), store)
+        return carry
+
+    lax.fori_loop(1, u.shape[1] - 1, middle, 0)
+    load_gains.wait()
+
+    lane1 = iota((1, LANES), 1)
+    for load in range(2):
+        for m in range(groups * SUB // LANES):
+            one, two = gain_in[0, load:load + 1, chunk(m)], gain_in[1, load:load + 1, chunk(m)]
+            gains[load, 2 * m:2 * m + 1, :] = jnp.where(lane1 < groups, one, pltpu.roll(two, groups, 1))
+            gains[load, 2 * m + 1:2 * m + 2, :] = jnp.where(lane1 < groups, pltpu.roll(one, groups, 1), two)
 
 
 def analysis_kernel(
-    u, f, outer_s, every, cyc, num, ids, grav, tbl,
-    inner_s, pay, gains,
-    tab, mat, windows, gain_in, first_ids, last_ids, near_sem, tab_sem,
+    u, f, face1, face2, every, cyc, num, tbl,
+    pay,
+    plane, rims, tab, mat, windows, first_ids, last_ids, near_sem, tab_sem,
 ):
     layers, rows, width = u.shape[1:]
     chunks = num.shape[0]
@@ -201,56 +213,45 @@
     at_end = jnp.logical_or(bottom, rad == rads - 1)
     top = layers - 1
     edge, inner = jnp.where(bottom, 0, top), jnp.where(bottom, 1, top - 1)
-    edge_s, inner_at = jnp.where(bottom, 0, 1), jnp.where(bottom, 0, top - 2)
     total = rows // SUB
-    at_core = every[jnp.where(lax.rem(rad, 2) == 1, 0, top)]
+    odd = lax.rem(rad, 2) == 1
+    at_core = every[jnp.where(odd, 0, top)]
     cycles = [
-        pltpu.make_async_copy(ids.at[pl.ds(0, SUB), pl.ds(0, LANES)], first_ids, near_sem.at[0]),
+        pltpu.make_async_copy(cyc.at[pl.ds(0, SUB), pl.ds(0, LANES)], first_ids, near_sem.at[0]),
         pltpu.make_async_copy(
-            ids.at[pl.ds(rows - SUB, SUB), pl.ds(width - LANES, LANES)], last_ids, near_sem.at[1]
+            cyc.at[pl.ds(rows - SUB, SUB), pl.ds(width - LANES, LANES)], last_ids, near_sem.at[1]
         ),
-        pltpu.make_async_copy(grav, gain_in, near_sem.at[2]),
     ]
-    for copy in cycles:
-        copy.start()
-
-    def middle(r, carry):
-        local_sweep(u, f, every, r, r - 1, r + 1, inner_s, r - 1)
-        return carry
-
-    lax.fori_loop(1, top, middle, 0)
+
+    table = pltpu.make_async_copy(tbl, tab, tab_sem.at[0])
+
+    @pl.when(at_end)
+    def _():
+        for copy in cycles + [table]:
+            copy.start()
+
+    for r in range(1, top):
+        def store(c, g, j, value, swept, r=r):
+            rims[c, r - 1, 0 if g == 0 else 1, :, chunk(j)] = swept
+
+        local_sweep(u, f, every, r, (r - 1, r + 1), store, groups=(0, total - 1))
 
     sub8, lane8 = iota((SUB, LANES), 0), iota((SUB, LANES), 1)
     before = sub8 < 2
     zero = jnp.zeros((SUB, LANES), jnp.float32)
     reach = 2 * width // LEAST_COUNT + 2
-    for copy in cycles:
-        copy.wait()
-    first, last = first_ids[0, 0], last_ids[SUB - 1, LANES - 1]
-    low_part = jnp.right_shift(jnp.maximum(first - reach, 0), 7)
-    high_part = jnp.minimum(jnp.right_shift(last + reach, 7), chunks - 1)
     pay[0:SUB, 0:LANES] = jnp.zeros((SUB, LANES), jnp.float32)
     pay[0:SUB, LANES:2 * LANES] = at_core[0:SUB]
     pay[0:SUB, 2 * LANES:3 * LANES] = at_core[SUB:]
 
-    lane1 = iota((1, LANES), 1)
-    for load in range(2):
-        for m in range(groups * SUB // LANES):
-            one, two = gain_in[0, load:load + 1, chunk(m)], gain_in[1, load:load + 1, chunk(m)]
-            gains[load, 2 * m:2 * m + 1, :] = jnp.where(lane1 < groups, one, pltpu.roll(two, groups, 1))
-            gains[load, 2 * m + 1:2 * m + 2, :] = jnp.where(lane1 < groups, pltpu.roll(one, groups, 1), two)
-
-    def table(b):
-        return [
-            pltpu.make_async_copy(tbl.at[jnp.minimum(low_part + b * BATCH + i, chunks - 1)], tab.at[i], tab_sem.at[i])
-            for i in range(BATCH)
-        ]
-
     @pl.when(at_end)
     def _():
-        for copy in table(0):
-            copy.start()
-
+        def keep_plane(c, g, j, value, swept):
+            plane[SUB * g:SUB * g + SUB, chunk(j)] = swept
+
+        local_sweep(u, f, every, inner, (inner - 1, inner + 1), keep_plane, parts=(0,))
+        first = jnp.broadcast_to(cyc[0:1, 0:1], (SUB, LANES))
+        last = jnp.broadcast_to(cyc[rows - 1:rows, width - 1:width], (SUB, LANES))
         own_first = jnp.zeros((SUB, LANES), jnp.int32)
         own_last = own_first
         for j in range(per_row):
@@ -265,11 +266,9 @@
         index = jnp.where(before, first - lane8, last + lane8)
         place, part = jnp.bitwise_and(index, LANES - 1), jnp.right_shift(index, 7)
         lengths = jnp.full((SUB, LANES), 2 ** 20, jnp.int32)
-        part_first, part_last = jnp.right_shift(first, 7), jnp.right_shift(last, 7)
-        for q in (part_first - 1, part_first, part_last, part_last + 1):
-            row = num[pl.ds(jnp.clip(q, 0, chunks - 1), 1), :]
-            known = jnp.logical_and(part == q, jnp.logical_and(part >= 0, part < chunks))
-            lengths = jnp.where(known, lane_gather(jnp.broadcast_to(row, (SUB, LANES)), place), lengths)
+        for q in range(chunks):
+            row = jnp.broadcast_to(num[q:q + 1, :], (SUB, LANES))
+            lengths = jnp.where(part == q, lane_gather(row, place), lengths)
         lengths = lengths - jnp.where(lane8 == 0, held_here, 0)
         limits = lane_scan(lengths, reach)
         caps = [jnp.broadcast_to(limits[:, i:i + 1], (SUB, LANES)) for i in range(reach)]
@@ -317,7 +316,7 @@
         for j in range(per_row):
             shifted = jnp.where(sub8 == 0, pltpu.roll(over[0][j], SUB - 1, 0),
                                 jnp.where(sub8 == 3, pltpu.roll(over[0][j], 1, 0), 0.0))
-            near = over_inner[j] + aside[j] + shifted + ends_of(outer_s, (0, edge_s), j)
+            near = over_inner[j] + aside[j] + shifted + ends_of(face2, (1, 0), j)
             value = relax(0, [over[c][j] for c in range(3)], near, zero, outer)
             spill.append(value * jnp.where(before, low_in, high_in))
         ends = [[over[0][j][1:2, :] for j in range(per_row)], [over[0][j][2:3, :] for j in range(per_row)]]
@@ -337,9 +336,9 @@
         windowed = [window_of(spill, spill_ids)]
         for g in range(total):
             here = rows_of(g)
-            centers = [spans(per_row, outer_s, c, edge_s, here) for c in range(3)]
-            near = lateral(outer_s, g, (0, edge_s), ends)
-            inners = spans(per_row, inner_s, 0, inner_at, here)
+            centers = [spans(per_row, face2, 1, c, here) for c in range(3)]
+            near = lateral(face2, g, (1, 0), ends)
+            inners = spans(per_row, plane, here)
             force = spans(per_row, f, 0, edge, here)
             values = [
                 relax(0, [center[j] for center in centers], near[j] + inners[j], force[j], outer)
@@ -350,18 +349,20 @@
             windows[0, i] = window
             windows[1, i] = start.astype(jnp.float32)
 
+        for copy in cycles:
+            copy.wait()
+        low_part = jnp.right_shift(jnp.maximum(first_ids[0, 0] - reach, 0), 7)
+        high_part = jnp.minimum(jnp.right_shift(last_ids[SUB - 1, LANES - 1] + reach, 7), chunks - 1)
         half = jnp.where(bottom, groups, 0)
 
+        table.wait()
+
         def batch(b, result):
-            @pl.when(b > 0)
-            def _():
-                for copy in table(b):
-                    copy.start()
-
-            means = []
+            means, blocks = [], []
             for i in range(BATCH):
                 q = low_part + b * BATCH + i
                 part = jnp.minimum(q, chunks - 1)
+                blocks.append(part)
                 acc = zero
                 for w in range(total + 1):
                     at = q * LANES + lane8 - windows[1, w].astype(jnp.int32)
@@ -370,12 +371,10 @@
                 mean = jnp.sum(acc, axis=0, keepdims=True) / num[pl.ds(part, 1), :].astype(jnp.float32)
                 mean = jnp.where(q < chunks, mean, 0.0)
                 means.append(jnp.broadcast_to(mean, (SUB, LANES)))
-            for copy in table(b):
-                copy.wait()
             for g in range(groups):
-                acc = tab[0, SUB * g:SUB * g + SUB, :] * means[0]
+                acc = tab[blocks[0], SUB * g:SUB * g + SUB, :] * means[0]
                 for i in range(1, BATCH):
-                    acc = acc + tab[i, SUB * g:SUB * g + SUB, :] * means[i]
+                    acc = acc + tab[blocks[i], SUB * g:SUB * g + SUB, :] * means[i]
                 column = jnp.broadcast_to(jnp.sum(acc, axis=1, keepdims=True), (SUB, LANES))
                 result = jnp.where(lane8 == g + half, result + column, result)
             return result
@@ -389,8 +388,13 @@
             for r in range(layers):
                 at = base + c * layers + r
                 ref[at:at + 1, :] = u[c, r, near:near + 1, :]
-                source, layer = (outer_s, r // top) if r in (0, top) else (inner_s, r - 1)
-                ref[at + tall:at + tall + 1, :] = source[c, layer, near:near + 1, :]
+                if r == 0:
+                    row = jnp.where(odd, face1[1, c, near:near + 1, :], face2[1, c, near:near + 1, :])
+                elif r == top:
+                    row = jnp.where(odd, face2[1, c, near:near + 1, :], face1[1, c, near:near + 1, :])
+                else:
+                    row = rims[c, r - 1, near // (rows - 1), near % SUB:near % SUB + 1, :]
+                ref[at + tall:at + tall + 1, :] = row
 
     pack(pay, SUB, 0)
     pack(pay, SUB + 2 * tall, rows - 1)
@@ -421,7 +425,7 @@
 
 
 def sweep_kernel(
-    u, f, outer_s, inner_s, face1, face2, ring, got, every,
+    u, f, own1, own2, inner_s, face1, face2, ring, got, every,
     out,
     s, rim, done, cf, out_sem,
 ):
@@ -522,7 +526,8 @@
                     elif layer == layers + 1:
                         value = hi((1, c) + at) + gain * u[(c, top) + at]
                     elif layer in (1, layers):
-                        value = outer_s[(c, layer // layers) + at]
+                        here1, here2 = own1[(1, c) + at], own2[(1, c) + at]
+                        value = jnp.where(rad_odd, here1, here2) if layer == 1 else jnp.where(rad_odd, here2, here1)
                     else:
                         value = inner_s[(c, layer - 2) + at]
                     if layer == 1:
@@ -601,7 +606,7 @@
                 spot = (slice(SUB * a, SUB * a + SUB), chunk(j))
                 cycle = ids[spot]
                 place, part = jnp.bitwise_and(cycle, LANES - 1), jnp.right_shift(cycle, 7)
-                values = [jnp.where(b == 0, 0.0, out[(k,) + spot]) for k in range(2)]
+                values = [zero if isinstance(b, int) else out[(k,) + spot] for k in range(2)]
                 for i in range(BATCH):
                     chosen = part == parts[i]
                     for k in range(2):
@@ -610,7 +615,8 @@
                     out[(k,) + spot] = values[k]
         return carry
 
-    lax.fori_loop(0, (high_part - low_part) // BATCH + 1, batch, 0)
+    batch(0, 0)
+    lax.fori_loop(1, (high_part - low_part) // BATCH + 1, batch, 0)
 
 
 def even_pairs(count):
@@ -646,11 +652,10 @@
             cycle_count.reshape(chunks, LANES), gravity, table,
         )
     ]
-    u, f, outer_s, face1, face2, mine, every, cyc, num = pl.pallas_call(
+    u, f, face1, face2, mine, every, cyc, num = pl.pallas_call(
         faces_kernel,
         out_shape=(
             whole, whole,
-            jax.ShapeDtypeStruct((3, 2, rows, width), f32),
             face, face,
             jax.ShapeDtypeStruct((COEFS, LANES), f32),
             jax.ShapeDtypeStruct((layers, COEFS, LANES), f32),
@@ -658,7 +663,7 @@
             jax.ShapeDtypeStruct((chunks, LANES), jnp.int32),
         ),
         in_specs=[HBM] * 7,
-        out_specs=(VMEM,) * 9,
+        out_specs=(VMEM,) * 8,
         scratch_shapes=[
             pltpu.SMEM(layer_id.shape, jnp.int32),
             pltpu.SMEM(stiffness.shape, f32),
@@ -667,7 +672,6 @@
             pltpu.SemaphoreType.DMA((2,)),
             pltpu.SemaphoreType.DMA((layers,)),
             pltpu.SemaphoreType.DMA((layers,)),
-            pltpu.SemaphoreType.DMA((4,)),
         ],
         compiler_params=pltpu.CompilerParams(vmem_limit_bytes=VMEM_LIMIT),
         name="faces",
@@ -676,28 +680,25 @@
     beside2 = lax.ppermute(face2, "rad", odd_pairs(rads)[:-2])
     beside1 = lax.ppermute(face1, "rad", even_pairs(rads))
 
-    inner_s, pay, gains = pl.pallas_call(
+    pay = pl.pallas_call(
         analysis_kernel,
-        out_shape=(
-            jax.ShapeDtypeStruct((3, layers - 2, rows, width), f32),
-            jax.ShapeDtypeStruct((SUB + 4 * tall, width), f32),
-            jax.ShapeDtypeStruct((2, SUB, LANES), f32),
-        ),
-        in_specs=[VMEM] * 6 + [HBM] * 3,
-        out_specs=(VMEM,) * 3,
+        out_shape=jax.ShapeDtypeStruct((SUB + 4 * tall, width), f32),
+        in_specs=[VMEM] * 7 + [HBM],
+        out_specs=VMEM,
         scratch_shapes=[
-            pltpu.VMEM((BATCH, degrees, LANES), f32),
+            pltpu.VMEM((rows, width), f32),
+            pltpu.VMEM((3, layers - 2, 2, SUB, width), f32),
+            pltpu.VMEM(table.shape, f32),
             pltpu.VMEM((2, COEFS, LANES), f32),
             pltpu.VMEM((2, rows // SUB + 1, SUB, LANES), f32),
-            pltpu.VMEM(gravity.shape, f32),
             pltpu.SMEM((SUB, LANES), jnp.int32),
             pltpu.SMEM((SUB, LANES), jnp.int32),
-            pltpu.SemaphoreType.DMA((3,)),
-            pltpu.SemaphoreType.DMA((BATCH,)),
+            pltpu.SemaphoreType.DMA((2,)),
+            pltpu.SemaphoreType.DMA((1,)),
         ],
         compiler_params=pltpu.CompilerParams(vmem_limit_bytes=VMEM_LIMIT),
         name="analysis",
-    )(u, f, outer_s, every, cyc, num, pinned[5], *pinned[7:])
+    )(u, f, face1, face2, every, cyc, num, pinned[8])
 
     chips = [[a * rads + b + c for a in range(lats) for c in range(cores)] for b in range(0, rads, cores)]
     ring = lax.all_gather(pay, ("lat", "rad"), axis_index_groups=chips)
@@ -711,10 +712,23 @@
     )(ring, mine)
     outward, beside1, beside2 = lax.optimization_barrier((outward, beside1, beside2))
     got = lax.ppermute(outward, "rad", odd_pairs(rads))
+    inner_s, gains = pl.pallas_call(
+        inner_kernel,
+        out_shape=(
+            jax.ShapeDtypeStruct((3, layers - 2, rows, width), f32),
+            jax.ShapeDtypeStruct((2, SUB, LANES), f32),
+        ),
+        in_specs=[VMEM] * 3 + [HBM],
+        out_specs=(VMEM,) * 2,
+        scratch_shapes=[pltpu.VMEM(gravity.shape, f32), pltpu.SemaphoreType.DMA((1,))],
+        compiler_params=pltpu.CompilerParams(vmem_limit_bytes=VMEM_LIMIT),
+        name="inner",
+    )(u, f, every, pinned[7])
+    got, inner_s = lax.optimization_barrier((got, inner_s))
     coef = outward[:SUB]
     if rads == 8:
         coef = coef + got[:SUB]
-        rest = lax.ppermute(coef, "rad", [(0, 3), (3, 0), (7, 4), (4, 7), (2, 5), (5, 2), (1, 6), (6, 1)])
+        rest = lax.ppermute(coef, "rad", [(0, 3), (3, 0), (7, 4), (4, 7), (1, 5), (5, 1), (2, 6), (6, 2)])
     else:
         coef = lax.psum(coef, "rad") * (1.0 / cores)
         rest = jnp.zeros_like(coef)
@@ -722,7 +736,7 @@
     smoothed = pl.pallas_call(
         sweep_kernel,
         out_shape=whole,
-        in_specs=[VMEM] * 9,
+        in_specs=[VMEM] * 10,
         out_specs=HBM,
         scratch_shapes=[
             pltpu.VMEM((3, layers + 2, rows, width), f32),
@@ -733,7 +747,7 @@
         ],
         compiler_params=pltpu.CompilerParams(vmem_limit_bytes=VMEM_LIMIT),
         name="sweeps",
-    )(u, f, outer_s, inner_s, beside1, beside2, ring, got, every)
+    )(u, f, face1, face2, inner_s, beside1, beside2, ring, got, every)
     coef, smoothed = lax.optimization_barrier((coef, smoothed))
 
     potential = pl.pallas_call(

time: 29.7 us -> 28.3 us (0.953)
  the two profiles are of different devices: /device:TPU:1 before, /device:TPU:0 now
where the time goes in v7:
time: 28.3 us; the launch traced here: 28.1 us
  blocking collectives  11.6 us (41%)
  Pallas kernels  9.12 us (32%)
  starting transfers between devices  4.81 us (17%)
  waiting for transfers between devices  1.88 us (7%)
  between operations  0.7 us (2%)
    all_gather x1, blocking collectives, local(): ring = lax.all_gather(pay, ('lat', 'rad'), axis_index_groups=chips)  11.6 us
    ppermute x1, starting transfers between devices, local(): got = lax.ppermute(outward, 'rad', odd_pairs(rads))  3.6 us
    pallas_call x1, Pallas kernels, local(): pl.pallas_call(analysis_kernel, out_shape=jax.ShapeDtypeStruct((SUB + 4 *...  2.42 us
    pallas_call x1, Pallas kernels, local(): pl.pallas_call(faces_kernel, out_shape=(whole, whole, face, face, jax.Sha...  2.1 us
    pallas_call x1, Pallas kernels, local(): pl.pallas_call(sweep_kernel, out_shape=whole, in_specs=[VMEM] * 10, out_s...  1.92 us
    pallas_call x1, Pallas kernels, local(): pl.pallas_call(functools.partial(synthesis_kernel, 2.0 / cycles), out_sha...  1.87 us
    ppermute x1, waiting for transfers between devices, local(): lax.ppermute(coef, 'rad', [(0, 3), (3, 0), (7, 4), (4, 7), (1, 5), (5, 1)...  1.1 us
    pallas_call x1, Pallas kernels, local(): pl.pallas_call(inner_kernel, out_shape=(jax.ShapeDtypeStruct((3, layers -...  0.79 us
  transfers between devices with their start and end apart: 4, of which 2 were waited for; matrix products, arithmetic and copies ran while one was open for 0% of the time, Pallas kernels for 18%

profile of v7, /device:TPU:0, one launch (start us, length us, event | category | flops | bytes accessed | tf_op | source)
XLA Modules:
  0.0 28.1 jit_solution(4549292842743101976)
XLA Ops:
  0.6 2.1 %faces.1 = (f32[3,4,64,384]{3,2,1,0:T(8,128)S(1)}, f32[3,4,64,384]{3,2,1,0:T(8,128)S(1)}, f32[2,3,64,384]{3,2,1,0:T(8,128)S(1)}, f32[2,3,64,384]{3,2,1,0:T(8,128...) custom-call(f32[3,4,64,384]{3,2,1,0:T(8,128)} %disp.1, ...), custom_call_target="tpu_custom_call" | custom-call | tf_op jit(solution)/shard_map/faces/pallas_call | solution.py:655
  2.7 0.5 %collective-permute-start = (f32[2,3,64,384]{3,2,1,0:T(8,128)S(1)}, f32[2,3,64,384]{3,2,1,0:T(8,128)S(1)}, u32[]{:S(2)}, u32[]{:S(2)}) collective-permute-start(f32[2,3,64,384]{3,2,1,0:T(8,128)S(1)} %get-tuple-element.21.face1.own1), channel_id=1, source_target_pairs={{0,1},{1,0},{2,3},{3,2},{4,5},{5,4},{6,7},{7,6},{8,9},{9,8},{10,11... | collective-permute-start | bytes 1769480 | tf_op jit(solution)/shard_map/ppermute | solution.py:681
  3.3 0.7 %collective-permute-start.1 = (f32[2,3,64,384]{3,2,1,0:T(8,128)S(1)}, f32[2,3,64,384]{3,2,1,0:T(8,128)S(1)}, u32[]{:S(2)}, u32[]{:S(2)}) collective-permute-start(f32[2,3,64,384]{3,2,1,0:T(8,128)S(1)} %get-tuple-element.22.face2.own2), channel_id=1, source_target_pairs={{1,2},{2,1},{3,4},{4,3},{5,6},{6,5},{9,10},{10,9},{11,12},{12,11},... | collective-permute-start | bytes 1769480 | tf_op jit(solution)/shard_map/ppermute | solution.py:680
  4.0 2.4 %analysis.1 = f32[56,384]{1,0:T(8,128)S(1)} custom-call(f32[3,4,64,384]{3,2,1,0:T(8,128)S(1)} %get-tuple-element.19.u, f32[3,4,64,384]{3,2,1,0:T(8,128)S(1)} %get-tuple-element.20.f, f32[2,3,64,384]{3,2,1,0:T(8,128)S(1)} %get-tuple-element.21.face1.own1, f32[2,3,64,384]{3,2,1,0:T(8,128)S(1)} %get-tuple-element.22.face2.own2, ...), custom_call_target="tpu_custom_call" | custom-call | tf_op jit(solution)/shard_map/analysis/pallas_call | solution.py:683
  6.4 11.6 %all-gather = f32[448,384]{1,0:T(8,128)S(1)} all-gather(f32[56,384]{1,0:T(8,128)S(1)} %analysis.1), channel_id=2, replica_groups={{0,1,8,9,16,17,24,25},{2,3,10,11,18,19,26,27},{4,5,12,13,20,21,28,29},{..., dimensions={0}, use_global_device_ids=true | all-gather | bytes 774144 | tf_op jit(solution)/shard_map/all_gather | solution.py:704
  18.0 0.0 collective-permute-done.face1
  18.0 0.0 collective-permute-done.1.face2
  18.0 3.6 %collective-permute-start.2 = (f32[48,128]{1,0:T(8,128)S(1)}, f32[48,128]{1,0:T(8,128)S(1)}, u32[]{:S(2)}, u32[]{:S(2)}) collective-permute-start(f32[48,128]{1,0:T(8,128)S(1)} %relay.1), channel_id=1, source_target_pairs={{1,2},{2,1},{3,4},{4,3},{5,6},{6,5},{7,0},{0,7},{9,10},{10,9},{11,... | collective-permute-start | bytes 73736 | tf_op jit(solution)/shard_map/ppermute | solution.py:714
  21.6 0.8 %inner.1 = (f32[3,2,64,384]{3,2,1,0:T(8,128)S(1)}, f32[2,8,128]{2,1,0:T(8,128)S(1)}) custom-call(f32[3,4,64,384]{3,2,1,0:T(8,128)S(1)} %get-tuple-element.19.u, f32[3,4,64,384]{3,2,1,0:T(8,128)S(1)} %get-tuple-element.20.f, f32[4,16,128]{2,1,0:T(8,128)S(1)} %get-tuple-element.23.every, f32[2,2,512]{2,1,0:T(2,128)} %grav.1), custom_call_target="tpu_custom_call" | custom-call | tf_op jit(solution)/shard_map/inner/pallas_call | solution.py:715
  22.4 0.8 %collective-permute-done.2.got = f32[48,128]{1,0:T(8,128)S(1)} collective-permute-done((f32[48,128]{1,0:T(8,128)S(1)}, f32[48,128]{1,0:T(8,128)S(1)}, u32[]{:S(2)}, u32[]{:S(2)}) %collective-permute-start.2) | collective-permute-done | bytes 24608 | tf_op jit(solution)/shard_map/ppermute | solution.py:714
  23.2 0.0 collective-permute-start.3
  23.2 0.0 copy-start
  23.2 1.9 %sweeps.1 = f32[3,4,64,384]{3,2,1,0:T(8,128)} custom-call(f32[3,4,64,384]{3,2,1,0:T(8,128)S(1)} %get-tuple-element.19.u, f32[3,4,64,384]{3,2,1,0:T(8,128)S(1)} %get-tuple-element.20.f, f32[2,3,64,384]{3,2,1,0:T(8,128)S(1)} %get-tuple-element.21.face1.own1, f32[2,3,64,384]{3,2,1,0:T(8,128)S(1)} %get-tuple-element.22.face2.own2, ...), custom_call_target="tpu_custom_call" | custom-call | tf_op jit(solution)/shard_map/sweeps/pallas_call | solution.py:736
  25.1 1.1 %collective-permute-done.3.rest = f32[8,128]{1,0:T(8,128)S(1)} collective-permute-done((f32[8,128]{1,0:T(8,128)S(1)}, f32[8,128]{1,0:T(8,128)S(1)}, u32[]{:S(2)}, u32[]{:S(2)}) %collective-permute-start.3) | collective-permute-done | bytes 4128 | tf_op jit(solution)/shard_map/ppermute | solution.py:731
  26.2 0.0 copy-done
  26.2 1.9 %synthesis.1 = f32[2,64,384]{2,1,0:T(8,128)} custom-call(f32[8,128]{1,0:T(8,128)S(1)} %slice_add_fusion.coef, f32[8,128]{1,0:T(8,128)S(1)} %collective-permute-done.3.rest, f32[2,8,128]{2,1,0:T(8,128)S(1)} %get-tuple-element.35.gains, s32[64,384]{1,0:T(8,128)S(1)} %get-tuple-element.24.cyc.ids, f32[12,512,128]{2,1,0:T(8,128)S(1)} %copy-done), custom_call_target="tpu_custom_call" | custom-call | tf_op jit(solution)/shard_map/synthesis/pallas_call | solution.py:753
  (2 shorter events, 0.0 us)
Async XLA Ops:
  2.7 15.2 %collective-permute-start = (f32[2,3,64,384]{3,2,1,0:T(8,128)S(1)}, f32[2,3,64,384]{3,2,1,0:T(8,128)S(1)}, u32[]{:S(2)}, u32[]{:S(2)}) collective-permute-start(f32[2,3,64,384]{3,2,1,0:T(8,128)S(1)} %get-tuple-element.21.face1.own1), channel_id=1, source_target_pairs={{0,1},{1,0},{2,3},{3,2},{4,5},{5,4},{6,7},{7,6},{8,9},{9,8},{10,11... | collective-permute-start | bytes 1769480 | tf_op jit(solution)/shard_map/ppermute | solution.py:681
  3.3 14.7 %collective-permute-start.1 = (f32[2,3,64,384]{3,2,1,0:T(8,128)S(1)}, f32[2,3,64,384]{3,2,1,0:T(8,128)S(1)}, u32[]{:S(2)}, u32[]{:S(2)}) collective-permute-start(f32[2,3,64,384]{3,2,1,0:T(8,128)S(1)} %get-tuple-element.22.face2.own2), channel_id=1, source_target_pairs={{1,2},{2,1},{3,4},{4,3},{5,6},{6,5},{9,10},{10,9},{11,12},{12,11},... | collective-permute-start | bytes 1769480 | tf_op jit(solution)/shard_map/ppermute | solution.py:680
  18.0 5.2 %collective-permute-start.2 = (f32[48,128]{1,0:T(8,128)S(1)}, f32[48,128]{1,0:T(8,128)S(1)}, u32[]{:S(2)}, u32[]{:S(2)}) collective-permute-start(f32[48,128]{1,0:T(8,128)S(1)} %relay.1), channel_id=1, source_target_pairs={{1,2},{2,1},{3,4},{4,3},{5,6},{6,5},{7,0},{0,7},{9,10},{10,9},{11,... | collective-permute-start | bytes 73736 | tf_op jit(solution)/shard_map/ppermute | solution.py:714
  23.2 3.0 %collective-permute-start.3 = (f32[8,128]{1,0:T(8,128)S(1)}, f32[8,128]{1,0:T(8,128)S(1)}, u32[]{:S(2)}, u32[]{:S(2)}) collective-permute-start(f32[8,128]{1,0:T(8,128)S(1)} %slice_add_fusion.coef), channel_id=1, source_target_pairs={{0,3},{3,0},{7,4},{4,7},{1,5},{5,1},{2,6},{6,2},{8,11},{11,8},{15,... | collective-permute-start | bytes 12296 | tf_op jit(solution)/shard_map/ppermute | solution.py:731
  23.2 3.0 %copy-start = (f32[12,512,128]{2,1,0:T(8,128)S(1)}, f32[12,512,128]{2,1,0:T(8,128)}, u32[]{:S(2)}) copy-start(f32[12,512,128]{2,1,0:T(8,128)} %constant.2.clone.tbl.tab) | copy-start | bytes 9437188

commit v8 on v7

--- a/solution.py
+++ b/solution.py
@@ -128,8 +128,8 @@
 
 
 def faces_kernel(
-    disp, forc, lid, stiff, coup, ids, cnt,
-    u, f, face1, face2, send, every, cyc, num,
+    disp, forc, lid, stiff, coup, ids, cnt, grav,
+    u, f, face1, face2, send, every, cyc, num, gain_in,
     lids, stiffs, coups, small_sem, near_sem, u_sem, f_sem,
 ):
     layers = disp.shape[1]
@@ -143,6 +143,7 @@
     cycles = [
         pltpu.make_async_copy(cnt, num, near_sem.at[0]),
         pltpu.make_async_copy(ids, cyc, near_sem.at[1]),
+        pltpu.make_async_copy(grav, gain_in, near_sem.at[2]),
     ]
     loads_u = [pltpu.make_async_copy(disp.at[:, r], u.at[:, r], u_sem.at[r]) for r in range(layers)]
     loads_f = [pltpu.make_async_copy(forc.at[:, r], f.at[:, r], f_sem.at[r]) for r in range(layers)]
@@ -175,10 +176,8 @@
         copy.wait()
 
 
-def inner_kernel(u, f, every, grav, inner_s, gains, gain_in, gain_sem):
+def inner_kernel(u, f, every, gain_in, inner_s, gains):
     groups = gain_in.shape[2] // SUB
-    load_gains = pltpu.make_async_copy(grav, gain_in, gain_sem.at[0])
-    load_gains.start()
 
     def middle(r, carry):
         def store(c, g, j, value, swept):
@@ -188,7 +187,6 @@
         return carry
 
     lax.fori_loop(1, u.shape[1] - 1, middle, 0)
-    load_gains.wait()
 
     lane1 = iota((1, LANES), 1)
     for load in range(2):
@@ -201,7 +199,7 @@
 def analysis_kernel(
     u, f, face1, face2, every, cyc, num, tbl,
     pay,
-    plane, rims, tab, mat, windows, first_ids, last_ids, near_sem, tab_sem,
+    plane, rims, tab, mat, windows, tab_sem,
 ):
     layers, rows, width = u.shape[1:]
     chunks = num.shape[0]
@@ -216,18 +214,22 @@
     total = rows // SUB
     odd = lax.rem(rad, 2) == 1
     at_core = every[jnp.where(odd, 0, top)]
-    cycles = [
-        pltpu.make_async_copy(cyc.at[pl.ds(0, SUB), pl.ds(0, LANES)], first_ids, near_sem.at[0]),
-        pltpu.make_async_copy(
-            cyc.at[pl.ds(rows - SUB, SUB), pl.ds(width - LANES, LANES)], last_ids, near_sem.at[1]
-        ),
-    ]
-
-    table = pltpu.make_async_copy(tbl, tab, tab_sem.at[0])
+    reach = 2 * width // LEAST_COUNT + 2
+    low_part = jnp.right_shift(jnp.maximum(jnp.min(cyc[0:1, 0:LANES]) - reach, 0), 7)
+    high_part = jnp.right_shift(jnp.max(cyc[rows - 1:rows, width - LANES:width]) + reach, 7)
+    high_part = jnp.minimum(high_part, chunks - 1)
+
+    def table(b):
+        return [
+            pltpu.make_async_copy(
+                tbl.at[jnp.minimum(low_part + b * BATCH + i, chunks - 1)], tab.at[i], tab_sem.at[i]
+            )
+            for i in range(BATCH)
+        ]
 
     @pl.when(at_end)
     def _():
-        for copy in cycles + [table]:
+        for copy in table(0):
             copy.start()
 
     for r in range(1, top):
@@ -239,7 +241,6 @@
     sub8, lane8 = iota((SUB, LANES), 0), iota((SUB, LANES), 1)
     before = sub8 < 2
     zero = jnp.zeros((SUB, LANES), jnp.float32)
-    reach = 2 * width // LEAST_COUNT + 2
     pay[0:SUB, 0:LANES] = jnp.zeros((SUB, LANES), jnp.float32)
     pay[0:SUB, LANES:2 * LANES] = at_core[0:SUB]
     pay[0:SUB, 2 * LANES:3 * LANES] = at_core[SUB:]
@@ -349,20 +350,19 @@
             windows[0, i] = window
             windows[1, i] = start.astype(jnp.float32)
 
-        for copy in cycles:
-            copy.wait()
-        low_part = jnp.right_shift(jnp.maximum(first_ids[0, 0] - reach, 0), 7)
-        high_part = jnp.minimum(jnp.right_shift(last_ids[SUB - 1, LANES - 1] + reach, 7), chunks - 1)
         half = jnp.where(bottom, groups, 0)
 
-        table.wait()
 
         def batch(b, result):
-            means, blocks = [], []
+            @pl.when(b > 0)
+            def _():
+                for copy in table(b):
+                    copy.start()
+
+            means = []
             for i in range(BATCH):
                 q = low_part + b * BATCH + i
                 part = jnp.minimum(q, chunks - 1)
-                blocks.append(part)
                 acc = zero
                 for w in range(total + 1):
                     at = q * LANES + lane8 - windows[1, w].astype(jnp.int32)
@@ -371,10 +371,12 @@
                 mean = jnp.sum(acc, axis=0, keepdims=True) / num[pl.ds(part, 1), :].astype(jnp.float32)
                 mean = jnp.where(q < chunks, mean, 0.0)
                 means.append(jnp.broadcast_to(mean, (SUB, LANES)))
+            for copy in table(b):
+                copy.wait()
             for g in range(groups):
-                acc = tab[blocks[0], SUB * g:SUB * g + SUB, :] * means[0]
+                acc = tab[0, SUB * g:SUB * g + SUB, :] * means[0]
                 for i in range(1, BATCH):
-                    acc = acc + tab[blocks[i], SUB * g:SUB * g + SUB, :] * means[i]
+                    acc = acc + tab[i, SUB * g:SUB * g + SUB, :] * means[i]
                 column = jnp.broadcast_to(jnp.sum(acc, axis=1, keepdims=True), (SUB, LANES))
                 result = jnp.where(lane8 == g + half, result + column, result)
             return result
@@ -571,13 +573,13 @@
         copy.wait()
 
 
-def synthesis_kernel(scale, coef, rest, gains, ids, tab, out, factors):
+def synthesis_kernel(scale, coef, rest, near, far, gains, ids, tab, out, factors):
     rows, width = ids.shape
     chunks = tab.shape[0]
     groups = tab.shape[1] // SUB
     per_row = width // LANES
     lane8 = iota((SUB, LANES), 1)
-    here = coef[...] + rest[...]
+    here = (coef[...] + rest[...]) + (near[...] + far[...])
     other = pltpu.roll(here, groups, 1)
     left = lane8 < groups
     surface = jnp.where(left, here, other)
@@ -652,7 +654,7 @@
             cycle_count.reshape(chunks, LANES), gravity, table,
         )
     ]
-    u, f, face1, face2, mine, every, cyc, num = pl.pallas_call(
+    u, f, face1, face2, mine, every, cyc, num, gain_in = pl.pallas_call(
         faces_kernel,
         out_shape=(
             whole, whole,
@@ -661,21 +663,22 @@
             jax.ShapeDtypeStruct((layers, COEFS, LANES), f32),
             jax.ShapeDtypeStruct(cycle_id.shape, jnp.int32),
             jax.ShapeDtypeStruct((chunks, LANES), jnp.int32),
+            jax.ShapeDtypeStruct(gravity.shape, f32),
         ),
-        in_specs=[HBM] * 7,
-        out_specs=(VMEM,) * 8,
+        in_specs=[HBM] * 8,
+        out_specs=(VMEM,) * 9,
         scratch_shapes=[
             pltpu.SMEM(layer_id.shape, jnp.int32),
             pltpu.SMEM(stiffness.shape, f32),
             pltpu.SMEM(coupling.shape[1:] + coupling.shape[:1], f32),
             pltpu.SemaphoreType.DMA((3,)),
-            pltpu.SemaphoreType.DMA((2,)),
+            pltpu.SemaphoreType.DMA((3,)),
             pltpu.SemaphoreType.DMA((layers,)),
             pltpu.SemaphoreType.DMA((layers,)),
         ],
         compiler_params=pltpu.CompilerParams(vmem_limit_bytes=VMEM_LIMIT),
         name="faces",
-    )(*pinned[:7])
+    )(*pinned[:8])
 
     beside2 = lax.ppermute(face2, "rad", odd_pairs(rads)[:-2])
     beside1 = lax.ppermute(face1, "rad", even_pairs(rads))
@@ -688,13 +691,10 @@
         scratch_shapes=[
             pltpu.VMEM((rows, width), f32),
             pltpu.VMEM((3, layers - 2, 2, SUB, width), f32),
-            pltpu.VMEM(table.shape, f32),
+            pltpu.VMEM((BATCH, degrees, LANES), f32),
             pltpu.VMEM((2, COEFS, LANES), f32),
             pltpu.VMEM((2, rows // SUB + 1, SUB, LANES), f32),
-            pltpu.SMEM((SUB, LANES), jnp.int32),
-            pltpu.SMEM((SUB, LANES), jnp.int32),
-            pltpu.SemaphoreType.DMA((2,)),
-            pltpu.SemaphoreType.DMA((1,)),
+            pltpu.SemaphoreType.DMA((BATCH,)),
         ],
         compiler_params=pltpu.CompilerParams(vmem_limit_bytes=VMEM_LIMIT),
         name="analysis",
@@ -718,20 +718,20 @@
             jax.ShapeDtypeStruct((3, layers - 2, rows, width), f32),
             jax.ShapeDtypeStruct((2, SUB, LANES), f32),
         ),
-        in_specs=[VMEM] * 3 + [HBM],
+        in_specs=[VMEM] * 4,
         out_specs=(VMEM,) * 2,
-        scratch_shapes=[pltpu.VMEM(gravity.shape, f32), pltpu.SemaphoreType.DMA((1,))],
         compiler_params=pltpu.CompilerParams(vmem_limit_bytes=VMEM_LIMIT),
         name="inner",
-    )(u, f, every, pinned[7])
+    )(u, f, every, gain_in)
     got, inner_s = lax.optimization_barrier((got, inner_s))
     coef = outward[:SUB]
     if rads == 8:
-        coef = coef + got[:SUB]
-        rest = lax.ppermute(coef, "rad", [(0, 3), (3, 0), (7, 4), (4, 7), (1, 5), (5, 1), (2, 6), (6, 2)])
+        near = lax.ppermute(coef, "rad", [(0, 3), (3, 0), (7, 4), (4, 7), (1, 5), (5, 1), (2, 6), (6, 2)])
+        far = lax.ppermute(coef, "rad", [(0, 4), (4, 0), (7, 3), (3, 7), (1, 6), (6, 1), (2, 5), (5, 2)])
+        rest = got[:SUB]
     else:
         coef = lax.psum(coef, "rad") * (1.0 / cores)
-        rest = jnp.zeros_like(coef)
+        near = far = rest = jnp.zeros_like(coef)
 
     smoothed = pl.pallas_call(
         sweep_kernel,
@@ -753,12 +753,12 @@
     potential = pl.pallas_call(
         functools.partial(synthesis_kernel, 2.0 / cycles),
         out_shape=jax.ShapeDtypeStruct((2, rows, width), f32),
-        in_specs=[VMEM] * 5,
+        in_specs=[VMEM] * 7,
         out_specs=VMEM,
         scratch_shapes=[pltpu.VMEM((2 * groups, SUB, LANES), f32)],
         compiler_params=pltpu.CompilerParams(vmem_limit_bytes=VMEM_LIMIT),
         name="synthesis",
-    )(coef, rest, gains, cyc, table)
+    )(coef, rest, near, far, gains, cyc, table)
     return smoothed, potential
 
 

time: 28.3 us -> 27.9 us (0.986)
  the two profiles are of different devices: /device:TPU:0 before, /device:TPU:1 now
where the time goes in v8:
time: 27.9 us; the launch traced here: 27.7 us
  blocking collectives  10.2 us (37%)
  starting transfers between devices  8.85 us (32%)
  Pallas kernels  6.88 us (25%)
  waiting for transfers between devices  1.06 us (4%)
  between operations  0.73 us (3%)
    all_gather x1, blocking collectives, local(): ring = lax.all_gather(pay, ('lat', 'rad'), axis_index_groups=chips)  10.2 us
    ppermute x1, starting transfers between devices, local(): beside2 = lax.ppermute(face2, 'rad', odd_pairs(rads)[:-2])  4.55 us
    pallas_call x1, Pallas kernels, local(): pl.pallas_call(faces_kernel, out_shape=(whole, whole, face, face, jax.Sha...  2.14 us
    pallas_call x1, Pallas kernels, local(): pl.pallas_call(sweep_kernel, out_shape=whole, in_specs=[VMEM] * 10, out_s...  1.93 us
    pallas_call x1, Pallas kernels, local(): pl.pallas_call(functools.partial(synthesis_kernel, 2.0 / cycles), out_sha...  1.87 us
    ppermute x1, starting transfers between devices, local(): lax.ppermute(coef, 'rad', [(0, 3), (3, 0), (7, 4), (4, 7), (1, 5), (5, 1)...  1.53 us
    ppermute x1, starting transfers between devices, local(): got = lax.ppermute(outward, 'rad', odd_pairs(rads))  1.45 us
    ppermute x1, starting transfers between devices, local(): lax.ppermute(coef, 'rad', [(0, 4), (4, 0), (7, 3), (3, 7), (1, 6), (6, 1)...  1.19 us
  transfers between devices with their start and end apart: 5, of which 1 were waited for; matrix products, arithmetic and copies ran while one was open for 0% of the time, Pallas kernels for 10%

profile of v8, /device:TPU:1, one launch (start us, length us, event | category | flops | bytes accessed | tf_op | source)
XLA Modules:
  0.0 27.7 jit_solution(14193543333235681787)
XLA Ops:
  0.6 2.1 %faces.1 = (f32[3,4,64,384]{3,2,1,0:T(8,128)S(1)}, f32[3,4,64,384]{3,2,1,0:T(8,128)S(1)}, f32[2,3,64,384]{3,2,1,0:T(8,128)S(1)}, f32[2,3,64,384]{3,2,1,0:T(8,128...) custom-call(f32[3,4,64,384]{3,2,1,0:T(8,128)} %disp.1, ...), custom_call_target="tpu_custom_call" | custom-call | tf_op jit(solution)/shard_map/faces/pallas_call | solution.py:657
  2.8 0.1 collective-permute-start
  2.9 4.6 %collective-permute-start.1 = (f32[2,3,64,384]{3,2,1,0:T(8,128)S(1)}, f32[2,3,64,384]{3,2,1,0:T(8,128)S(1)}, u32[]{:S(2)}, u32[]{:S(2)}) collective-permute-start(f32[2,3,64,384]{3,2,1,0:T(8,128)S(1)} %get-tuple-element.23.face2.own2), channel_id=1, source_target_pairs={{1,2},{2,1},{3,4},{4,3},{5,6},{6,5},{9,10},{10,9},{11,12},{12,11},... | collective-permute-start | bytes 1769480 | tf_op jit(solution)/shard_map/ppermute | solution.py:683
  7.5 0.3 %analysis.1 = f32[56,384]{1,0:T(8,128)S(1)} custom-call(f32[3,4,64,384]{3,2,1,0:T(8,128)S(1)} %get-tuple-element.20.u, f32[3,4,64,384]{3,2,1,0:T(8,128)S(1)} %get-tuple-element.21.f, f32[2,3,64,384]{3,2,1,0:T(8,128)S(1)} %get-tuple-element.22.face1.own1, f32[2,3,64,384]{3,2,1,0:T(8,128)S(1)} %get-tuple-element.23.face2.own2, ...), custom_call_target="tpu_custom_call" | custom-call | tf_op jit(solution)/shard_map/analysis/pallas_call | solution.py:686
  7.8 10.2 %all-gather = f32[448,384]{1,0:T(8,128)S(1)} all-gather(f32[56,384]{1,0:T(8,128)S(1)} %analysis.1), channel_id=2, replica_groups={{0,1,8,9,16,17,24,25},{2,3,10,11,18,19,26,27},{4,5,12,13,20,21,28,29},{..., dimensions={0}, use_global_device_ids=true | all-gather | bytes 774144 | tf_op jit(solution)/shard_map/all_gather | solution.py:704
  18.0 0.0 collective-permute-done.face1
  18.0 0.0 collective-permute-done.1.face2
  18.0 1.4 %collective-permute-start.2 = (f32[48,128]{1,0:T(8,128)S(1)}, f32[48,128]{1,0:T(8,128)S(1)}, u32[]{:S(2)}, u32[]{:S(2)}) collective-permute-start(f32[48,128]{1,0:T(8,128)S(1)} %relay.1), channel_id=1, source_target_pairs={{1,2},{2,1},{3,4},{4,3},{5,6},{6,5},{7,0},{0,7},{9,10},{10,9},{11,... | collective-permute-start | bytes 73736 | tf_op jit(solution)/shard_map/ppermute | solution.py:714
  19.5 1.5 %collective-permute-start.3 = (f32[8,128]{1,0:T(8,128)S(1)}, f32[8,128]{1,0:T(8,128)S(1)}, u32[]{:S(2)}, u32[]{:S(2)}) collective-permute-start(f32[8,128]{1,0:T(8,128)S(1)} %slice.6.coef), channel_id=1, source_target_pairs={{0,3},{3,0},{7,4},{4,7},{1,5},{5,1},{2,6},{6,2},{8,11},{11,8},{15,... | collective-permute-start | bytes 12296 | tf_op jit(solution)/shard_map/ppermute | solution.py:729
  21.0 1.2 %collective-permute-start.4 = (f32[8,128]{1,0:T(8,128)S(1)}, f32[8,128]{1,0:T(8,128)S(1)}, u32[]{:S(2)}, u32[]{:S(2)}) collective-permute-start(f32[8,128]{1,0:T(8,128)S(1)} %slice.6.coef), channel_id=1, source_target_pairs={{0,4},{4,0},{7,3},{3,7},{1,6},{6,1},{2,5},{5,2},{8,12},{12,8},{15,... | collective-permute-start | bytes 12296 | tf_op jit(solution)/shard_map/ppermute | solution.py:730
  22.2 0.6 %inner.1 = (f32[3,2,64,384]{3,2,1,0:T(8,128)S(1)}, f32[2,8,128]{2,1,0:T(8,128)S(1)}) custom-call(f32[3,4,64,384]{3,2,1,0:T(8,128)S(1)} %get-tuple-element.20.u, f32[3,4,64,384]{3,2,1,0:T(8,128)S(1)} %get-tuple-element.21.f, f32[4,16,128]{2,1,0:T(8,128)S(1)} %get-tuple-element.24.every, f32[2,2,512]{2,1,0:T(2,128)S(1)} %get-tuple-element.29.gain_in), custom_call_target="tpu_custom_call" | custom-call | tf_op jit(solution)/shard_map/inner/pallas_call | solution.py:715
  22.8 0.0 collective-permute-done.2.got
  22.8 0.0 copy-start
  22.9 1.9 %sweeps.1 = f32[3,4,64,384]{3,2,1,0:T(8,128)} custom-call(f32[3,4,64,384]{3,2,1,0:T(8,128)S(1)} %get-tuple-element.20.u, f32[3,4,64,384]{3,2,1,0:T(8,128)S(1)} %get-tuple-element.21.f, f32[2,3,64,384]{3,2,1,0:T(8,128)S(1)} %get-tuple-element.22.face1.own1, f32[2,3,64,384]{3,2,1,0:T(8,128)S(1)} %get-tuple-element.23.face2.own2, ...), custom_call_target="tpu_custom_call" | custom-call | tf_op jit(solution)/shard_map/sweeps/pallas_call | solution.py:736
  24.8 0.0 collective-permute-done.3.near
  24.8 1.0 %collective-permute-done.4.far = f32[8,128]{1,0:T(8,128)S(1)} collective-permute-done((f32[8,128]{1,0:T(8,128)S(1)}, f32[8,128]{1,0:T(8,128)S(1)}, u32[]{:S(2)}, u32[]{:S(2)}) %collective-permute-start.4) | collective-permute-done | bytes 4128 | tf_op jit(solution)/shard_map/ppermute | solution.py:730
  25.9 0.0 copy-done
  25.9 1.9 %synthesis.1 = f32[2,64,384]{2,1,0:T(8,128)} custom-call(f32[8,128]{1,0:T(8,128)S(1)} %slice.6.coef, f32[8,128]{1,0:T(8,128)S(1)} %slice.7.rest, f32[8,128]{1,0:T(8,128)S(1)} %collective-permute-done.3.near, f32[8,128]{1,0:T(8,128)S(1)} %collective-permute-done.4.far, f32[2,8,128]{2,1,0:T(8,128)S(1)} %get-tuple-element.37.gains, ...), custom_call_target="tpu_custom_call" | custom-call | tf_op jit(solution)/shard_map/synthesis/pallas_call | solution.py:753
  (3 shorter events, 0.0 us)
Async XLA Ops:
  2.8 15.2 %collective-permute-start = (f32[2,3,64,384]{3,2,1,0:T(8,128)S(1)}, f32[2,3,64,384]{3,2,1,0:T(8,128)S(1)}, u32[]{:S(2)}, u32[]{:S(2)}) collective-permute-start(f32[2,3,64,384]{3,2,1,0:T(8,128)S(1)} %get-tuple-element.22.face1.own1), channel_id=1, source_target_pairs={{0,1},{1,0},{2,3},{3,2},{4,5},{5,4},{6,7},{7,6},{8,9},{9,8},{10,11... | collective-permute-start | bytes 1769480 | tf_op jit(solution)/shard_map/ppermute | solution.py:684
  2.9 15.1 %collective-permute-start.1 = (f32[2,3,64,384]{3,2,1,0:T(8,128)S(1)}, f32[2,3,64,384]{3,2,1,0:T(8,128)S(1)}, u32[]{:S(2)}, u32[]{:S(2)}) collective-permute-start(f32[2,3,64,384]{3,2,1,0:T(8,128)S(1)} %get-tuple-element.23.face2.own2), channel_id=1, source_target_pairs={{1,2},{2,1},{3,4},{4,3},{5,6},{6,5},{9,10},{10,9},{11,12},{12,11},... | collective-permute-start | bytes 1769480 | tf_op jit(solution)/shard_map/ppermute | solution.py:683
  18.0 4.8 %collective-permute-start.2 = (f32[48,128]{1,0:T(8,128)S(1)}, f32[48,128]{1,0:T(8,128)S(1)}, u32[]{:S(2)}, u32[]{:S(2)}) collective-permute-start(f32[48,128]{1,0:T(8,128)S(1)} %relay.1), channel_id=1, source_target_pairs={{1,2},{2,1},{3,4},{4,3},{5,6},{6,5},{7,0},{0,7},{9,10},{10,9},{11,... | collective-permute-start | bytes 73736 | tf_op jit(solution)/shard_map/ppermute | solution.py:714
  19.5 5.3 %collective-permute-start.3 = (f32[8,128]{1,0:T(8,128)S(1)}, f32[8,128]{1,0:T(8,128)S(1)}, u32[]{:S(2)}, u32[]{:S(2)}) collective-permute-start(f32[8,128]{1,0:T(8,128)S(1)} %slice.6.coef), channel_id=1, source_target_pairs={{0,3},{3,0},{7,4},{4,7},{1,5},{5,1},{2,6},{6,2},{8,11},{11,8},{15,... | collective-permute-start | bytes 12296 | tf_op jit(solution)/shard_map/ppermute | solution.py:729
  21.0 4.8 %collective-permute-start.4 = (f32[8,128]{1,0:T(8,128)S(1)}, f32[8,128]{1,0:T(8,128)S(1)}, u32[]{:S(2)}, u32[]{:S(2)}) collective-permute-start(f32[8,128]{1,0:T(8,128)S(1)} %slice.6.coef), channel_id=1, source_target_pairs={{0,4},{4,0},{7,3},{3,7},{1,6},{6,1},{2,5},{5,2},{8,12},{12,8},{15,... | collective-permute-start | bytes 12296 | tf_op jit(solution)/shard_map/ppermute | solution.py:730
  22.8 3.0 %copy-start = (f32[12,512,128]{2,1,0:T(8,128)S(1)}, f32[12,512,128]{2,1,0:T(8,128)}, u32[]{:S(2)}) copy-start(f32[12,512,128]{2,1,0:T(8,128)} %constant.2.clone.tbl.tab) | copy-start | bytes 9437188

commit v9 on v8

--- a/solution.py
+++ b/solution.py
@@ -402,6 +402,10 @@
     pack(pay, SUB + 2 * tall, rows - 1)
 
 
+def first_chunk(cyc):
+    return jnp.right_shift(jnp.min(cyc[0:1, 0:LANES]), 7)
+
+
 def relay_kernel(ring, send, out):
     cores = 2
     lat, lats = lax.axis_index("lat"), lax.axis_size("lat")
@@ -427,12 +431,19 @@
 
 
 def sweep_kernel(
-    u, f, own1, own2, inner_s, face1, face2, ring, got, every,
-    out,
-    s, rim, done, cf, out_sem,
+    u, f, own1, own2, inner_s, face1, face2, ring, got, every, cyc, tbl,
+    out, tab,
+    s, rim, done, cf, out_sem, tab_sem,
 ):
     layers, rows, width = u.shape[1:]
     per_row = width // LANES
+    first = first_chunk(cyc)
+    table = [
+        pltpu.make_async_copy(tbl.at[jnp.minimum(first + i, tbl.shape[0] - 1)], tab.at[i], tab_sem.at[i])
+        for i in range(BATCH)
+    ]
+    for copy in table:
+        copy.start()
     total = rows // SUB
     tall = 3 * layers
     top = layers - 1
@@ -569,13 +580,13 @@
                         c, [values[d][j] for d in range(3)], near, f[c, r, here, chunk(j)], coef
                     )
         stores[r].start()
-    for copy in stores:
+    for copy in stores + table:
         copy.wait()
 
 
-def synthesis_kernel(scale, coef, rest, near, far, gains, ids, tab, out, factors):
+def synthesis_kernel(scale, coef, rest, near, far, gains, ids, tab, tbl, out, factors, more, more_sem):
     rows, width = ids.shape
-    chunks = tab.shape[0]
+    chunks = tbl.shape[0]
     groups = tab.shape[1] // SUB
     per_row = width // LANES
     lane8 = iota((SUB, LANES), 1)
@@ -588,16 +599,26 @@
     zero = jnp.zeros((SUB, LANES), jnp.float32)
     for i in range(2 * groups):
         factors[i] = jnp.broadcast_to(modes[:, i:i + 1], (SUB, LANES))
-    low_part = jnp.right_shift(jnp.min(ids[0:1, 0:LANES]), 7)
+    low_part = first_chunk(ids)
     high_part = jnp.right_shift(jnp.max(ids[rows - 1:rows, width - LANES:width]), 7)
 
     def batch(b, carry):
         parts = [low_part + b * BATCH + i for i in range(BATCH)]
-        blocks = [jnp.minimum(part, chunks - 1) for part in parts]
+        source = tab
+        if not isinstance(b, int):
+            source = more
+            copies = [
+                pltpu.make_async_copy(tbl.at[jnp.minimum(part, chunks - 1)], more.at[i], more_sem.at[i])
+                for i, part in enumerate(parts)
+            ]
+            for copy in copies:
+                copy.start()
+            for copy in copies:
+                copy.wait()
         sums = [[zero] * BATCH for _ in range(2)]
         for g in range(groups):
             for i in range(BATCH):
-                block = tab[blocks[i], SUB * g:SUB * g + SUB, :]
+                block = source[i, SUB * g:SUB * g + SUB, :]
                 for k in range(2):
                     sums[k][i] = sums[k][i] + factors[k * groups + g] * block
         for k in range(2):
@@ -726,39 +747,43 @@
     got, inner_s = lax.optimization_barrier((got, inner_s))
     coef = outward[:SUB]
     if rads == 8:
+        far = lax.ppermute(coef, "rad", [(0, 4), (4, 0), (7, 3), (3, 7), (1, 6), (6, 1), (2, 5), (5, 2)])
         near = lax.ppermute(coef, "rad", [(0, 3), (3, 0), (7, 4), (4, 7), (1, 5), (5, 1), (2, 6), (6, 2)])
-        far = lax.ppermute(coef, "rad", [(0, 4), (4, 0), (7, 3), (3, 7), (1, 6), (6, 1), (2, 5), (5, 2)])
         rest = got[:SUB]
     else:
         coef = lax.psum(coef, "rad") * (1.0 / cores)
         near = far = rest = jnp.zeros_like(coef)
 
-    smoothed = pl.pallas_call(
+    smoothed, tab = pl.pallas_call(
         sweep_kernel,
-        out_shape=whole,
-        in_specs=[VMEM] * 10,
-        out_specs=HBM,
+        out_shape=(whole, jax.ShapeDtypeStruct((BATCH, degrees, LANES), f32)),
+        in_specs=[VMEM] * 11 + [HBM],
+        out_specs=(HBM, VMEM),
         scratch_shapes=[
             pltpu.VMEM((3, layers + 2, rows, width), f32),
             pltpu.VMEM((2 * layers, 3, SUB, width), f32),
             pltpu.VMEM((3, layers, rows, width), f32),
             pltpu.VMEM((layers + 2, COEFS, LANES), f32),
             pltpu.SemaphoreType.DMA((layers,)),
+            pltpu.SemaphoreType.DMA((BATCH,)),
         ],
         compiler_params=pltpu.CompilerParams(vmem_limit_bytes=VMEM_LIMIT),
         name="sweeps",
-    )(u, f, face1, face2, inner_s, beside1, beside2, ring, got, every)
-    coef, smoothed = lax.optimization_barrier((coef, smoothed))
+    )(u, f, face1, face2, inner_s, beside1, beside2, ring, got, every, cyc, pinned[8])
 
     potential = pl.pallas_call(
         functools.partial(synthesis_kernel, 2.0 / cycles),
         out_shape=jax.ShapeDtypeStruct((2, rows, width), f32),
-        in_specs=[VMEM] * 7,
+        in_specs=[VMEM] * 7 + [HBM],
         out_specs=VMEM,
-        scratch_shapes=[pltpu.VMEM((2 * groups, SUB, LANES), f32)],
+        scratch_shapes=[
+            pltpu.VMEM((2 * groups, SUB, LANES), f32),
+            pltpu.VMEM((BATCH, degrees, LANES), f32),
+            pltpu.SemaphoreType.DMA((BATCH,)),
+        ],
         compiler_params=pltpu.CompilerParams(vmem_limit_bytes=VMEM_LIMIT),
         name="synthesis",
-    )(coef, rest, near, far, gains, cyc, table)
+    )(coef, rest, far, near, gains, cyc, tab, pinned[8])
     return smoothed, potential
 
 

time: 27.9 us -> 27.6 us (0.989)
  Pallas kernels: 6.88 us -> 6.6 us
    pallas_call x1, Pallas kernels: 1.87 us -> 1.54 us  [local(): pl.pallas_call(functools.partial(synthesis_kernel, 2.0 / cycles), out_sha...]
  transfers between devices with their start and end apart: 5 -> 5, of which waited for: 1 -> 1; matrix products, arithmetic and copies ran while one was open for 0% -> 0% of each run, Pallas kernels for 10% -> 11%
where the time goes in v9:
time: 27.6 us; the launch traced here: 27.4 us
  blocking collectives  10.2 us (37%)
  starting transfers between devices  8.85 us (32%)
  Pallas kernels  6.6 us (24%)
  waiting for transfers between devices  1.02 us (4%)
  between operations  0.72 us (3%)
    all_gather x1, blocking collectives, local(): ring = lax.all_gather(pay, ('lat', 'rad'), axis_index_groups=chips)  10.2 us
    ppermute x1, starting transfers between devices, local(): beside2 = lax.ppermute(face2, 'rad', odd_pairs(rads)[:-2])  4.55 us
    pallas_call x1, Pallas kernels, local(): pl.pallas_call(faces_kernel, out_shape=(whole, whole, face, face, jax.Sha...  2.14 us
    pallas_call x1, Pallas kernels, local(): pl.pallas_call(sweep_kernel, out_shape=(whole, jax.ShapeDtypeStruct((BATC...  1.98 us
    pallas_call x1, Pallas kernels, local(): pl.pallas_call(functools.partial(synthesis_kernel, 2.0 / cycles), out_sha...  1.54 us
    ppermute x1, starting transfers between devices, local(): lax.ppermute(coef, 'rad', [(0, 3), (3, 0), (7, 4), (4, 7), (1, 5), (5, 1)...  1.53 us
    ppermute x1, starting transfers between devices, local(): got = lax.ppermute(outward, 'rad', odd_pairs(rads))  1.45 us
    ppermute x1, starting transfers between devices, local(): lax.ppermute(coef, 'rad', [(0, 4), (4, 0), (7, 3), (3, 7), (1, 6), (6, 1)...  1.19 us
  transfers between devices with their start and end apart: 5, of which 1 were waited for; matrix products, arithmetic and copies ran while one was open for 0% of the time, Pallas kernels for 11%

profile of v9, /device:TPU:1, one launch (start us, length us, event | category | flops | bytes accessed | tf_op | source)
XLA Modules:
  0.0 27.4 jit_solution(8625524901933670977)
XLA Ops:
  0.6 2.1 %faces.1 = (f32[3,4,64,384]{3,2,1,0:T(8,128)S(1)}, f32[3,4,64,384]{3,2,1,0:T(8,128)S(1)}, f32[2,3,64,384]{3,2,1,0:T(8,128)S(1)}, f32[2,3,64,384]{3,2,1,0:T(8,128...) custom-call(f32[3,4,64,384]{3,2,1,0:T(8,128)} %disp.1, ...), custom_call_target="tpu_custom_call" | custom-call | tf_op jit(solution)/shard_map/faces/pallas_call | solution.py:678
  2.8 0.1 collective-permute-start
  2.9 4.6 %collective-permute-start.1 = (f32[2,3,64,384]{3,2,1,0:T(8,128)S(1)}, f32[2,3,64,384]{3,2,1,0:T(8,128)S(1)}, u32[]{:S(2)}, u32[]{:S(2)}) collective-permute-start(f32[2,3,64,384]{3,2,1,0:T(8,128)S(1)} %get-tuple-element.23.face2.own2), channel_id=1, source_target_pairs={{1,2},{2,1},{3,4},{4,3},{5,6},{6,5},{9,10},{10,9},{11,12},{12,11},... | collective-permute-start | bytes 1769480 | tf_op jit(solution)/shard_map/ppermute | solution.py:704
  7.5 0.3 %analysis.1 = f32[56,384]{1,0:T(8,128)S(1)} custom-call(f32[3,4,64,384]{3,2,1,0:T(8,128)S(1)} %get-tuple-element.20.u, f32[3,4,64,384]{3,2,1,0:T(8,128)S(1)} %get-tuple-element.21.f, f32[2,3,64,384]{3,2,1,0:T(8,128)S(1)} %get-tuple-element.22.face1.own1, f32[2,3,64,384]{3,2,1,0:T(8,128)S(1)} %get-tuple-element.23.face2.own2, ...), custom_call_target="tpu_custom_call" | custom-call | tf_op jit(solution)/shard_map/analysis/pallas_call | solution.py:707
  7.8 10.2 %all-gather = f32[448,384]{1,0:T(8,128)S(1)} all-gather(f32[56,384]{1,0:T(8,128)S(1)} %analysis.1), channel_id=2, replica_groups={{0,1,8,9,16,17,24,25},{2,3,10,11,18,19,26,27},{4,5,12,13,20,21,28,29},{..., dimensions={0}, use_global_device_ids=true | all-gather | bytes 774144 | tf_op jit(solution)/shard_map/all_gather | solution.py:725
  18.0 0.0 collective-permute-done.face1
  18.0 0.0 collective-permute-done.1.face2
  18.0 1.4 %collective-permute-start.2 = (f32[48,128]{1,0:T(8,128)S(1)}, f32[48,128]{1,0:T(8,128)S(1)}, u32[]{:S(2)}, u32[]{:S(2)}) collective-permute-start(f32[48,128]{1,0:T(8,128)S(1)} %relay.1), channel_id=1, source_target_pairs={{1,2},{2,1},{3,4},{4,3},{5,6},{6,5},{7,0},{0,7},{9,10},{10,9},{11,... | collective-permute-start | bytes 73736 | tf_op jit(solution)/shard_map/ppermute | solution.py:735
  19.5 1.5 %collective-permute-start.4 = (f32[8,128]{1,0:T(8,128)S(1)}, f32[8,128]{1,0:T(8,128)S(1)}, u32[]{:S(2)}, u32[]{:S(2)}) collective-permute-start(f32[8,128]{1,0:T(8,128)S(1)} %slice.6.coef), channel_id=1, source_target_pairs={{0,3},{3,0},{7,4},{4,7},{1,5},{5,1},{2,6},{6,2},{8,11},{11,8},{15,... | collective-permute-start | bytes 12296 | tf_op jit(solution)/shard_map/ppermute | solution.py:751
  21.0 1.2 %collective-permute-start.3 = (f32[8,128]{1,0:T(8,128)S(1)}, f32[8,128]{1,0:T(8,128)S(1)}, u32[]{:S(2)}, u32[]{:S(2)}) collective-permute-start(f32[8,128]{1,0:T(8,128)S(1)} %slice.6.coef), channel_id=1, source_target_pairs={{0,4},{4,0},{7,3},{3,7},{1,6},{6,1},{2,5},{5,2},{8,12},{12,8},{15,... | collective-permute-start | bytes 12296 | tf_op jit(solution)/shard_map/ppermute | solution.py:750
  22.2 0.6 %inner.1 = (f32[3,2,64,384]{3,2,1,0:T(8,128)S(1)}, f32[2,8,128]{2,1,0:T(8,128)S(1)}) custom-call(f32[3,4,64,384]{3,2,1,0:T(8,128)S(1)} %get-tuple-element.20.u, f32[3,4,64,384]{3,2,1,0:T(8,128)S(1)} %get-tuple-element.21.f, f32[4,16,128]{2,1,0:T(8,128)S(1)} %get-tuple-element.24.every, f32[2,2,512]{2,1,0:T(2,128)S(1)} %get-tuple-element.29.gain_in), custom_call_target="tpu_custom_call" | custom-call | tf_op jit(solution)/shard_map/inner/pallas_call | solution.py:736
  22.8 0.0 collective-permute-done.2.got
  22.8 2.0 %sweeps.1 = (f32[3,4,64,384]{3,2,1,0:T(8,128)}, f32[5,512,128]{2,1,0:T(8,128)S(1)}) custom-call(f32[3,4,64,384]{3,2,1,0:T(8,128)S(1)} %get-tuple-element.20.u, f32[3,4,64,384]{3,2,1,0:T(8,128)S(1)} %get-tuple-element.21.f, f32[2,3,64,384]{3,2,1,0:T(8,128)S(1)} %get-tuple-element.22.face1.own1, f32[2,3,64,384]{3,2,1,0:T(8,128)S(1)} %get-tuple-element.23.face2.own2, ...), custom_call_target="tpu_custom_call" | custom-call | tf_op jit(solution)/shard_map/sweeps/pallas_call | solution.py:757
  24.8 0.0 collective-permute-done.4.far
  24.8 1.0 %collective-permute-done.3.near = f32[8,128]{1,0:T(8,128)S(1)} collective-permute-done((f32[8,128]{1,0:T(8,128)S(1)}, f32[8,128]{1,0:T(8,128)S(1)}, u32[]{:S(2)}, u32[]{:S(2)}) %collective-permute-start.3) | collective-permute-done | bytes 4128 | tf_op jit(solution)/shard_map/ppermute | solution.py:750
  25.9 1.5 %synthesis.1 = f32[2,64,384]{2,1,0:T(8,128)} custom-call(f32[8,128]{1,0:T(8,128)S(1)} %slice.6.coef, f32[8,128]{1,0:T(8,128)S(1)} %slice.7.rest, f32[8,128]{1,0:T(8,128)S(1)} %collective-permute-done.3.near, f32[8,128]{1,0:T(8,128)S(1)} %collective-permute-done.4.far, f32[2,8,128]{2,1,0:T(8,128)S(1)} %get-tuple-element.36.gains, ...), custom_call_target="tpu_custom_call" | custom-call | tf_op jit(solution)/shard_map/synthesis/pallas_call | solution.py:774
  (3 shorter events, 0.0 us)
Async XLA Ops:
  2.8 15.2 %collective-permute-start = (f32[2,3,64,384]{3,2,1,0:T(8,128)S(1)}, f32[2,3,64,384]{3,2,1,0:T(8,128)S(1)}, u32[]{:S(2)}, u32[]{:S(2)}) collective-permute-start(f32[2,3,64,384]{3,2,1,0:T(8,128)S(1)} %get-tuple-element.22.face1.own1), channel_id=1, source_target_pairs={{0,1},{1,0},{2,3},{3,2},{4,5},{5,4},{6,7},{7,6},{8,9},{9,8},{10,11... | collective-permute-start | bytes 1769480 | tf_op jit(solution)/shard_map/ppermute | solution.py:705
  2.9 15.1 %collective-permute-start.1 = (f32[2,3,64,384]{3,2,1,0:T(8,128)S(1)}, f32[2,3,64,384]{3,2,1,0:T(8,128)S(1)}, u32[]{:S(2)}, u32[]{:S(2)}) collective-permute-start(f32[2,3,64,384]{3,2,1,0:T(8,128)S(1)} %get-tuple-element.23.face2.own2), channel_id=1, source_target_pairs={{1,2},{2,1},{3,4},{4,3},{5,6},{6,5},{9,10},{10,9},{11,12},{12,11},... | collective-permute-start | bytes 1769480 | tf_op jit(solution)/shard_map/ppermute | solution.py:704
  18.0 4.8 %collective-permute-start.2 = (f32[48,128]{1,0:T(8,128)S(1)}, f32[48,128]{1,0:T(8,128)S(1)}, u32[]{:S(2)}, u32[]{:S(2)}) collective-permute-start(f32[48,128]{1,0:T(8,128)S(1)} %relay.1), channel_id=1, source_target_pairs={{1,2},{2,1},{3,4},{4,3},{5,6},{6,5},{7,0},{0,7},{9,10},{10,9},{11,... | collective-permute-start | bytes 73736 | tf_op jit(solution)/shard_map/ppermute | solution.py:735
  19.5 5.3 %collective-permute-start.4 = (f32[8,128]{1,0:T(8,128)S(1)}, f32[8,128]{1,0:T(8,128)S(1)}, u32[]{:S(2)}, u32[]{:S(2)}) collective-permute-start(f32[8,128]{1,0:T(8,128)S(1)} %slice.6.coef), channel_id=1, source_target_pairs={{0,3},{3,0},{7,4},{4,7},{1,5},{5,1},{2,6},{6,2},{8,11},{11,8},{15,... | collective-permute-start | bytes 12296 | tf_op jit(solution)/shard_map/ppermute | solution.py:751
  21.0 4.8 %collective-permute-start.3 = (f32[8,128]{1,0:T(8,128)S(1)}, f32[8,128]{1,0:T(8,128)S(1)}, u32[]{:S(2)}, u32[]{:S(2)}) collective-permute-start(f32[8,128]{1,0:T(8,128)S(1)} %slice.6.coef), channel_id=1, source_target_pairs={{0,4},{4,0},{7,3},{3,7},{1,6},{6,1},{2,5},{5,2},{8,12},{12,8},{15,... | collective-permute-start | bytes 12296 | tf_op jit(solution)/shard_map/ppermute | solution.py:750

commit v10 on v9

--- a/solution.py
+++ b/solution.py
@@ -417,11 +417,11 @@
     for i in range(1, members):
         coef = coef + ring[i, 0:SUB, 0:LANES]
     out[0:SUB, :] = coef
-    out[SUB:SUB + COEFS, :] = send[...]
+    out[SUB:2 * SUB, :] = send[0:SUB, :]
     before, after = cores * jnp.maximum(lat - 1, 0) + core, cores * jnp.minimum(lat + 1, lats - 1) + core
     low_in, high_in = lat > 0, lat < lats - 1
     for j in range(width // LANES):
-        base = SUB + COEFS + SUB * j
+        base = 2 * SUB + SUB * j
         out[base:base + SUB, :] = jnp.zeros((SUB, LANES), jnp.float32)
         for c in range(3):
             for at, member, valid, start in ((c, before, low_in, 2 * tall), (3 + c, after, high_in, 0)):
@@ -464,18 +464,16 @@
         return jnp.concatenate([low, high], axis=0)
 
     mate = 1 - core
-    own_chip = jnp.concatenate(
-        [ring[cores * lat + mate, 0:SUB, LANES:2 * LANES], ring[cores * lat + mate, 0:SUB, 2 * LANES:3 * LANES]], axis=0
-    )
-    other_chip = got[SUB:SUB + COEFS, :]
+    own_chip = ring[cores * lat + mate, 0:SUB, LANES:2 * LANES]
+    other_chip = got[SUB:2 * SUB, :]
     lowest, highest = rad == 0, rad == rads - 1
-    cf[0] = jnp.where(rad_odd, own_chip, jnp.where(lowest, 0.0, other_chip))
-    cf[layers + 1] = jnp.where(rad_odd, jnp.where(highest, 0.0, other_chip), own_chip)
+    cf[0, 0:SUB, :] = jnp.where(rad_odd, own_chip, jnp.where(lowest, 0.0, other_chip))
+    cf[layers + 1, 0:SUB, :] = jnp.where(rad_odd, jnp.where(highest, 0.0, other_chip), own_chip)
     for r in range(layers):
         cf[1 + r] = every[r]
     corner_low, corner_high = [], []
     for j in range(per_row):
-        base = SUB + COEFS + SUB * j
+        base = 2 * SUB + SUB * j
         other = got[base:base + SUB, :]
         rows_own = []
         for member, valid, start in ((lower + mate, low_in, 2 * tall), (upper + mate, high_in, 0)):
@@ -725,7 +723,7 @@
     ring = lax.all_gather(pay, ("lat", "rad"), axis_index_groups=chips)
     outward = pl.pallas_call(
         relay_kernel,
-        out_shape=jax.ShapeDtypeStruct((SUB + COEFS + SUB * per_row, LANES), f32),
+        out_shape=jax.ShapeDtypeStruct((2 * SUB + SUB * per_row, LANES), f32),
         in_specs=[VMEM] * 2,
         out_specs=VMEM,
         compiler_params=pltpu.CompilerParams(vmem_limit_bytes=VMEM_LIMIT),

time: 27.6 us -> 27.6 us (level)
  no operation moved by 1% of the time
where the time goes in v10:
time: 27.6 us; the launch traced here: 27.4 us
  blocking collectives  10.2 us (37%)
  starting transfers between devices  8.84 us (32%)
  Pallas kernels  6.7 us (24%)
  waiting for transfers between devices  0.93 us (3%)
  between operations  0.72 us (3%)
    all_gather x1, blocking collectives, local(): ring = lax.all_gather(pay, ('lat', 'rad'), axis_index_groups=chips)  10.2 us
    ppermute x1, starting transfers between devices, local(): beside2 = lax.ppermute(face2, 'rad', odd_pairs(rads)[:-2])  4.55 us
    pallas_call x1, Pallas kernels, local(): pl.pallas_call(faces_kernel, out_shape=(whole, whole, face, face, jax.Sha...  2.16 us
    pallas_call x1, Pallas kernels, local(): pl.pallas_call(sweep_kernel, out_shape=(whole, jax.ShapeDtypeStruct((BATC...  2.06 us
    pallas_call x1, Pallas kernels, local(): pl.pallas_call(functools.partial(synthesis_kernel, 2.0 / cycles), out_sha...  1.54 us
    ppermute x1, starting transfers between devices, local(): lax.ppermute(coef, 'rad', [(0, 3), (3, 0), (7, 4), (4, 7), (1, 5), (5, 1)...  1.53 us
    ppermute x1, starting transfers between devices, local(): got = lax.ppermute(outward, 'rad', odd_pairs(rads))  1.45 us
    ppermute x1, starting transfers between devices, local(): lax.ppermute(coef, 'rad', [(0, 4), (4, 0), (7, 3), (3, 7), (1, 6), (6, 1)...  1.19 us
  transfers between devices with their start and end apart: 5, of which 1 were waited for; matrix products, arithmetic and copies ran while one was open for 0% of the time, Pallas kernels for 11%

profile of v10, /device:TPU:1, one launch (start us, length us, event | category | flops | bytes accessed | tf_op | source)
XLA Modules:
  0.0 27.4 jit_solution(2228936061395055423)
XLA Ops:
  0.6 2.2 %faces.1 = (f32[3,4,64,384]{3,2,1,0:T(8,128)S(1)}, f32[3,4,64,384]{3,2,1,0:T(8,128)S(1)}, f32[2,3,64,384]{3,2,1,0:T(8,128)S(1)}, f32[2,3,64,384]{3,2,1,0:T(8,128...) custom-call(f32[3,4,64,384]{3,2,1,0:T(8,128)} %disp.1, ...), custom_call_target="tpu_custom_call" | custom-call | tf_op jit(solution)/shard_map/faces/pallas_call | solution.py:676
  2.8 0.1 collective-permute-start
  2.9 4.6 %collective-permute-start.1 = (f32[2,3,64,384]{3,2,1,0:T(8,128)S(1)}, f32[2,3,64,384]{3,2,1,0:T(8,128)S(1)}, u32[]{:S(2)}, u32[]{:S(2)}) collective-permute-start(f32[2,3,64,384]{3,2,1,0:T(8,128)S(1)} %get-tuple-element.23.face2.own2), channel_id=1, source_target_pairs={{1,2},{2,1},{3,4},{4,3},{5,6},{6,5},{9,10},{10,9},{11,12},{12,11},... | collective-permute-start | bytes 1769480 | tf_op jit(solution)/shard_map/ppermute | solution.py:702
  7.5 0.3 %analysis.1 = f32[56,384]{1,0:T(8,128)S(1)} custom-call(f32[3,4,64,384]{3,2,1,0:T(8,128)S(1)} %get-tuple-element.20.u, f32[3,4,64,384]{3,2,1,0:T(8,128)S(1)} %get-tuple-element.21.f, f32[2,3,64,384]{3,2,1,0:T(8,128)S(1)} %get-tuple-element.22.face1.own1, f32[2,3,64,384]{3,2,1,0:T(8,128)S(1)} %get-tuple-element.23.face2.own2, ...), custom_call_target="tpu_custom_call" | custom-call | tf_op jit(solution)/shard_map/analysis/pallas_call | solution.py:705
  7.8 10.2 %all-gather = f32[448,384]{1,0:T(8,128)S(1)} all-gather(f32[56,384]{1,0:T(8,128)S(1)} %analysis.1), channel_id=2, replica_groups={{0,1,8,9,16,17,24,25},{2,3,10,11,18,19,26,27},{4,5,12,13,20,21,28,29},{..., dimensions={0}, use_global_device_ids=true | all-gather | bytes 774144 | tf_op jit(solution)/shard_map/all_gather | solution.py:723
  18.0 0.0 collective-permute-done.face1
  18.0 0.0 collective-permute-done.1.face2
  18.1 1.4 %collective-permute-start.2 = (f32[40,128]{1,0:T(8,128)S(1)}, f32[40,128]{1,0:T(8,128)S(1)}, u32[]{:S(2)}, u32[]{:S(2)}) collective-permute-start(f32[40,128]{1,0:T(8,128)S(1)} %relay.1), channel_id=1, source_target_pairs={{1,2},{2,1},{3,4},{4,3},{5,6},{6,5},{7,0},{0,7},{9,10},{10,9},{11,... | collective-permute-start | bytes 61448 | tf_op jit(solution)/shard_map/ppermute | solution.py:733
  19.5 1.5 %collective-permute-start.4 = (f32[8,128]{1,0:T(8,128)S(1)}, f32[8,128]{1,0:T(8,128)S(1)}, u32[]{:S(2)}, u32[]{:S(2)}) collective-permute-start(f32[8,128]{1,0:T(8,128)S(1)} %slice.6.coef), channel_id=1, source_target_pairs={{0,3},{3,0},{7,4},{4,7},{1,5},{5,1},{2,6},{6,2},{8,11},{11,8},{15,... | collective-permute-start | bytes 12296 | tf_op jit(solution)/shard_map/ppermute | solution.py:749
  21.0 1.2 %collective-permute-start.3 = (f32[8,128]{1,0:T(8,128)S(1)}, f32[8,128]{1,0:T(8,128)S(1)}, u32[]{:S(2)}, u32[]{:S(2)}) collective-permute-start(f32[8,128]{1,0:T(8,128)S(1)} %slice.6.coef), channel_id=1, source_target_pairs={{0,4},{4,0},{7,3},{3,7},{1,6},{6,1},{2,5},{5,2},{8,12},{12,8},{15,... | collective-permute-start | bytes 12296 | tf_op jit(solution)/shard_map/ppermute | solution.py:748
  22.2 0.6 %inner.1 = (f32[3,2,64,384]{3,2,1,0:T(8,128)S(1)}, f32[2,8,128]{2,1,0:T(8,128)S(1)}) custom-call(f32[3,4,64,384]{3,2,1,0:T(8,128)S(1)} %get-tuple-element.20.u, f32[3,4,64,384]{3,2,1,0:T(8,128)S(1)} %get-tuple-element.21.f, f32[4,16,128]{2,1,0:T(8,128)S(1)} %get-tuple-element.24.every, f32[2,2,512]{2,1,0:T(2,128)S(1)} %get-tuple-element.29.gain_in), custom_call_target="tpu_custom_call" | custom-call | tf_op jit(solution)/shard_map/inner/pallas_call | solution.py:734
  22.9 0.0 collective-permute-done.2.got
  22.9 2.1 %sweeps.1 = (f32[3,4,64,384]{3,2,1,0:T(8,128)}, f32[5,512,128]{2,1,0:T(8,128)S(1)}) custom-call(f32[3,4,64,384]{3,2,1,0:T(8,128)S(1)} %get-tuple-element.20.u, f32[3,4,64,384]{3,2,1,0:T(8,128)S(1)} %get-tuple-element.21.f, f32[2,3,64,384]{3,2,1,0:T(8,128)S(1)} %get-tuple-element.22.face1.own1, f32[2,3,64,384]{3,2,1,0:T(8,128)S(1)} %get-tuple-element.23.face2.own2, ...), custom_call_target="tpu_custom_call" | custom-call | tf_op jit(solution)/shard_map/sweeps/pallas_call | solution.py:755
  24.9 0.0 collective-permute-done.4.far
  25.0 0.9 %collective-permute-done.3.near = f32[8,128]{1,0:T(8,128)S(1)} collective-permute-done((f32[8,128]{1,0:T(8,128)S(1)}, f32[8,128]{1,0:T(8,128)S(1)}, u32[]{:S(2)}, u32[]{:S(2)}) %collective-permute-start.3) | collective-permute-done | bytes 4128 | tf_op jit(solution)/shard_map/ppermute | solution.py:748
  25.9 1.5 %synthesis.1 = f32[2,64,384]{2,1,0:T(8,128)} custom-call(f32[8,128]{1,0:T(8,128)S(1)} %slice.6.coef, f32[8,128]{1,0:T(8,128)S(1)} %slice.7.rest, f32[8,128]{1,0:T(8,128)S(1)} %collective-permute-done.3.near, f32[8,128]{1,0:T(8,128)S(1)} %collective-permute-done.4.far, f32[2,8,128]{2,1,0:T(8,128)S(1)} %get-tuple-element.36.gains, ...), custom_call_target="tpu_custom_call" | custom-call | tf_op jit(solution)/shard_map/synthesis/pallas_call | solution.py:772
  (3 shorter events, 0.0 us)
Async XLA Ops:
  2.8 15.2 %collective-permute-start = (f32[2,3,64,384]{3,2,1,0:T(8,128)S(1)}, f32[2,3,64,384]{3,2,1,0:T(8,128)S(1)}, u32[]{:S(2)}, u32[]{:S(2)}) collective-permute-start(f32[2,3,64,384]{3,2,1,0:T(8,128)S(1)} %get-tuple-element.22.face1.own1), channel_id=1, source_target_pairs={{0,1},{1,0},{2,3},{3,2},{4,5},{5,4},{6,7},{7,6},{8,9},{9,8},{10,11... | collective-permute-start | bytes 1769480 | tf_op jit(solution)/shard_map/ppermute | solution.py:703
  2.9 15.1 %collective-permute-start.1 = (f32[2,3,64,384]{3,2,1,0:T(8,128)S(1)}, f32[2,3,64,384]{3,2,1,0:T(8,128)S(1)}, u32[]{:S(2)}, u32[]{:S(2)}) collective-permute-start(f32[2,3,64,384]{3,2,1,0:T(8,128)S(1)} %get-tuple-element.23.face2.own2), channel_id=1, source_target_pairs={{1,2},{2,1},{3,4},{4,3},{5,6},{6,5},{9,10},{10,9},{11,12},{12,11},... | collective-permute-start | bytes 1769480 | tf_op jit(solution)/shard_map/ppermute | solution.py:702
  18.1 4.8 %collective-permute-start.2 = (f32[40,128]{1,0:T(8,128)S(1)}, f32[40,128]{1,0:T(8,128)S(1)}, u32[]{:S(2)}, u32[]{:S(2)}) collective-permute-start(f32[40,128]{1,0:T(8,128)S(1)} %relay.1), channel_id=1, source_target_pairs={{1,2},{2,1},{3,4},{4,3},{5,6},{6,5},{7,0},{0,7},{9,10},{10,9},{11,... | collective-permute-start | bytes 61448 | tf_op jit(solution)/shard_map/ppermute | solution.py:733
  19.5 5.4 %collective-permute-start.4 = (f32[8,128]{1,0:T(8,128)S(1)}, f32[8,128]{1,0:T(8,128)S(1)}, u32[]{:S(2)}, u32[]{:S(2)}) collective-permute-start(f32[8,128]{1,0:T(8,128)S(1)} %slice.6.coef), channel_id=1, source_target_pairs={{0,3},{3,0},{7,4},{4,7},{1,5},{5,1},{2,6},{6,2},{8,11},{11,8},{15,... | collective-permute-start | bytes 12296 | tf_op jit(solution)/shard_map/ppermute | solution.py:749
  21.0 4.8 %collective-permute-start.3 = (f32[8,128]{1,0:T(8,128)S(1)}, f32[8,128]{1,0:T(8,128)S(1)}, u32[]{:S(2)}, u32[]{:S(2)}) collective-permute-start(f32[8,128]{1,0:T(8,128)S(1)} %slice.6.coef), channel_id=1, source_target_pairs={{0,4},{4,0},{7,3},{3,7},{1,6},{6,1},{2,5},{5,2},{8,12},{12,8},{15,... | collective-permute-start | bytes 12296 | tf_op jit(solution)/shard_map/ppermute | solution.py:748
